TPU v7x, 32 devices: a whole 2x2x4 slice. The times are simulated.
32 devices in a mesh: tm: 4 (over x, core), space: 8 (over z, y).
Axes of the slice: x: 2, y: 2, z: 4, core: 2. Of those that a mesh axis runs over, the one named last changes fastest.
Arguments:
- forcing: bfloat16 [4, 4, 6, 256, 1024], P('tm', None, None, None, 'space'), may hold values from -6 to 6
- zonal_courant: float32 [4, 256, 1024], P('tm', None, 'space'), may hold values from -0.3 to 0.3
- meridional_courant: float32 [4, 256, 1024], P('tm', None, 'space'), may hold values from -0.3 to 0.3
- zonal_faces: float32 [4, 256, 1024], P('tm', None, 'space'), may hold values from 0.1 to 0.4
- meridional_faces: float32 [4, 256, 1024], P('tm', None, 'space'), may hold values from 0.1 to 0.4
- coupling: float32 [4, 6, 6], P('tm'), may hold values from -0.375 to 0.375
Outputs:
- adjoint_start: float32 [4, 6, 256, 1024], P('tm', None, None, 'space')
All inputs are finite; a program needn't handle non-finite values.
Results may differ from a plain program's by a relative error of at most 0.0015.
Values may be sent and summed in bfloat16 or wider, within the bound.
No kernel may reach another device: no remote copies, remote signals or barrier semaphores. Data moves between devices by JAX's collectives and lax.ppermute only.
A program may use at most 64 MiB of HBM per device.

v0:
```python
import functools

import jax
import jax.numpy as jnp
from jax import lax
from jax.experimental import pallas as pl
from jax.experimental.pallas import tpu as pltpu
from jax.sharding import PartitionSpec as P

SWEEPS = 2
OMEGA = 0.4
SUB = 8
REACH = SWEEPS + 1
VMEM_BYTES = 48 * 2**20
F32 = jnp.float32
BF16 = jnp.bfloat16


class Sizes:
    def __init__(self, forcing_shape):
        _, self.steps, self.fields, self.rows, self.strip = forcing_shape
        self.lanes = self.rows // 2
        self.halo = 2 * REACH * self.steps
        self.main = self.strip // 2 + 2 * self.halo
        self.window = self.main + self.halo
        self.span = self.window // SUB
        self.shift = self.strip - self.main
        self.own = self.strip // 2
        self.groups = [-(-REACH * (self.steps + k) // SUB) for k in range(self.steps)]
        self.group_start = [self.fields * sum(self.groups[:k]) for k in range(self.steps)]
        self.coef_start = self.fields * sum(self.groups)
        self.coef_groups = self.halo // SUB
        self.payload = self.coef_start + 4 * self.coef_groups
        self.message = self.own + self.halo


def half_and_chip():
    tm = lax.axis_index("tm")
    return lax.rem(tm, 2), tm // 2


def prepare_kernel(z, fo, zc, mc, zf, mf, cp, keep_f, send_f, keep_c, send_c, pay_a, pay_b, buf):
    half, _ = half_and_chip()
    left = half == 0
    row = lax.broadcasted_iota(jnp.int32, (z.rows, z.strip), 0)

    def columns(values, slot):
        buf[slot] = values
        return [buf[slot, pl.ds(p, z.lanes, stride=2), :].T for p in range(2)]

    def split(both, groups, start, keep, send):
        for p in range(2):
            low, high = both[p][: z.main], both[p][z.shift :]
            keep[p] = jnp.where(left, low, high).astype(keep.dtype)
            send[p] = jnp.where(left, high, low).astype(send.dtype)
        for g in range(groups):
            lo, hi = SUB * g, z.strip - SUB * (groups - g)
            west = jnp.concatenate([both[p][lo : lo + SUB] for p in range(2)], axis=0)
            east = jnp.concatenate([both[p][hi : hi + SUB] for p in range(2)], axis=0)
            pay_a[start + g] = jnp.where(left, west, east).astype(BF16)
            pay_b[start + g] = jnp.where(left, east, west).astype(BF16)

    slots = buf.shape[0]
    count = 0
    for c, ref in enumerate((zf, mf, zc, mc)):
        values = ref[0]
        if c == 1:
            values = jnp.where(row < z.rows - 1, values, jnp.zeros_like(values))
        both = columns(values, count % slots)
        split(both, z.coef_groups, z.coef_start + c * z.coef_groups, keep_c.at[c], send_c.at[c])
        count += 1
    for ref in (keep_c, send_c):
        ref[4, 0, : z.fields, : z.fields] = cp[0]
    for k in range(z.steps):
        for f in range(z.fields):
            both = columns(fo[0, k, f].astype(F32), count % slots)
            split(both, z.groups[k], z.group_start[k] + f * z.groups[k], keep_f.at[k, f], send_f.at[k, f])
            count += 1


def fill_ghosts(ref, span, count):
    for n in range(count):
        for p in range(2):
            ref[0, n, p] = pltpu.roll(ref[span, n, p], 1, 0)
            ref[span + 1, n, p] = pltpu.roll(ref[1, n, p], SUB - 1, 0)


def chain_kernel(z, first, active, *refs):
    n_in = 6 if first else 10
    kf, rf, kc, rc, ra, rb = refs[:6]
    refs = refs[6:]
    if not first:
        msg_in, edge_in = refs[:2]
        refs = refs[4:]
    ko, so, msg, edge = refs[:4]
    (vf, vc, vp, seg, co, kk, r, u1, u2, pz, tmp, obuf, sems) = refs[4:]
    half, chip = half_and_chip()
    span, fields = z.span, z.fields
    lane = lax.broadcasted_iota(jnp.int32, (SUB, z.lanes), 1)
    zero = jnp.zeros((SUB, z.lanes), F32)

    def east_roll(v):
        return pltpu.roll(v, 1, 1)

    def west_roll(v):
        return pltpu.roll(v, z.lanes - 1, 1)

    def rows_at(offset, count):
        return pl.ds(pl.multiple_of(offset, SUB), count)

    def window_rows(t, main, groups):
        at = tmp.at[t]
        at[rows_at(z.main * half, z.halo), :] = jnp.zeros((z.halo, z.lanes), F32)
        at[rows_at(z.halo * (1 - half), z.main), :] = main
        for g, values in enumerate(groups):
            back = z.halo - SUB * (len(groups) - g)
            at[rows_at(jnp.where(half == 0, back, z.main + SUB * g), SUB), :] = values

    def segments(t):
        return [tmp[t, pl.ds(i, SUB, stride=span), :] for i in range(span)]

    def assemble(q):
        for k in range(z.steps):
            for f in range(fields):
                tiles = [vp[q, z.group_start[k] + f * z.groups[k] + g].astype(F32) for g in range(z.groups[k])]
                for p in range(2):
                    t = (2 * f + p) % tmp.shape[0]
                    window_rows(t, vf[q, k, f, p].astype(F32), [v[SUB * p : SUB * p + SUB] for v in tiles])
                    for i, v in enumerate(segments(t)):
                        seg[k, i, f, p] = v
        for c in range(4):
            start = z.coef_start + c * z.coef_groups
            tiles = [vp[q, start + g].astype(F32) for g in range(z.coef_groups)]
            for p in range(2):
                t = (2 * c + p) % tmp.shape[0]
                window_rows(t, vc[q, c, p], [v[SUB * p : SUB * p + SUB] for v in tiles])
                for i, v in enumerate(segments(t)):
                    u1[i + 1, c, p] = v
        fill_ghosts(u1, span, 1)
        for i in range(1, span + 1):
            be, bo = u1[i, 1, 0], u1[i, 1, 1]
            south = (east_roll(bo), be)
            for p in range(2):
                a, aw, b = u1[i, 0, p], u1[i - 1, 0, p], u1[i, 1, p]
                co[i, 0, p] = 1.0 - OMEGA * (1.0 + (a + aw) + (b + south[p]))
                co[i, 1, p] = OMEGA * a
                co[i, 2, p] = OMEGA * aw
                co[i, 3, p] = OMEGA * b
                co[i, 4, p] = OMEGA * south[p]
                co[i, 5, p] = (0.5 * OMEGA) * u1[i, 2, p]
                co[i, 6, p] = (0.5 * OMEGA) * u1[i, 3, p]
        for g in range(fields):
            for f in range(fields):
                value = vc[q, 4, 0, g : g + 1, f : f + 1]
                if f == g:
                    value = value + 1.0
                kk[g * fields + f] = jnp.broadcast_to(OMEGA * value, (SUB, z.lanes))

    def sweep(src, dst, i, source):
        ga = [co[i, c, 0] for c in range(5)]
        gb = [co[i, c, 1] for c in range(5)]
        for f in range(fields):
            a, b = src[i, f, 0], src[i, f, 1]
            va = ga[0] * a + ga[1] * src[i + 1, f, 0] + ga[2] * src[i - 1, f, 0] + ga[3] * b + ga[4] * east_roll(b)
            vb = gb[0] * b + gb[1] * src[i + 1, f, 1] + gb[2] * src[i - 1, f, 1] + gb[3] * west_roll(a) + gb[4] * a
            va = va + (a if source is None else source[i, f, 0])
            vb = vb + (b if source is None else source[i, f, 1])
            dst[i, f, 0] = va
            dst[i, f, 1] = vb
            if source is not None:
                pz[i, f, 0] = co[i, 5, 0] * va
                pz[i, f, 1] = co[i, 5, 1] * vb

    def step(k):
        fill_ghosts(r, span, fields)
        for i in range(1, span + 1):
            sweep(r, u1, i, None)
        fill_ghosts(u1, span, fields)
        for i in range(1, span + 1):
            sweep(u1, u2, i, r)
        fill_ghosts(pz, span, fields)
        for i in range(1, span + 1):
            us = [[u2[i, g, p] for p in range(2)] for g in range(fields)]
            for f in range(fields):
                qa, qb = co[i, 6, 0] * us[f][0], co[i, 6, 1] * us[f][1]
                qba = jnp.where(lane == 0, zero, east_roll(qb))
                qab = jnp.where(lane == z.lanes - 1, zero, west_roll(qa))
                oa = (pz[i + 1, f, 0] - pz[i - 1, f, 0]) + (qb - qba)
                ob = (pz[i + 1, f, 1] - pz[i - 1, f, 1]) + (qab - qa)
                for g in range(fields):
                    w = kk[g * fields + f]
                    oa = oa + w * us[g][0]
                    ob = ob + w * us[g][1]
                r[i, f, 0] = oa + seg[k, i - 1, f, 0]
                r[i, f, 1] = ob + seg[k, i - 1, f, 1]

    def to_rows(t, f, p):
        for i in range(span):
            tmp[t, pl.ds(i, SUB, stride=span), :] = r[i + 1, f, p]

    @pl.when(chip == active)
    def _():
        copies = [
            pltpu.make_async_copy(kf, vf.at[1 - half], sems.at[0]),
            pltpu.make_async_copy(rf, vf.at[half], sems.at[1]),
            pltpu.make_async_copy(kc, vc.at[1 - half], sems.at[2]),
            pltpu.make_async_copy(rc, vc.at[half], sems.at[3]),
            pltpu.make_async_copy(ra, vp.at[half], sems.at[4]),
            pltpu.make_async_copy(rb, vp.at[1 - half], sems.at[5]),
        ]
        for copy in copies:
            copy.start()
        if not first:
            offset = jnp.where(half == 0, 0, z.main)
            for f in range(fields):
                for p in range(2):
                    t = (2 * f + p) % tmp.shape[0]
                    tmp[t] = jnp.zeros((z.window, z.lanes), F32)
                    for g in range(z.message // SUB):
                        v = msg_in[f, g].astype(F32)[SUB * p : SUB * p + SUB]
                        tmp[t, z.halo + SUB * g : z.halo + SUB * (g + 1), :] = v
                    for g in range(z.halo // SUB):
                        v = edge_in[f, g].astype(F32)[SUB * p : SUB * p + SUB]
                        tmp[t, rows_at(offset + SUB * g, SUB), :] = v
                    for i, v in enumerate(segments(t)):
                        r[i + 1, f, p] = v
        for copy in copies:
            copy.wait()

        def sub_window(q, carry):
            assemble(q)
            begin = 0
            if first:
                begin = jnp.where(q == 0, 1, 0)

                @pl.when(q == 0)
                def _():
                    for i in range(span):
                        for f in range(fields):
                            for p in range(2):
                                r[i + 1, f, p] = seg[z.steps - 1, i, f, p]

            def one(n, c):
                step(z.steps - 1 - n)
                return c

            lax.fori_loop(begin, z.steps, one, 0)
            place = jnp.where(q == half, 1, 0)
            for f in range(fields):
                for p in range(2):
                    t = (2 * f + p) % tmp.shape[0]
                    to_rows(t, f, p)
                    obuf[place, f, p] = tmp[t, rows_at(z.halo * (1 + half), z.own), :]
            return carry

        lax.fori_loop(0, 2, sub_window, 0)
        outs = [
            pltpu.make_async_copy(obuf.at[0], ko, sems.at[0]),
            pltpu.make_async_copy(obuf.at[1], so, sems.at[1]),
        ]
        for copy in outs:
            copy.start()
        if first:
            offset = jnp.where(half == 0, z.halo, z.main - z.halo)
            for f in range(fields):
                for p in range(2):
                    to_rows(p, f, p)
                for g in range(z.message // SUB):
                    at = z.halo + SUB * g
                    msg[f, g] = jnp.concatenate([tmp[p, at : at + SUB, :] for p in range(2)], axis=0).astype(BF16)
                for g in range(z.halo // SUB):
                    tiles = [tmp[p, rows_at(offset + SUB * g, SUB), :] for p in range(2)]
                    edge[f, g] = jnp.concatenate(tiles, axis=0).astype(BF16)
        for copy in outs:
            copy.wait()


def finish_kernel(z, keep, got, out):
    half, _ = half_and_chip()
    for f in range(z.fields):
        for p in range(2):
            a, b = keep[f, p], got[f, p]
            west = jnp.where(half == 0, a, b)
            east = jnp.where(half == 0, b, a)
            out[0, f, pl.ds(p, z.lanes, stride=2), :] = jnp.concatenate([west, east], axis=0).T


def shape(dims, dtype):
    return jax.ShapeDtypeStruct(tuple(dims), dtype)


def in_vmem(count):
    return [pl.BlockSpec(memory_space=pltpu.VMEM)] * count


def anywhere(count):
    return [pl.BlockSpec(memory_space=pl.ANY)] * count


def per_device(forcing, zonal_courant, meridional_courant, zonal_faces, meridional_faces, coupling):
    z = Sizes(forcing.shape)
    assert z.window % SUB == 0 and z.main % 16 == 0 and z.shift % 16 == 0
    tm_count, strips = lax.axis_size("tm"), lax.axis_size("space")
    chips = tm_count // 2
    params = pltpu.CompilerParams(vmem_limit_bytes=VMEM_BYTES)
    f_shape = (z.steps, z.fields, 2, z.main, z.lanes)
    c_shape = (5, 2, z.main, z.lanes)
    pay_shape = (z.payload, 2 * SUB, z.lanes)
    keep_f, send_f, keep_c, send_c, pay_a, pay_b = pl.pallas_call(
        functools.partial(prepare_kernel, z),
        out_shape=[
            shape(f_shape, BF16),
            shape(f_shape, BF16),
            shape(c_shape, F32),
            shape(c_shape, F32),
            shape(pay_shape, BF16),
            shape(pay_shape, BF16),
        ],
        in_specs=in_vmem(6),
        out_specs=in_vmem(6),
        scratch_shapes=[pltpu.VMEM((4, z.rows, z.strip), F32)],
        compiler_params=params,
        name="prepare",
    )(forcing, zonal_courant, meridional_courant, zonal_faces, meridional_faces, coupling)

    def device(tm, space):
        return tm * strips + space % strips

    everyone = [(t, s) for t in range(tm_count) for s in range(strips)]
    partner = [(t, t ^ 1) for t in range(tm_count)]
    perm_a = [(device(t, s), device(t ^ 1, s + 1 if t % 2 else s - 1)) for t, s in everyone]
    perm_b = [(device(t, s), device(t, s - 1 if t % 2 else s + 1)) for t, s in everyone]
    got_a = lax.ppermute(pay_a, ("tm", "space"), perm_a)
    got_b = lax.ppermute(pay_b, ("tm", "space"), perm_b)
    got_f = lax.ppermute(send_f, "tm", partner)
    got_c = lax.ppermute(send_c, "tm", partner)
    half_shape = (z.fields, 2, z.own, z.lanes)
    msg_shape = (z.fields, z.message // SUB, 2 * SUB, z.lanes)
    edge_shape = (z.fields, z.halo // SUB, 2 * SUB, z.lanes)
    scratch = [
        pltpu.VMEM((2,) + f_shape, BF16),
        pltpu.VMEM((2,) + c_shape, F32),
        pltpu.VMEM((2,) + pay_shape, BF16),
        pltpu.VMEM((z.steps, z.span, z.fields, 2, SUB, z.lanes), F32),
        pltpu.VMEM((z.span + 2, 8, 2, SUB, z.lanes), F32),
        pltpu.VMEM((z.fields * z.fields, SUB, z.lanes), F32),
    ]
    scratch += [pltpu.VMEM((z.span + 2, z.fields, 2, SUB, z.lanes), F32)] * 4
    scratch += [
        pltpu.VMEM((4, z.window, z.lanes), F32),
        pltpu.VMEM((2,) + half_shape, F32),
        pltpu.SemaphoreType.DMA((6,)),
    ]
    carried = ()
    for turn in range(chips):
        first = turn == 0
        active = chips - 1 - turn
        kept, sent, msg, edge = pl.pallas_call(
            functools.partial(chain_kernel, z, first, active),
            out_shape=[
                shape(half_shape, F32),
                shape(half_shape, F32),
                shape(msg_shape, BF16),
                shape(edge_shape, BF16),
            ],
            in_specs=anywhere(6) + ([] if first else in_vmem(2) + anywhere(2)),
            out_specs=anywhere(2) + in_vmem(2),
            input_output_aliases={} if first else {8: 0, 9: 1},
            scratch_shapes=scratch,
            compiler_params=params,
            name="chain",
        )(keep_f, got_f, keep_c, got_c, got_a, got_b, *carried)
        if turn + 1 < chips:
            down = [(device(t, s), device((t - 2) % tm_count, s)) for t, s in everyone]
            across = [
                (device(t, s), device(((t ^ 1) - 2) % tm_count, s + 1 if t % 2 else s - 1)) for t, s in everyone
            ]
            msg = lax.ppermute(msg, ("tm", "space"), down)
            edge = lax.ppermute(edge, ("tm", "space"), across)
            carried = (msg, edge, kept, sent)
    got = lax.ppermute(sent, "tm", partner)
    return pl.pallas_call(
        functools.partial(finish_kernel, z),
        out_shape=shape((1, z.fields, z.rows, z.strip), F32),
        in_specs=in_vmem(2),
        out_specs=pl.BlockSpec(memory_space=pltpu.VMEM),
        compiler_params=params,
        name="finish",
    )(kept, got)


def solution(mesh):
    return jax.shard_map(
        per_device,
        mesh=mesh,
        in_specs=(
            P("tm", None, None, None, "space"),
            P("tm", None, "space"),
            P("tm", None, "space"),
            P("tm", None, "space"),
            P("tm", None, "space"),
            P("tm", None, None),
        ),
        out_specs=P("tm", None, None, "space"),
        check_vma=False,
    )
```

profile of v0, /device:TPU:0, one launch (start us, length us, event | category | flops | bytes accessed | tf_op | source)
XLA Modules:
  0.0 64.3 jit_solution(16858152354861021633)
XLA Ops:
  0.0 0.7 %copy.9.cp = f32[1,6,6]{2,1,0:T(8,128)S(1)} copy(f32[1,6,6]{2,0,1:T(1,128)} %param.11) | data formatting | bytes 288 | tf_op args[5]
  0.7 0.0 copy-start
  0.7 0.9 %copy-done = f32[1,256,128]{2,1,0:T(8,128)S(1)} copy-done((f32[1,256,128]{2,1,0:T(8,128)S(1)}, f32[1,256,128]{2,1,0:T(8,128)}, u32[]{:S(2)}) %copy-start) | copy-done | bytes 131096
  1.6 0.9 %copy-done.1 = f32[1,256,128]{2,1,0:T(8,128)S(1)} copy-done((f32[1,256,128]{2,1,0:T(8,128)S(1)}, f32[1,256,128]{2,1,0:T(8,128)}, u32[]{:S(2)}) %copy-start.1) | copy-done | bytes 131096
  2.5 0.9 %copy-done.2 = f32[1,256,128]{2,1,0:T(8,128)S(1)} copy-done((f32[1,256,128]{2,1,0:T(8,128)S(1)}, f32[1,256,128]{2,1,0:T(8,128)}, u32[]{:S(2)}) %copy-start.2) | copy-done | bytes 131096
  3.4 0.9 %copy-done.3 = f32[1,256,128]{2,1,0:T(8,128)S(1)} copy-done((f32[1,256,128]{2,1,0:T(8,128)S(1)}, f32[1,256,128]{2,1,0:T(8,128)}, u32[]{:S(2)}) %copy-start.3) | copy-done | bytes 131096
  4.3 2.3 %prepare.1 = (bf16[4,6,2,112,128]{4,3,2,1,0:T(8,128)(2,1)S(1)}, bf16[4,6,2,112,128]{4,3,2,1,0:T(8,128)(2,1)S(1)}, f32[5,2,112,128]{3,2,1,0:T(8,128)S(1)}, f32[5,...) custom-call(bf16[1,4,6,256,128]{4,3,2,1,0:T(8,128)(2,1)} %fo.1, ...), custom_call_target="tpu_custom_call" | custom-call | tf_op jit(solution)/shard_map/prepare/pallas_call | solution.py:309
  6.6 0.5 collective-permute-start
  7.2 0.1 collective-permute-start.1
  7.2 5.7 %collective-permute-start.2 = (bf16[72,16,128]{2,1,0:T(8,128)(2,1)S(1)}, bf16[72,16,128]{2,1,0:T(8,128)(2,1)S(1)}, u32[]{:S(2)}, u32[]{:S(2)}) collective-permute-start(bf16[72,16,128]{2,1,0:T(8,128)(2,1)S(1)} %get-tuple-element.21), channel_id=1, source_target_pairs={{0,15},{1,8},{2,9},{3,10},{4,11},{5,12},{6,13},{7,14},{8,1},{9,2},... | collective-permute-start | bytes 884744 | tf_op jit(solution)/shard_map/ppermute | solution.py:333
  12.9 0.0 collective-permute-start.3
  12.9 6.9 %collective-permute-done.2.refs_4_ = bf16[72,16,128]{2,1,0:T(8,128)(2,1)S(1)} collective-permute-done((bf16[72,16,128]{2,1,0:T(8,128)(2,1)S(1)}, bf16[72,16,128]{2,1,0:T(8,128)(2,1)S(1)}, u32[]{:S(2)}, u32[]{:S(2)}) %collective-permute-start.2) | collective-permute-done | bytes 294944 | tf_op jit(solution)/shard_map/ppermute | solution.py:333
  19.8 3.6 %collective-permute-done.3.refs_5_ = bf16[72,16,128]{2,1,0:T(8,128)(2,1)S(1)} collective-permute-done((bf16[72,16,128]{2,1,0:T(8,128)(2,1)S(1)}, bf16[72,16,128]{2,1,0:T(8,128)(2,1)S(1)}, u32[]{:S(2)}, u32[]{:S(2)}) %collective-permute-start.3) | collective-permute-done | bytes 294944 | tf_op jit(solution)/shard_map/ppermute | solution.py:334
  23.3 0.0 collective-permute-done.1.refs_3_
  23.3 0.0 collective-permute-done.refs_1_
  23.3 0.1 chain.2
  23.4 14.6 %collective-permute-start.4 = (bf16[6,11,16,128]{3,2,1,0:T(8,128)(2,1)S(1)}, bf16[6,11,16,128]{3,2,1,0:T(8,128)(2,1)S(1)}, u32[]{:S(2)}, u32[]{:S(2)}) collective-permute-start(bf16[6,11,16,128]{3,2,1,0:T(8,128)(2,1)S(1)} %get-tuple-element.23), channel_id=1, source_target_pairs={{0,16},{1,17},{2,18},{3,19},{4,20},{5,21},{6,22},{7,23},{8,24},{9,... | collective-permute-start | bytes 811016 | tf_op jit(solution)/shard_map/ppermute | solution.py:378
  38.0 3.0 %collective-permute-start.5 = (bf16[6,3,16,128]{3,2,1,0:T(8,128)(2,1)S(1)}, bf16[6,3,16,128]{3,2,1,0:T(8,128)(2,1)S(1)}, u32[]{:S(2)}, u32[]{:S(2)}) collective-permute-start(bf16[6,3,16,128]{3,2,1,0:T(8,128)(2,1)S(1)} %get-tuple-element.24), channel_id=1, source_target_pairs={{0,31},{1,24},{2,25},{3,26},{4,27},{5,28},{6,29},{7,30},{8,17},{9,... | collective-permute-start | bytes 221192 | tf_op jit(solution)/shard_map/ppermute | solution.py:379
  41.0 4.5 %collective-permute-done.5.refs_7_ = bf16[6,3,16,128]{3,2,1,0:T(8,128)(2,1)S(1)} collective-permute-done((bf16[6,3,16,128]{3,2,1,0:T(8,128)(2,1)S(1)}, bf16[6,3,16,128]{3,2,1,0:T(8,128)(2,1)S(1)}, u32[]{:S(2)}, u32[]{:S(2)}) %collective-permute-start.5) | collective-permute-done | bytes 73760 | tf_op jit(solution)/shard_map/ppermute | solution.py:379
  45.5 0.3 collective-permute-done.4.refs_6_
  45.8 15.2 %chain.3 = (f32[6,2,64,128]{3,2,1,0:T(8,128)S(1)}, f32[6,2,64,128]{3,2,1,0:T(8,128)S(1)}, bf16[6,11,16,128]{3,2,1,0:T(8,128)(2,1)}, bf16[6,3,16,128]{3,2,1,0:T(8,128)(2,1)}) custom-call(bf16[4,6,2,112,128]{4,3,2,1,0:T(8,128)(2,1)S(1)} %get-tuple-element.17.refs_0_, ...), custom_call_target="tpu_custom_call", output_to_operand_aliasing={{0}: (8, {}), {1}: (9, {})} | custom-call | tf_op jit(solution)/shard_map/chain/pallas_call | solution.py:358
  61.0 0.8 %collective-permute-start.6 = (f32[6,2,64,128]{3,2,1,0:T(8,128)S(1)}, f32[6,2,64,128]{3,2,1,0:T(8,128)S(1)}, u32[]{:S(2)}, u32[]{:S(2)}) collective-permute-start(f32[6,2,64,128]{3,2,1,0:T(8,128)S(1)} %get-tuple-element.28), channel_id=1, source_target_pairs={{0,8},{8,0},{16,24},{24,16},{1,9},{9,1},{17,25},{25,17},{2,10},{10... | collective-permute-start | bytes 1179656 | tf_op jit(solution)/shard_map/ppermute | solution.py:381
  61.8 1.3 %collective-permute-done.6.got = f32[6,2,64,128]{3,2,1,0:T(8,128)S(1)} collective-permute-done((f32[6,2,64,128]{3,2,1,0:T(8,128)S(1)}, f32[6,2,64,128]{3,2,1,0:T(8,128)S(1)}, u32[]{:S(2)}, u32[]{:S(2)}) %collective-permute-start.6) | collective-permute-done | bytes 393248 | tf_op jit(solution)/shard_map/ppermute | solution.py:381
  63.1 1.2 %finish.1 = f32[1,6,256,128]{3,2,1,0:T(8,128)} custom-call(f32[6,2,64,128]{3,2,1,0:T(8,128)S(1)} %get-tuple-element.27.keep, f32[6,2,64,128]{3,2,1,0:T(8,128)S(1)} %collective-permute-done.6.got), custom_call_target="tpu_custom_call" | custom-call | tf_op jit(solution)/shard_map/finish/pallas_call | solution.py:382
  (3 shorter events, 0.0 us)
Async XLA Ops:
  0.7 0.9 %copy-start = (f32[1,256,128]{2,1,0:T(8,128)S(1)}, f32[1,256,128]{2,1,0:T(8,128)}, u32[]{:S(2)}) copy-start(f32[1,256,128]{2,1,0:T(8,128)} %zc.1) | copy-start | bytes 393220
  1.6 0.9 %copy-start.1 = (f32[1,256,128]{2,1,0:T(8,128)S(1)}, f32[1,256,128]{2,1,0:T(8,128)}, u32[]{:S(2)}) copy-start(f32[1,256,128]{2,1,0:T(8,128)} %mc.1) | copy-start | bytes 393220
  2.5 0.9 %copy-start.2 = (f32[1,256,128]{2,1,0:T(8,128)S(1)}, f32[1,256,128]{2,1,0:T(8,128)}, u32[]{:S(2)}) copy-start(f32[1,256,128]{2,1,0:T(8,128)} %zf.1) | copy-start | bytes 393220
  3.4 0.9 %copy-start.3 = (f32[1,256,128]{2,1,0:T(8,128)S(1)}, f32[1,256,128]{2,1,0:T(8,128)}, u32[]{:S(2)}) copy-start(f32[1,256,128]{2,1,0:T(8,128)} %mf.1) | copy-start | bytes 393220
  6.6 16.7 %collective-permute-start = (bf16[4,6,2,112,128]{4,3,2,1,0:T(8,128)(2,1)S(1)}, bf16[4,6,2,112,128]{4,3,2,1,0:T(8,128)(2,1)S(1)}, u32[]{:S(2)}, u32[]{:S(2)}) collective-permute-start(bf16[4,6,2,112,128]{4,3,2,1,0:T(8,128)(2,1)S(1)} %get-tuple-element.18), channel_id=1, source_target_pairs={{0,8},{8,0},{16,24},{24,16},{1,9},{9,1},{17,25},{25,17},{2,10},{10... | collective-permute-start | bytes 4128776 | tf_op jit(solution)/shard_map/ppermute | solution.py:335
  7.2 16.2 %collective-permute-start.1 = (f32[5,2,112,128]{3,2,1,0:T(8,128)S(1)}, f32[5,2,112,128]{3,2,1,0:T(8,128)S(1)}, u32[]{:S(2)}, u32[]{:S(2)}) collective-permute-start(f32[5,2,112,128]{3,2,1,0:T(8,128)S(1)} %get-tuple-element.20), channel_id=1, source_target_pairs={{0,8},{8,0},{16,24},{24,16},{1,9},{9,1},{17,25},{25,17},{2,10},{10... | collective-permute-start | bytes 1720328 | tf_op jit(solution)/shard_map/ppermute | solution.py:336
  7.2 12.5 %collective-permute-start.2 = (bf16[72,16,128]{2,1,0:T(8,128)(2,1)S(1)}, bf16[72,16,128]{2,1,0:T(8,128)(2,1)S(1)}, u32[]{:S(2)}, u32[]{:S(2)}) collective-permute-start(bf16[72,16,128]{2,1,0:T(8,128)(2,1)S(1)} %get-tuple-element.21), channel_id=1, source_target_pairs={{0,15},{1,8},{2,9},{3,10},{4,11},{5,12},{6,13},{7,14},{8,1},{9,2},... | collective-permute-start | bytes 884744 | tf_op jit(solution)/shard_map/ppermute | solution.py:333
  12.9 10.4 %collective-permute-start.3 = (bf16[72,16,128]{2,1,0:T(8,128)(2,1)S(1)}, bf16[72,16,128]{2,1,0:T(8,128)(2,1)S(1)}, u32[]{:S(2)}, u32[]{:S(2)}) collective-permute-start(bf16[72,16,128]{2,1,0:T(8,128)(2,1)S(1)} %get-tuple-element.22), channel_id=1, source_target_pairs={{0,1},{1,2},{2,3},{3,4},{4,5},{5,6},{6,7},{7,0},{8,15},{9,8},{10,9... | collective-permute-start | bytes 884744 | tf_op jit(solution)/shard_map/ppermute | solution.py:334
  23.4 22.4 %collective-permute-start.4 = (bf16[6,11,16,128]{3,2,1,0:T(8,128)(2,1)S(1)}, bf16[6,11,16,128]{3,2,1,0:T(8,128)(2,1)S(1)}, u32[]{:S(2)}, u32[]{:S(2)}) collective-permute-start(bf16[6,11,16,128]{3,2,1,0:T(8,128)(2,1)S(1)} %get-tuple-element.23), channel_id=1, source_target_pairs={{0,16},{1,17},{2,18},{3,19},{4,20},{5,21},{6,22},{7,23},{8,24},{9,... | collective-permute-start | bytes 811016 | tf_op jit(solution)/shard_map/ppermute | solution.py:378
  38.0 7.5 %collective-permute-start.5 = (bf16[6,3,16,128]{3,2,1,0:T(8,128)(2,1)S(1)}, bf16[6,3,16,128]{3,2,1,0:T(8,128)(2,1)S(1)}, u32[]{:S(2)}, u32[]{:S(2)}) collective-permute-start(bf16[6,3,16,128]{3,2,1,0:T(8,128)(2,1)S(1)} %get-tuple-element.24), channel_id=1, source_target_pairs={{0,31},{1,24},{2,25},{3,26},{4,27},{5,28},{6,29},{7,30},{8,17},{9,... | collective-permute-start | bytes 221192 | tf_op jit(solution)/shard_map/ppermute | solution.py:379
  61.0 2.2 %collective-permute-start.6 = (f32[6,2,64,128]{3,2,1,0:T(8,128)S(1)}, f32[6,2,64,128]{3,2,1,0:T(8,128)S(1)}, u32[]{:S(2)}, u32[]{:S(2)}) collective-permute-start(f32[6,2,64,128]{3,2,1,0:T(8,128)S(1)} %get-tuple-element.28), channel_id=1, source_target_pairs={{0,8},{8,0},{16,24},{24,16},{1,9},{9,1},{17,25},{25,17},{2,10},{10... | collective-permute-start | bytes 1179656 | tf_op jit(solution)/shard_map/ppermute | solution.py:381
where the time goes:
time: 64.5 us; the launch traced here: 64.3 us
  starting transfers between devices  24.7 us (38%)
  Pallas kernels  18.7 us (29%)
  waiting for transfers between devices  16.5 us (26%)
  local copies, waits for them, and re-layouts  4.3 us (7%)
    pallas_call x2, Pallas kernels, per_device(): pl.pallas_call(functools.partial(chain_kernel, z, first, active), out_sha...  15.2 us
    ppermute x1, starting transfers between devices, per_device(): msg = lax.ppermute(msg, ('tm', 'space'), down)  14.6 us
    ppermute x1, waiting for transfers between devices, per_device(): got_a = lax.ppermute(pay_a, ('tm', 'space'), perm_a)  6.86 us
    ppermute x1, starting transfers between devices, per_device(): got_a = lax.ppermute(pay_a, ('tm', 'space'), perm_a)  5.67 us
    ppermute x1, waiting for transfers between devices, per_device(): edge = lax.ppermute(edge, ('tm', 'space'), across)  4.47 us
    unnamed x9, local copies, waits for them, and re-layouts  4.3 us
    ppermute x1, waiting for transfers between devices, per_device(): got_b = lax.ppermute(pay_b, ('tm', 'space'), perm_b)  3.56 us
    ppermute x1, starting transfers between devices, per_device(): edge = lax.ppermute(edge, ('tm', 'space'), across)  3.02 us
  transfers between devices with their start and end apart: 7, of which 5 were waited for; matrix products, arithmetic and copies ran while one was open for 0% of the time, Pallas kernels for 0%

commit v1 on v0

v1 whole, which is shorter than its diff:
```python
import functools

import jax
import jax.numpy as jnp
from jax import lax
from jax.experimental import pallas as pl
from jax.experimental.pallas import tpu as pltpu
from jax.sharding import PartitionSpec as P

SWEEPS = 2
OMEGA = 0.4
SUB = 8
REACH = SWEEPS + 1
VMEM_BYTES = 20 * 2**20
F32 = jnp.float32
BF16 = jnp.bfloat16


class Sizes:
    def __init__(self, forcing_shape):
        _, self.steps, self.fields, self.rows, self.strip = forcing_shape
        self.lanes = self.rows // 2
        self.halo = 2 * REACH * self.steps
        self.main = self.strip // 2 + 2 * self.halo
        self.window = self.main + self.halo
        self.span = self.window // SUB
        self.shift = self.strip - self.main
        self.own = self.strip // 2
        self.groups = [-(-REACH * (self.steps + k) // SUB) for k in range(self.steps)]
        self.group_start = [self.fields * sum(self.groups[:k]) for k in range(self.steps)]
        self.coef_start = self.fields * sum(self.groups)
        self.coef_groups = self.halo // SUB
        self.payload = self.coef_start + 4 * self.coef_groups
        self.message = self.own + self.halo


def half_and_chip():
    tm = lax.axis_index("tm")
    return lax.rem(tm, 2), tm // 2


def prepare_kernel(z, fo_in, zc, mc, zf, mf, cp_in, keep_f, send_f, keep_c, send_c, pay_a, pay_b, fo, co, cp, buf, sems):
    half, _ = half_and_chip()
    left = half == 0
    row = lax.broadcasted_iota(jnp.int32, (z.rows, z.strip), 0)
    coef_copies = [
        pltpu.make_async_copy(ref.at[0], co.at[c], sems.at[c]) for c, ref in enumerate((zf, mf, zc, mc))
    ]
    forcing_copies = [pltpu.make_async_copy(fo_in.at[0, k], fo.at[k], sems.at[5 + k]) for k in range(z.steps)]
    mixing_copy = pltpu.make_async_copy(cp_in, cp, sems.at[4])
    for copy in coef_copies + [mixing_copy] + forcing_copies:
        copy.start()

    def columns(values, slot):
        buf[slot] = values
        return [buf[slot, pl.ds(p, z.lanes, stride=2), :].T for p in range(2)]

    def split(both, groups, start, keep, send):
        for p in range(2):
            low, high = both[p][: z.main], both[p][z.shift :]
            keep[p] = jnp.where(left, low, high).astype(keep.dtype)
            send[p] = jnp.where(left, high, low).astype(send.dtype)
        for g in range(groups):
            lo, hi = SUB * g, z.strip - SUB * (groups - g)
            west = jnp.concatenate([both[p][lo : lo + SUB] for p in range(2)], axis=0)
            east = jnp.concatenate([both[p][hi : hi + SUB] for p in range(2)], axis=0)
            pay_a[start + g] = jnp.where(left, west, east).astype(BF16)
            pay_b[start + g] = jnp.where(left, east, west).astype(BF16)

    slots = buf.shape[0]
    count = 0
    for c in range(4):
        coef_copies[c].wait()
        values = co[c]
        if c == 1:
            values = jnp.where(row < z.rows - 1, values, jnp.zeros_like(values))
        both = columns(values, count % slots)
        split(both, z.coef_groups, z.coef_start + c * z.coef_groups, keep_c.at[c], send_c.at[c])
        count += 1
    mixing_copy.wait()
    for ref in (keep_c, send_c):
        for g in range(z.fields):
            ref[4, 0, g : g + 1, : z.fields] = cp[g]
    for k in range(z.steps):
        forcing_copies[k].wait()
        for f in range(z.fields):
            both = columns(fo[k, f].astype(F32), count % slots)
            split(both, z.groups[k], z.group_start[k] + f * z.groups[k], keep_f.at[k, f], send_f.at[k, f])
            count += 1


def fill_ghosts(ref, span, count):
    for n in range(count):
        for p in range(2):
            ref[0, n, p] = pltpu.roll(ref[span, n, p], 1, 0)
            ref[span + 1, n, p] = pltpu.roll(ref[1, n, p], SUB - 1, 0)


class Band:
    def __init__(self, z, scratch):
        self.z = z
        self.r, self.u1, self.u2, self.pz, self.co, self.kk = scratch
        self.lane = lax.broadcasted_iota(jnp.int32, (SUB, z.lanes), 1)

    def east(self, v):
        return pltpu.roll(v, 1, 1)

    def west(self, v):
        return pltpu.roll(v, self.z.lanes - 1, 1)

    def set_operators(self, rows_c, q, offset, span):
        z, u1, co = self.z, self.u1, self.co
        for c in range(4):
            for p in range(2):
                for i in range(span):
                    u1[i + 1, c, p] = rows_c[q, c, p, pl.ds(offset + i, SUB, stride=span), :]
        fill_ghosts(u1, span, 1)
        for i in range(1, span + 1):
            be, bo = u1[i, 1, 0], u1[i, 1, 1]
            south = (self.east(bo), be)
            for p in range(2):
                a, aw, b = u1[i, 0, p], u1[i - 1, 0, p], u1[i, 1, p]
                co[i, 0, p] = 1.0 - OMEGA * (1.0 + (a + aw) + (b + south[p]))
                co[i, 1, p] = OMEGA * a
                co[i, 2, p] = OMEGA * aw
                co[i, 3, p] = OMEGA * b
                co[i, 4, p] = OMEGA * south[p]
                co[i, 5, p] = (0.5 * OMEGA) * u1[i, 2, p]
                co[i, 6, p] = (0.5 * OMEGA) * u1[i, 3, p]
        for g in range(z.fields):
            for f in range(z.fields):
                value = rows_c[q, 4, 0, g : g + 1, f : f + 1]
                if f == g:
                    value = value + 1.0
                self.kk[g * z.fields + f] = jnp.broadcast_to(OMEGA * value, (SUB, z.lanes))

    def load(self, at, offset, span):
        for i in range(span):
            for f in range(self.z.fields):
                for p in range(2):
                    self.r[i + 1, f, p] = at[f, p, pl.ds(offset + i, SUB, stride=span), :]

    def store(self, at, span):
        for i in range(span):
            for f in range(self.z.fields):
                for p in range(2):
                    at[f, p, pl.ds(i, SUB, stride=span), :] = self.r[i + 1, f, p]

    def sweep(self, src, dst, i, source):
        co = self.co
        ga = [co[i, c, 0] for c in range(5)]
        gb = [co[i, c, 1] for c in range(5)]
        for f in range(self.z.fields):
            a, b = src[i, f, 0], src[i, f, 1]
            va = ga[0] * a + ga[1] * src[i + 1, f, 0] + ga[2] * src[i - 1, f, 0] + ga[3] * b + ga[4] * self.east(b)
            vb = gb[0] * b + gb[1] * src[i + 1, f, 1] + gb[2] * src[i - 1, f, 1] + gb[3] * self.west(a) + gb[4] * a
            va = va + (a if source is None else source[i, f, 0])
            vb = vb + (b if source is None else source[i, f, 1])
            dst[i, f, 0] = va
            dst[i, f, 1] = vb
            if source is not None:
                self.pz[i, f, 0] = co[i, 5, 0] * va
                self.pz[i, f, 1] = co[i, 5, 1] * vb

    def step(self, forcing, offset, span):
        z, r, u1, u2, pz, co, kk = self.z, self.r, self.u1, self.u2, self.pz, self.co, self.kk
        zero = jnp.zeros((SUB, z.lanes), F32)
        fill_ghosts(r, span, z.fields)
        for i in range(1, span + 1):
            self.sweep(r, u1, i, None)
        fill_ghosts(u1, span, z.fields)
        for i in range(1, span + 1):
            self.sweep(u1, u2, i, r)
        fill_ghosts(pz, span, z.fields)
        for i in range(1, span + 1):
            us = [[u2[i, g, p] for p in range(2)] for g in range(z.fields)]
            for f in range(z.fields):
                qa, qb = co[i, 6, 0] * us[f][0], co[i, 6, 1] * us[f][1]
                qba = jnp.where(self.lane == 0, zero, self.east(qb))
                qab = jnp.where(self.lane == z.lanes - 1, zero, self.west(qa))
                oa = (pz[i + 1, f, 0] - pz[i - 1, f, 0]) + (qb - qba)
                ob = (pz[i + 1, f, 1] - pz[i - 1, f, 1]) + (qab - qa)
                for g in range(z.fields):
                    w = kk[g * z.fields + f]
                    oa = oa + w * us[g][0]
                    ob = ob + w * us[g][1]
                rows = pl.ds(offset + i - 1, SUB, stride=span)
                r[i, f, 0] = oa + forcing[f, 0, rows, :]
                r[i, f, 1] = ob + forcing[f, 1, rows, :]

    def steps(self, rows_f, q, begin, offset, span):
        last = self.z.steps - 1

        def one(n, carry):
            self.step(rows_f.at[q, last - n], offset, span)
            return carry

        lax.fori_loop(begin, last + 1, one, 0)


def aligned(offset, count):
    return pl.ds(pl.multiple_of(offset, SUB), count)


def inner_kernel(z, active, kf, rf, kc, rc, rows_f, rows_c, inner, *scratch):
    half, chip = half_and_chip()
    main_at = z.halo * (1 - half)
    blank = jnp.zeros((z.halo, z.lanes), F32)

    def put(ref, values):
        ref[aligned(main_at, z.main), :] = values.astype(F32)
        ref[aligned(z.main * half, z.halo), :] = blank

    for q, forcing, coefs in ((1 - half, kf, kc), (half, rf, rc)):
        for c in range(4):
            for p in range(2):
                put(rows_c.at[q, c, p], coefs[c, p])
        rows_c[q, 4, 0, :SUB, :] = coefs[4, 0, :SUB, :]
        for k in range(z.steps):
            for f in range(z.fields):
                for p in range(2):
                    put(rows_f.at[q, k, f, p], forcing[k, f, p])

    @pl.when(chip == active)
    def _():
        band = Band(z, scratch)
        span = z.main // SUB
        band.load(rows_f.at[0, z.steps - 1], main_at, span)

        def sub_window(q, carry):
            band.set_operators(rows_c, q, main_at, span)
            band.steps(rows_f, q, 1 - q, main_at, span)
            band.store(inner.at[q], span)
            return carry

        lax.fori_loop(0, 2, sub_window, 0)


def tile_of(ref, f, at):
    return jnp.concatenate([ref[f, p, at, :] for p in range(2)], axis=0).astype(BF16)


def rim_kernel(z, active, ra, rb, inner, rows_f_in, rows_c_in, rows_f, rows_c, ko, so, msg, edge, obuf, tmp, *scratch):
    half, chip = half_and_chip()
    for q, pay in ((half, ra), (1 - half, rb)):

        def put(ref, start, groups):
            for g in range(groups):
                tile = pay[start + g].astype(F32)
                at = jnp.where(half == 0, z.halo - SUB * (groups - g), z.main + SUB * g)
                for p in range(2):
                    ref[p, aligned(at, SUB), :] = tile[SUB * p : SUB * (p + 1)]

        for c in range(4):
            put(rows_c.at[q, c], z.coef_start + c * z.coef_groups, z.coef_groups)
        for k in range(z.steps):
            for f in range(z.fields):
                put(rows_f.at[q, k, f], z.group_start[k] + f * z.groups[k], z.groups[k])

    @pl.when(chip == active)
    def _():
        band = Band(z, scratch)
        span = 3 * z.halo // SUB
        offset = (z.window - 3 * z.halo) * half
        rim = slice(z.halo, 2 * z.halo)
        band.load(rows_f.at[0, z.steps - 1], offset, span)

        def sub_window(q, carry):
            band.set_operators(rows_c, q, offset, span)
            band.steps(rows_f, q, 1 - q, offset, span)
            band.store(tmp, span)
            place = jnp.where(q == half, 1, 0)
            for f in range(z.fields):
                for p in range(2):
                    obuf[place, f, p] = inner[q, f, p, aligned((z.main - z.own) * half, z.own), :]
                    obuf[place, f, p, aligned((z.own - z.halo) * half, z.halo), :] = tmp[f, p, rim, :]
            return carry

        lax.fori_loop(0, 2, sub_window, 0)
        ko[...] = obuf[0]
        so[...] = obuf[1]
        last = inner.at[1]
        for f in range(z.fields):
            for g in range(z.message // SUB):
                msg[f, g] = tile_of(last, f, aligned(z.halo * half + SUB * g, SUB))
            for g in range(z.halo // SUB):
                tile = tile_of(tmp, f, slice(z.halo + SUB * g, z.halo + SUB * (g + 1)))
                edge[f, g] = tile
                msg[f, (z.message - z.halo) // SUB * half + g] = tile


def late_kernel(z, active, msg, edge, rows_f, rows_c, ko_in, so_in, ko, so, obuf, tmp, *scratch):
    half, chip = half_and_chip()

    @pl.when(chip == active)
    def _():
        band = Band(z, scratch)
        wide, narrow = z.main // SUB, (z.main - z.halo) // SUB
        inset = z.halo // 2
        offset = z.halo * half

        def put(ref, f, g, at):
            tile = ref[f, g].astype(F32)
            for p in range(2):
                tmp[f, p, aligned(at, SUB), :] = tile[SUB * p : SUB * (p + 1)]

        for f in range(z.fields):
            for g in range(z.message // SUB):
                put(msg, f, g, z.halo * (1 - half) + SUB * g)
            for g in range(z.halo // SUB):
                put(edge, f, g, z.message * half + SUB * g)
        band.load(tmp, 0, wide)
        band.set_operators(rows_c, 0, offset, wide)
        band.steps(rows_f, 0, 0, offset, wide)
        band.store(tmp, wide)
        for f in range(z.fields):
            for p in range(2):
                obuf[1 - half, f, p] = tmp[f, p, z.halo : z.halo + z.own, :]
        band.load(tmp, inset, narrow)
        band.set_operators(rows_c, 1, offset + inset, narrow)
        band.steps(rows_f, 1, 0, offset + inset, narrow)
        band.store(tmp, narrow)
        for f in range(z.fields):
            for p in range(2):
                obuf[half, f, p] = tmp[f, p, inset : inset + z.own, :]
        ko[...] = obuf[0]
        so[...] = obuf[1]


def finish_kernel(z, keep, got, out):
    half, _ = half_and_chip()
    for f in range(z.fields):
        for p in range(2):
            a, b = keep[f, p], got[f, p]
            west = jnp.where(half == 0, a, b)
            east = jnp.where(half == 0, b, a)
            out[0, f, pl.ds(p, z.lanes, stride=2), :] = jnp.concatenate([west, east], axis=0).T


def shape(dims, dtype):
    return jax.ShapeDtypeStruct(tuple(dims), dtype)


def in_vmem(count):
    return [pl.BlockSpec(memory_space=pltpu.VMEM)] * count


def in_hbm(count):
    return [pl.BlockSpec(memory_space=pltpu.HBM)] * count


def per_device(forcing, zonal_courant, meridional_courant, zonal_faces, meridional_faces, coupling):
    z = Sizes(forcing.shape)
    tm_count, strips = lax.axis_size("tm"), lax.axis_size("space")
    assert tm_count == 4 and z.main % 16 == 0 and z.shift % 16 == 0
    params = pltpu.CompilerParams(vmem_limit_bytes=VMEM_BYTES)
    f_shape = (z.steps, z.fields, 2, z.main, z.lanes)
    c_shape = (5, 2, z.main, z.lanes)
    pay_shape = (z.payload, 2 * SUB, z.lanes)
    keep_f, send_f, keep_c, send_c, pay_a, pay_b = pl.pallas_call(
        functools.partial(prepare_kernel, z),
        out_shape=[
            shape(f_shape, BF16),
            shape(f_shape, BF16),
            shape(c_shape, F32),
            shape(c_shape, F32),
            shape(pay_shape, BF16),
            shape(pay_shape, BF16),
        ],
        in_specs=in_hbm(6),
        out_specs=in_vmem(6),
        scratch_shapes=[
            pltpu.VMEM(forcing.shape[1:], BF16),
            pltpu.VMEM((4, z.rows, z.strip), F32),
            pltpu.VMEM((z.fields, 1, z.fields), F32),
            pltpu.VMEM((4, z.rows, z.strip), F32),
            pltpu.SemaphoreType.DMA((5 + z.steps,)),
        ],
        compiler_params=params,
        name="prepare",
    )(
        *[
            pltpu.with_memory_space_constraint(array, pltpu.HBM)
            for array in (
                forcing,
                zonal_courant,
                meridional_courant,
                zonal_faces,
                meridional_faces,
                jnp.swapaxes(coupling, 0, 1),
            )
        ]
    )

    def device(tm, space):
        return tm * strips + space % strips

    everyone = [(t, s) for t in range(tm_count) for s in range(strips)]
    partner = [(t, t ^ 1) for t in range(tm_count)]
    perm_a = [(device(t, s), device(t ^ 1, s + 1 if t % 2 else s - 1)) for t, s in everyone]
    perm_b = [(device(t, s), device(t, s - 1 if t % 2 else s + 1)) for t, s in everyone]
    got_f = lax.ppermute(send_f, "tm", partner)
    got_c = lax.ppermute(send_c, "tm", partner)
    got_a = lax.ppermute(pay_a, ("tm", "space"), perm_a)
    got_b = lax.ppermute(pay_b, ("tm", "space"), perm_b)

    def band_scratch(span):
        state = pltpu.VMEM((span + 2, z.fields, 2, SUB, z.lanes), F32)
        return [state] * 4 + [
            pltpu.VMEM((span + 2, 7, 2, SUB, z.lanes), F32),
            pltpu.VMEM((z.fields * z.fields, SUB, z.lanes), F32),
        ]

    rows_f_shape = shape((2, z.steps, z.fields, 2, z.window, z.lanes), F32)
    rows_c_shape = shape((2, 5, 2, z.window, z.lanes), F32)
    half_dims = (z.fields, 2, z.own, z.lanes)
    rows_f, rows_c, inner = pl.pallas_call(
        functools.partial(inner_kernel, z, 1),
        out_shape=[rows_f_shape, rows_c_shape, shape((2, z.fields, 2, z.main, z.lanes), F32)],
        in_specs=in_vmem(4),
        out_specs=in_vmem(3),
        scratch_shapes=band_scratch(z.main // SUB),
        compiler_params=params,
        cost_estimate=pl.CostEstimate(flops=10**9, bytes_accessed=2 * 10**7, transcendentals=0),
        name="inner",
    )(keep_f, got_f, keep_c, got_c)
    rows_f, rows_c, kept, sent, msg, edge = pl.pallas_call(
        functools.partial(rim_kernel, z, 1),
        out_shape=[
            rows_f_shape,
            rows_c_shape,
            shape(half_dims, F32),
            shape(half_dims, F32),
            shape((z.fields, z.message // SUB, 2 * SUB, z.lanes), BF16),
            shape((z.fields, z.halo // SUB, 2 * SUB, z.lanes), BF16),
        ],
        in_specs=in_vmem(5),
        out_specs=in_vmem(6),
        input_output_aliases={3: 0, 4: 1},
        scratch_shapes=[
            pltpu.VMEM((2,) + half_dims, F32),
            pltpu.VMEM((z.fields, 2, 3 * z.halo, z.lanes), F32),
        ]
        + band_scratch(3 * z.halo // SUB),
        compiler_params=params,
        name="rim",
    )(got_a, got_b, inner, rows_f, rows_c)
    down = [(device(t, s), device((t - 2) % tm_count, s)) for t, s in everyone]
    across = [(device(t, s), device(((t ^ 1) - 2) % tm_count, s + 1 if t % 2 else s - 1)) for t, s in everyone]
    msg = lax.ppermute(msg, ("tm", "space"), down)
    edge = lax.ppermute(edge, ("tm", "space"), across)
    kept, sent = pl.pallas_call(
        functools.partial(late_kernel, z, 0),
        out_shape=[shape(half_dims, F32), shape(half_dims, F32)],
        in_specs=in_vmem(6),
        out_specs=in_vmem(2),
        input_output_aliases={4: 0, 5: 1},
        scratch_shapes=[
            pltpu.VMEM((2,) + half_dims, F32),
            pltpu.VMEM((z.fields, 2, z.main, z.lanes), F32),
        ]
        + band_scratch(z.main // SUB),
        compiler_params=params,
        name="late",
    )(msg, edge, rows_f, rows_c, kept, sent)
    got = lax.ppermute(sent, "tm", partner)
    return pl.pallas_call(
        functools.partial(finish_kernel, z),
        out_shape=shape((1, z.fields, z.rows, z.strip), F32),
        in_specs=in_vmem(2),
        out_specs=pl.BlockSpec(memory_space=pltpu.VMEM),
        compiler_params=params,
        name="finish",
    )(kept, got)


def solution(mesh):
    return jax.shard_map(
        per_device,
        mesh=mesh,
        in_specs=(
            P("tm", None, None, None, "space"),
            P("tm", None, "space"),
            P("tm", None, "space"),
            P("tm", None, "space"),
            P("tm", None, "space"),
            P("tm", None, None),
        ),
        out_specs=P("tm", None, None, "space"),
        check_vma=False,
    )
```

time: 64.5 us -> 46.9 us (0.73)
  starting transfers between devices: 24.7 us -> 17.4 us
  Pallas kernels: 18.7 us -> 13.3 us
  local copies, waits for them, and re-layouts: 4.3 us -> 0 us
    ppermute x1, starting transfers between devices: 14.6 us -> 7.25 us  [per_device(): msg = lax.ppermute(msg, ('tm', 'space'), down)]
    pallas_call x2 -> x3, Pallas kernels: 15.2 us -> 9.86 us  [the longest x1 9.23 us: per_device(): pl.pallas_call(functools.partial(late_kernel, z, 0), out_shape=[shape(hal...]
    unnamed x9 -> x0, local copies, waits for them, and re-layouts: 4.3 us -> none
  transfers between devices with their start and end apart: 7 -> 7, of which waited for: 5 -> 5; matrix products, arithmetic and copies ran while one was open for 0% -> 0% of each run, Pallas kernels for 0% -> 1%
where the time goes in v1:
time: 46.9 us; the launch traced here: 46.8 us
  starting transfers between devices  17.4 us (37%)
  waiting for transfers between devices  16 us (34%)
  Pallas kernels  13.3 us (28%)
    pallas_call x1, Pallas kernels, per_device(): pl.pallas_call(functools.partial(late_kernel, z, 0), out_shape=[shape(hal...  9.23 us
    ppermute x1, starting transfers between devices, per_device(): msg = lax.ppermute(msg, ('tm', 'space'), down)  7.25 us
    ppermute x1, waiting for transfers between devices, per_device(): got_a = lax.ppermute(pay_a, ('tm', 'space'), perm_a)  6.3 us
    ppermute x1, starting transfers between devices, per_device(): got_a = lax.ppermute(pay_a, ('tm', 'space'), perm_a)  5.67 us
    ppermute x1, waiting for transfers between devices, per_device(): edge = lax.ppermute(edge, ('tm', 'space'), across)  4.43 us
    ppermute x1, waiting for transfers between devices, per_device(): got_b = lax.ppermute(pay_b, ('tm', 'space'), perm_b)  3.56 us
    ppermute x1, starting transfers between devices, per_device(): edge = lax.ppermute(edge, ('tm', 'space'), across)  3.05 us
    pallas_call x1, Pallas kernels, per_device(): pl.pallas_call(functools.partial(prepare_kernel, z), out_shape=[shape(f_s...  2.25 us
  transfers between devices with their start and end apart: 7, of which 5 were waited for; matrix products, arithmetic and copies ran while one was open for 0% of the time, Pallas kernels for 1%

profile of v1, /device:TPU:0, one launch (start us, length us, event | category | flops | bytes accessed | tf_op | source)
XLA Modules:
  0.0 46.8 jit_solution(17306840971632267919)
XLA Ops:
  0.0 2.2 %prepare.1 = (bf16[4,6,2,112,128]{4,3,2,1,0:T(8,128)(2,1)S(1)}, bf16[4,6,2,112,128]{4,3,2,1,0:T(8,128)(2,1)S(1)}, f32[5,2,112,128]{3,2,1,0:T(8,128)S(1)}, f32[5,...) custom-call(bf16[1,4,6,256,128]{4,3,2,1,0:T(8,128)(2,1)} %fo_in.1, ...), custom_call_target="tpu_custom_call" | custom-call | tf_op jit(solution)/shard_map/prepare/pallas_call | solution.py:360
  2.3 0.5 %collective-permute-start.2 = (bf16[4,6,2,112,128]{4,3,2,1,0:T(8,128)(2,1)S(1)}, bf16[4,6,2,112,128]{4,3,2,1,0:T(8,128)(2,1)S(1)}, u32[]{:S(2)}, u32[]{:S(2)}) collective-permute-start(bf16[4,6,2,112,128]{4,3,2,1,0:T(8,128)(2,1)S(1)} %get-tuple-element.25), channel_id=1, source_target_pairs={{0,8},{8,0},{16,24},{24,16},{1,9},{9,1},{17,25},{25,17},{2,10},{10... | collective-permute-start | bytes 4128776 | tf_op jit(solution)/shard_map/ppermute | solution.py:402
  2.8 0.1 collective-permute-start.3
  2.9 5.7 %collective-permute-start = (bf16[72,16,128]{2,1,0:T(8,128)(2,1)S(1)}, bf16[72,16,128]{2,1,0:T(8,128)(2,1)S(1)}, u32[]{:S(2)}, u32[]{:S(2)}) collective-permute-start(bf16[72,16,128]{2,1,0:T(8,128)(2,1)S(1)} %get-tuple-element.22), channel_id=1, source_target_pairs={{0,15},{1,8},{2,9},{3,10},{4,11},{5,12},{6,13},{7,14},{8,1},{9,2},... | collective-permute-start | bytes 884744 | tf_op jit(solution)/shard_map/ppermute | solution.py:404
  8.5 0.0 collective-permute-start.1
  8.5 0.0 collective-permute-done.3.rc
  8.5 0.0 collective-permute-done.2.rf
  8.5 0.5 %inner.1 = (f32[2,4,6,2,136,128]{5,4,3,2,1,0:T(8,128)S(1)}, f32[2,5,2,136,128]{4,3,2,1,0:T(8,128)S(1)}, f32[2,6,2,112,128]{4,3,2,1,0:T(8,128)S(1)}) custom-call(bf16[4,6,2,112,128]{4,3,2,1,0:T(8,128)(2,1)S(1)} %get-tuple-element.24.kf, bf16[4,6,2,112,128]{4,3,2,1,0:T(8,128)(2,1)S(1)} %collective-permute-done.2.rf, ...), custom_call_target="tpu_custom_call" | custom-call | flops 1000000000 | bytes 20000000 | tf_op jit(solution)/shard_map/inner/pallas_call | solution.py:417
  9.1 6.3 %collective-permute-done.ra = bf16[72,16,128]{2,1,0:T(8,128)(2,1)S(1)} collective-permute-done((bf16[72,16,128]{2,1,0:T(8,128)(2,1)S(1)}, bf16[72,16,128]{2,1,0:T(8,128)(2,1)S(1)}, u32[]{:S(2)}, u32[]{:S(2)}) %collective-permute-start) | collective-permute-done | bytes 294944 | tf_op jit(solution)/shard_map/ppermute | solution.py:404
  15.4 3.6 %collective-permute-done.1.rb = bf16[72,16,128]{2,1,0:T(8,128)(2,1)S(1)} collective-permute-done((bf16[72,16,128]{2,1,0:T(8,128)(2,1)S(1)}, bf16[72,16,128]{2,1,0:T(8,128)(2,1)S(1)}, u32[]{:S(2)}, u32[]{:S(2)}) %collective-permute-start.1) | collective-permute-done | bytes 294944 | tf_op jit(solution)/shard_map/ppermute | solution.py:405
  18.9 0.1 rim.1
  19.0 7.3 %collective-permute-start.4 = (bf16[6,11,16,128]{3,2,1,0:T(8,128)(2,1)S(1)}, bf16[6,11,16,128]{3,2,1,0:T(8,128)(2,1)S(1)}, u32[]{:S(2)}, u32[]{:S(2)}) collective-permute-start(bf16[6,11,16,128]{3,2,1,0:T(8,128)(2,1)S(1)} %get-tuple-element.31), channel_id=1, source_target_pairs={{0,16},{1,17},{2,18},{3,19},{4,20},{5,21},{6,22},{7,23},{8,24},{9,... | collective-permute-start | bytes 811016 | tf_op jit(solution)/shard_map/ppermute | solution.py:450
  26.3 3.0 %collective-permute-start.5 = (bf16[6,3,16,128]{3,2,1,0:T(8,128)(2,1)S(1)}, bf16[6,3,16,128]{3,2,1,0:T(8,128)(2,1)S(1)}, u32[]{:S(2)}, u32[]{:S(2)}) collective-permute-start(bf16[6,3,16,128]{3,2,1,0:T(8,128)(2,1)S(1)} %get-tuple-element.32), channel_id=1, source_target_pairs={{0,31},{1,24},{2,25},{3,26},{4,27},{5,28},{6,29},{7,30},{8,17},{9,... | collective-permute-start | bytes 221192 | tf_op jit(solution)/shard_map/ppermute | solution.py:451
  29.3 4.4 %collective-permute-done.5.edge = bf16[6,3,16,128]{3,2,1,0:T(8,128)(2,1)S(1)} collective-permute-done((bf16[6,3,16,128]{3,2,1,0:T(8,128)(2,1)S(1)}, bf16[6,3,16,128]{3,2,1,0:T(8,128)(2,1)S(1)}, u32[]{:S(2)}, u32[]{:S(2)}) %collective-permute-start.5) | collective-permute-done | bytes 73760 | tf_op jit(solution)/shard_map/ppermute | solution.py:451
  33.8 0.4 collective-permute-done.4.msg
  34.2 9.2 %late.1 = (f32[6,2,64,128]{3,2,1,0:T(8,128)S(1)}, f32[6,2,64,128]{3,2,1,0:T(8,128)S(1)}) custom-call(bf16[6,11,16,128]{3,2,1,0:T(8,128)(2,1)S(1)} %collective-permute-done.4.msg, bf16[6,3,16,128]{3,2,1,0:T(8,128)(2,1)S(1)} %collective-permute-done.5.edge, ...), custom_call_target="tpu_custom_call", output_to_operand_aliasing={{0}: (4, {}), {1}: (5, {})} | custom-call | tf_op jit(solution)/shard_map/late/pallas_call | solution.py:452
  43.4 0.9 %collective-permute-start.6 = (f32[6,2,64,128]{3,2,1,0:T(8,128)S(1)}, f32[6,2,64,128]{3,2,1,0:T(8,128)S(1)}, u32[]{:S(2)}, u32[]{:S(2)}) collective-permute-start(f32[6,2,64,128]{3,2,1,0:T(8,128)S(1)} %get-tuple-element.38), channel_id=1, source_target_pairs={{0,8},{8,0},{16,24},{24,16},{1,9},{9,1},{17,25},{25,17},{2,10},{10... | collective-permute-start | bytes 1179656 | tf_op jit(solution)/shard_map/ppermute | solution.py:466
  44.3 1.3 %collective-permute-done.6.got = f32[6,2,64,128]{3,2,1,0:T(8,128)S(1)} collective-permute-done((f32[6,2,64,128]{3,2,1,0:T(8,128)S(1)}, f32[6,2,64,128]{3,2,1,0:T(8,128)S(1)}, u32[]{:S(2)}, u32[]{:S(2)}) %collective-permute-start.6) | collective-permute-done | bytes 393248 | tf_op jit(solution)/shard_map/ppermute | solution.py:466
  45.6 1.2 %finish.1 = f32[1,6,256,128]{3,2,1,0:T(8,128)} custom-call(f32[6,2,64,128]{3,2,1,0:T(8,128)S(1)} %get-tuple-element.37.keep, f32[6,2,64,128]{3,2,1,0:T(8,128)S(1)} %collective-permute-done.6.got), custom_call_target="tpu_custom_call" | custom-call | tf_op jit(solution)/shard_map/finish/pallas_call | solution.py:467
Async XLA Ops:
  2.3 6.3 %collective-permute-start.2 = (bf16[4,6,2,112,128]{4,3,2,1,0:T(8,128)(2,1)S(1)}, bf16[4,6,2,112,128]{4,3,2,1,0:T(8,128)(2,1)S(1)}, u32[]{:S(2)}, u32[]{:S(2)}) collective-permute-start(bf16[4,6,2,112,128]{4,3,2,1,0:T(8,128)(2,1)S(1)} %get-tuple-element.25), channel_id=1, source_target_pairs={{0,8},{8,0},{16,24},{24,16},{1,9},{9,1},{17,25},{25,17},{2,10},{10... | collective-permute-start | bytes 4128776 | tf_op jit(solution)/shard_map/ppermute | solution.py:402
  2.8 5.8 %collective-permute-start.3 = (f32[5,2,112,128]{3,2,1,0:T(8,128)S(1)}, f32[5,2,112,128]{3,2,1,0:T(8,128)S(1)}, u32[]{:S(2)}, u32[]{:S(2)}) collective-permute-start(f32[5,2,112,128]{3,2,1,0:T(8,128)S(1)} %get-tuple-element.27), channel_id=1, source_target_pairs={{0,8},{8,0},{16,24},{24,16},{1,9},{9,1},{17,25},{25,17},{2,10},{10... | collective-permute-start | bytes 1720328 | tf_op jit(solution)/shard_map/ppermute | solution.py:403
  2.9 12.5 %collective-permute-start = (bf16[72,16,128]{2,1,0:T(8,128)(2,1)S(1)}, bf16[72,16,128]{2,1,0:T(8,128)(2,1)S(1)}, u32[]{:S(2)}, u32[]{:S(2)}) collective-permute-start(bf16[72,16,128]{2,1,0:T(8,128)(2,1)S(1)} %get-tuple-element.22), channel_id=1, source_target_pairs={{0,15},{1,8},{2,9},{3,10},{4,11},{5,12},{6,13},{7,14},{8,1},{9,2},... | collective-permute-start | bytes 884744 | tf_op jit(solution)/shard_map/ppermute | solution.py:404
  8.5 10.4 %collective-permute-start.1 = (bf16[72,16,128]{2,1,0:T(8,128)(2,1)S(1)}, bf16[72,16,128]{2,1,0:T(8,128)(2,1)S(1)}, u32[]{:S(2)}, u32[]{:S(2)}) collective-permute-start(bf16[72,16,128]{2,1,0:T(8,128)(2,1)S(1)} %get-tuple-element.23), channel_id=1, source_target_pairs={{0,1},{1,2},{2,3},{3,4},{4,5},{5,6},{6,7},{7,0},{8,15},{9,8},{10,9... | collective-permute-start | bytes 884744 | tf_op jit(solution)/shard_map/ppermute | solution.py:405
  19.0 15.1 %collective-permute-start.4 = (bf16[6,11,16,128]{3,2,1,0:T(8,128)(2,1)S(1)}, bf16[6,11,16,128]{3,2,1,0:T(8,128)(2,1)S(1)}, u32[]{:S(2)}, u32[]{:S(2)}) collective-permute-start(bf16[6,11,16,128]{3,2,1,0:T(8,128)(2,1)S(1)} %get-tuple-element.31), channel_id=1, source_target_pairs={{0,16},{1,17},{2,18},{3,19},{4,20},{5,21},{6,22},{7,23},{8,24},{9,... | collective-permute-start | bytes 811016 | tf_op jit(solution)/shard_map/ppermute | solution.py:450
  26.3 7.5 %collective-permute-start.5 = (bf16[6,3,16,128]{3,2,1,0:T(8,128)(2,1)S(1)}, bf16[6,3,16,128]{3,2,1,0:T(8,128)(2,1)S(1)}, u32[]{:S(2)}, u32[]{:S(2)}) collective-permute-start(bf16[6,3,16,128]{3,2,1,0:T(8,128)(2,1)S(1)} %get-tuple-element.32), channel_id=1, source_target_pairs={{0,31},{1,24},{2,25},{3,26},{4,27},{5,28},{6,29},{7,30},{8,17},{9,... | collective-permute-start | bytes 221192 | tf_op jit(solution)/shard_map/ppermute | solution.py:451
  43.4 2.2 %collective-permute-start.6 = (f32[6,2,64,128]{3,2,1,0:T(8,128)S(1)}, f32[6,2,64,128]{3,2,1,0:T(8,128)S(1)}, u32[]{:S(2)}, u32[]{:S(2)}) collective-permute-start(f32[6,2,64,128]{3,2,1,0:T(8,128)S(1)} %get-tuple-element.38), channel_id=1, source_target_pairs={{0,8},{8,0},{16,24},{24,16},{1,9},{9,1},{17,25},{25,17},{2,10},{10... | collective-permute-start | bytes 1179656 | tf_op jit(solution)/shard_map/ppermute | solution.py:466

commit v2 on v1

--- a/solution.py
+++ b/solution.py
@@ -32,6 +32,9 @@
         self.coef_groups = self.halo // SUB
         self.payload = self.coef_start + 4 * self.coef_groups
         self.message = self.own + self.halo
+        self.core = self.message - self.halo
+        self.wide, self.narrow = self.main // SUB, (self.main - self.halo) // SUB
+        self.inset = self.halo // 2
 
 
 def half_and_chip():
@@ -120,7 +123,9 @@
             south = (self.east(bo), be)
             for p in range(2):
                 a, aw, b = u1[i, 0, p], u1[i - 1, 0, p], u1[i, 1, p]
-                co[i, 0, p] = 1.0 - OMEGA * (1.0 + (a + aw) + (b + south[p]))
+                centre = 1.0 - OMEGA * (1.0 + (a + aw) + (b + south[p]))
+                co[i, 0, p] = centre
+                co[i, 7, p] = 1.0 + centre
                 co[i, 1, p] = OMEGA * a
                 co[i, 2, p] = OMEGA * aw
                 co[i, 3, p] = OMEGA * b
@@ -148,19 +153,20 @@
 
     def sweep(self, src, dst, i, source):
         co = self.co
-        ga = [co[i, c, 0] for c in range(5)]
-        gb = [co[i, c, 1] for c in range(5)]
+        first = 7 if source is None else 0
+        ga = [co[i, c, 0] for c in (first, 1, 2, 3, 4)]
+        gb = [co[i, c, 1] for c in (first, 1, 2, 3, 4)]
         for f in range(self.z.fields):
             a, b = src[i, f, 0], src[i, f, 1]
             va = ga[0] * a + ga[1] * src[i + 1, f, 0] + ga[2] * src[i - 1, f, 0] + ga[3] * b + ga[4] * self.east(b)
             vb = gb[0] * b + gb[1] * src[i + 1, f, 1] + gb[2] * src[i - 1, f, 1] + gb[3] * self.west(a) + gb[4] * a
-            va = va + (a if source is None else source[i, f, 0])
-            vb = vb + (b if source is None else source[i, f, 1])
+            if source is not None:
+                va = va + source[i, f, 0]
+                vb = vb + source[i, f, 1]
+                self.pz[i, f, 0] = co[i, 5, 0] * va
+                self.pz[i, f, 1] = co[i, 5, 1] * vb
             dst[i, f, 0] = va
             dst[i, f, 1] = vb
-            if source is not None:
-                self.pz[i, f, 0] = co[i, 5, 0] * va
-                self.pz[i, f, 1] = co[i, 5, 1] * vb
 
     def step(self, forcing, offset, span):
         z, r, u1, u2, pz, co, kk = self.z, self.r, self.u1, self.u2, self.pz, self.co, self.kk
@@ -202,7 +208,11 @@
     return pl.ds(pl.multiple_of(offset, SUB), count)
 
 
-def inner_kernel(z, active, kf, rf, kc, rc, rows_f, rows_c, inner, *scratch):
+def tile_of(ref, f, at):
+    return jnp.concatenate([ref[f, p, at, :] for p in range(2)], axis=0).astype(BF16)
+
+
+def inner_kernel(z, active, kf, rf, kc, rc, rows_f, rows_c, inner, core, *scratch):
     half, chip = half_and_chip()
     main_at = z.halo * (1 - half)
     blank = jnp.zeros((z.halo, z.lanes), F32)
@@ -234,13 +244,13 @@
             return carry
 
         lax.fori_loop(0, 2, sub_window, 0)
-
-
-def tile_of(ref, f, at):
-    return jnp.concatenate([ref[f, p, at, :] for p in range(2)], axis=0).astype(BF16)
-
-
-def rim_kernel(z, active, ra, rb, inner, rows_f_in, rows_c_in, rows_f, rows_c, ko, so, msg, edge, obuf, tmp, *scratch):
+        for f in range(z.fields):
+            for g in range(z.core // SUB):
+                core[f, g] = tile_of(inner.at[1], f, slice(z.halo + SUB * g, z.halo + SUB * (g + 1)))
+
+
+def rim_kernel(z, active, ra, rb, inner, rows_f_in, rows_c_in, rows_f, rows_c, ko, so, edge, *refs):
+    late_operators, (obuf, tmp), scratch = refs[:4], refs[4:6], refs[6:]
     half, chip = half_and_chip()
     for q, pay in ((half, ra), (1 - half, rb)):
 
@@ -256,6 +266,12 @@
         for k in range(z.steps):
             for f in range(z.fields):
                 put(rows_f.at[q, k, f], z.group_start[k] + f * z.groups[k], z.groups[k])
+
+    @pl.when(chip != active)
+    def _():
+        for q, span, offset in ((0, z.wide, z.halo * half), (1, z.narrow, z.halo * half + z.inset)):
+            band = Band(z, scratch[:4] + late_operators[2 * q : 2 * q + 2])
+            band.set_operators(rows_c, q, offset, span)
 
     @pl.when(chip == active)
     def _():
@@ -269,6 +285,13 @@
             band.set_operators(rows_c, q, offset, span)
             band.steps(rows_f, q, 1 - q, offset, span)
             band.store(tmp, span)
+
+            @pl.when(q == 1)
+            def _():
+                for f in range(z.fields):
+                    for g in range(z.halo // SUB):
+                        edge[f, g] = tile_of(tmp, f, slice(z.halo + SUB * g, z.halo + SUB * (g + 1)))
+
             place = jnp.where(q == half, 1, 0)
             for f in range(z.fields):
                 for p in range(2):
@@ -279,50 +302,39 @@
         lax.fori_loop(0, 2, sub_window, 0)
         ko[...] = obuf[0]
         so[...] = obuf[1]
-        last = inner.at[1]
-        for f in range(z.fields):
-            for g in range(z.message // SUB):
-                msg[f, g] = tile_of(last, f, aligned(z.halo * half + SUB * g, SUB))
-            for g in range(z.halo // SUB):
-                tile = tile_of(tmp, f, slice(z.halo + SUB * g, z.halo + SUB * (g + 1)))
-                edge[f, g] = tile
-                msg[f, (z.message - z.halo) // SUB * half + g] = tile
-
-
-def late_kernel(z, active, msg, edge, rows_f, rows_c, ko_in, so_in, ko, so, obuf, tmp, *scratch):
+
+
+def late_kernel(z, active, core, near, far, rows_f, ko_in, so_in, co0, kk0, co1, kk1, ko, so, obuf, tmp, *scratch):
     half, chip = half_and_chip()
 
     @pl.when(chip == active)
     def _():
-        band = Band(z, scratch)
-        wide, narrow = z.main // SUB, (z.main - z.halo) // SUB
-        inset = z.halo // 2
         offset = z.halo * half
 
-        def put(ref, f, g, at):
-            tile = ref[f, g].astype(F32)
-            for p in range(2):
-                tmp[f, p, aligned(at, SUB), :] = tile[SUB * p : SUB * (p + 1)]
-
-        for f in range(z.fields):
-            for g in range(z.message // SUB):
-                put(msg, f, g, z.halo * (1 - half) + SUB * g)
-            for g in range(z.halo // SUB):
-                put(edge, f, g, z.message * half + SUB * g)
-        band.load(tmp, 0, wide)
-        band.set_operators(rows_c, 0, offset, wide)
-        band.steps(rows_f, 0, 0, offset, wide)
-        band.store(tmp, wide)
+        def put(ref, at):
+            for f in range(z.fields):
+                for g in range(ref.shape[1]):
+                    tile = ref[f, g].astype(F32)
+                    for p in range(2):
+                        tmp[f, p, aligned(at + SUB * g, SUB), :] = tile[SUB * p : SUB * (p + 1)]
+
+        put(core, 2 * z.halo * (1 - half))
+        put(near, z.halo + (z.core - z.halo) * half)
+        put(far, z.message * half)
+        band = Band(z, scratch + (co0, kk0))
+        band.load(tmp, 0, z.wide)
+        band.steps(rows_f, 0, 0, offset, z.wide)
+        band.store(tmp, z.wide)
         for f in range(z.fields):
             for p in range(2):
                 obuf[1 - half, f, p] = tmp[f, p, z.halo : z.halo + z.own, :]
-        band.load(tmp, inset, narrow)
-        band.set_operators(rows_c, 1, offset + inset, narrow)
-        band.steps(rows_f, 1, 0, offset + inset, narrow)
-        band.store(tmp, narrow)
+        band = Band(z, scratch + (co1, kk1))
+        band.load(tmp, z.inset, z.narrow)
+        band.steps(rows_f, 1, 0, offset + z.inset, z.narrow)
+        band.store(tmp, z.narrow)
         for f in range(z.fields):
             for p in range(2):
-                obuf[half, f, p] = tmp[f, p, inset : inset + z.own, :]
+                obuf[half, f, p] = tmp[f, p, z.inset : z.inset + z.own, :]
         ko[...] = obuf[0]
         so[...] = obuf[1]
 
@@ -406,63 +418,73 @@
 
     def band_scratch(span):
         state = pltpu.VMEM((span + 2, z.fields, 2, SUB, z.lanes), F32)
-        return [state] * 4 + [
-            pltpu.VMEM((span + 2, 7, 2, SUB, z.lanes), F32),
-            pltpu.VMEM((z.fields * z.fields, SUB, z.lanes), F32),
-        ]
+        return [state] * 4
+
+    def operators(span):
+        return [shape(dims, F32) for dims in ((span + 2, 8, 2, SUB, z.lanes), (z.fields**2, SUB, z.lanes))]
+
+    def operator_scratch(span):
+        return [pltpu.VMEM(spec.shape, spec.dtype) for spec in operators(span)]
 
     rows_f_shape = shape((2, z.steps, z.fields, 2, z.window, z.lanes), F32)
     rows_c_shape = shape((2, 5, 2, z.window, z.lanes), F32)
     half_dims = (z.fields, 2, z.own, z.lanes)
-    rows_f, rows_c, inner = pl.pallas_call(
+    def tiles(columns):
+        return shape((z.fields, columns // SUB, 2 * SUB, z.lanes), BF16)
+
+    rows_f, rows_c, inner, core = pl.pallas_call(
         functools.partial(inner_kernel, z, 1),
-        out_shape=[rows_f_shape, rows_c_shape, shape((2, z.fields, 2, z.main, z.lanes), F32)],
+        out_shape=[rows_f_shape, rows_c_shape, shape((2, z.fields, 2, z.main, z.lanes), F32), tiles(z.core)],
         in_specs=in_vmem(4),
-        out_specs=in_vmem(3),
-        scratch_shapes=band_scratch(z.main // SUB),
+        out_specs=in_vmem(4),
+        scratch_shapes=band_scratch(z.wide) + operator_scratch(z.wide),
         compiler_params=params,
         cost_estimate=pl.CostEstimate(flops=10**9, bytes_accessed=2 * 10**7, transcendentals=0),
         name="inner",
     )(keep_f, got_f, keep_c, got_c)
-    rows_f, rows_c, kept, sent, msg, edge = pl.pallas_call(
+    down = [(device(t, s), device(t - 2, s)) for t, s in everyone if t >= 2]
+    across = [(device(t, s), device((t ^ 1) - 2, s + 1 if t % 2 else s - 1)) for t, s in everyone if t >= 2]
+    core = lax.ppermute(core, ("tm", "space"), down)
+    rows_f, rows_c, kept, sent, edge, *late_operators = pl.pallas_call(
         functools.partial(rim_kernel, z, 1),
         out_shape=[
             rows_f_shape,
             rows_c_shape,
             shape(half_dims, F32),
             shape(half_dims, F32),
-            shape((z.fields, z.message // SUB, 2 * SUB, z.lanes), BF16),
-            shape((z.fields, z.halo // SUB, 2 * SUB, z.lanes), BF16),
-        ],
+            tiles(z.halo),
+        ]
+        + operators(z.wide)
+        + operators(z.narrow),
         in_specs=in_vmem(5),
-        out_specs=in_vmem(6),
+        out_specs=in_vmem(9),
         input_output_aliases={3: 0, 4: 1},
         scratch_shapes=[
             pltpu.VMEM((2,) + half_dims, F32),
             pltpu.VMEM((z.fields, 2, 3 * z.halo, z.lanes), F32),
         ]
-        + band_scratch(3 * z.halo // SUB),
+        + band_scratch(z.wide)
+        + operator_scratch(3 * z.halo // SUB),
         compiler_params=params,
+        cost_estimate=pl.CostEstimate(flops=10**9, bytes_accessed=2 * 10**7, transcendentals=0),
         name="rim",
     )(got_a, got_b, inner, rows_f, rows_c)
-    down = [(device(t, s), device((t - 2) % tm_count, s)) for t, s in everyone]
-    across = [(device(t, s), device(((t ^ 1) - 2) % tm_count, s + 1 if t % 2 else s - 1)) for t, s in everyone]
-    msg = lax.ppermute(msg, ("tm", "space"), down)
-    edge = lax.ppermute(edge, ("tm", "space"), across)
+    far = lax.ppermute(edge, ("tm", "space"), across)
+    near = lax.ppermute(edge, ("tm", "space"), down)
     kept, sent = pl.pallas_call(
         functools.partial(late_kernel, z, 0),
         out_shape=[shape(half_dims, F32), shape(half_dims, F32)],
-        in_specs=in_vmem(6),
+        in_specs=in_vmem(10),
         out_specs=in_vmem(2),
         input_output_aliases={4: 0, 5: 1},
         scratch_shapes=[
             pltpu.VMEM((2,) + half_dims, F32),
             pltpu.VMEM((z.fields, 2, z.main, z.lanes), F32),
         ]
-        + band_scratch(z.main // SUB),
+        + band_scratch(z.wide),
         compiler_params=params,
         name="late",
-    )(msg, edge, rows_f, rows_c, kept, sent)
+    )(core, near, far, rows_f, kept, sent, *late_operators)
     got = lax.ppermute(sent, "tm", partner)
     return pl.pallas_call(
         functools.partial(finish_kernel, z),

time: 46.9 us -> 43.4 us (0.925)
  starting transfers between devices: 17.4 us -> 10.3 us
  waiting for transfers between devices: 16 us -> 20.9 us
  Pallas kernels: 13.3 us -> 11.9 us
    ppermute x2 -> x3, starting transfers between devices: 10.3 us -> 3.88 us  [the longest x1 1.29 us: per_device(): core = lax.ppermute(core, ('tm', 'space'), down)]
    ppermute x2 -> x3, waiting for transfers between devices: 4.81 us -> 10.8 us  [the longest x1 10.8 us: per_device(): far = lax.ppermute(edge, ('tm', 'space'), across)]
    pallas_call x1, Pallas kernels: 9.23 us -> 7.62 us  [per_device(): pl.pallas_call(functools.partial(late_kernel, z, 0), out_shape=[shape(hal...]
    ppermute x1, waiting for transfers between devices: 6.3 us -> 5 us  [per_device(): got_a = lax.ppermute(pay_a, ('tm', 'space'), perm_a)]
    ppermute x1, starting transfers between devices: 0.86 us -> 0.2 us  [per_device(): got = lax.ppermute(sent, 'tm', partner)]
  transfers between devices with their start and end apart: 7 -> 8, of which waited for: 5 -> 4; matrix products, arithmetic and copies ran while one was open for 0% -> 0% of each run, Pallas kernels for 1% -> 2%
where the time goes in v2:
time: 43.4 us; the launch traced here: 43.2 us
  waiting for transfers between devices  20.9 us (48%)
  Pallas kernels  11.9 us (27%)
  starting transfers between devices  10.3 us (24%)
    ppermute x1, waiting for transfers between devices, per_device(): far = lax.ppermute(edge, ('tm', 'space'), across)  10.8 us
    pallas_call x1, Pallas kernels, per_device(): pl.pallas_call(functools.partial(late_kernel, z, 0), out_shape=[shape(hal...  7.62 us
    ppermute x1, starting transfers between devices, per_device(): got_a = lax.ppermute(pay_a, ('tm', 'space'), perm_a)  5.67 us
    ppermute x1, waiting for transfers between devices, per_device(): got_a = lax.ppermute(pay_a, ('tm', 'space'), perm_a)  5 us
    ppermute x1, waiting for transfers between devices, per_device(): got_b = lax.ppermute(pay_b, ('tm', 'space'), perm_b)  3.56 us
    pallas_call x1, Pallas kernels, per_device(): pl.pallas_call(functools.partial(prepare_kernel, z), out_shape=[shape(f_s...  2.25 us
    ppermute x1, waiting for transfers between devices, per_device(): got = lax.ppermute(sent, 'tm', partner)  1.58 us
    ppermute x1, starting transfers between devices, per_device(): core = lax.ppermute(core, ('tm', 'space'), down)  1.29 us
  transfers between devices with their start and end apart: 8, of which 4 were waited for; matrix products, arithmetic and copies ran while one was open for 0% of the time, Pallas kernels for 2%

profile of v2, /device:TPU:0, one launch (start us, length us, event | category | flops | bytes accessed | tf_op | source)
XLA Modules:
  0.0 43.2 jit_solution(299865933770935410)
XLA Ops:
  0.0 2.2 %prepare.1 = (bf16[4,6,2,112,128]{4,3,2,1,0:T(8,128)(2,1)S(1)}, bf16[4,6,2,112,128]{4,3,2,1,0:T(8,128)(2,1)S(1)}, f32[5,2,112,128]{3,2,1,0:T(8,128)S(1)}, f32[5,...) custom-call(bf16[1,4,6,256,128]{4,3,2,1,0:T(8,128)(2,1)} %fo_in.1, ...), custom_call_target="tpu_custom_call" | custom-call | tf_op jit(solution)/shard_map/prepare/pallas_call | solution.py:372
  2.3 0.5 %collective-permute-start = (bf16[4,6,2,112,128]{4,3,2,1,0:T(8,128)(2,1)S(1)}, bf16[4,6,2,112,128]{4,3,2,1,0:T(8,128)(2,1)S(1)}, u32[]{:S(2)}, u32[]{:S(2)}) collective-permute-start(bf16[4,6,2,112,128]{4,3,2,1,0:T(8,128)(2,1)S(1)} %get-tuple-element.26), channel_id=1, source_target_pairs={{0,8},{8,0},{16,24},{24,16},{1,9},{9,1},{17,25},{25,17},{2,10},{10... | collective-permute-start | bytes 4128776 | tf_op jit(solution)/shard_map/ppermute | solution.py:414
  2.8 0.1 collective-permute-start.1
  2.9 5.7 %collective-permute-start.3 = (bf16[72,16,128]{2,1,0:T(8,128)(2,1)S(1)}, bf16[72,16,128]{2,1,0:T(8,128)(2,1)S(1)}, u32[]{:S(2)}, u32[]{:S(2)}) collective-permute-start(bf16[72,16,128]{2,1,0:T(8,128)(2,1)S(1)} %get-tuple-element.30), channel_id=1, source_target_pairs={{0,15},{1,8},{2,9},{3,10},{4,11},{5,12},{6,13},{7,14},{8,1},{9,2},... | collective-permute-start | bytes 884744 | tf_op jit(solution)/shard_map/ppermute | solution.py:416
  8.5 0.0 collective-permute-start.4
  8.5 0.0 collective-permute-done.1.rc
  8.5 0.0 collective-permute-done.rf
  8.5 0.5 %inner.1 = (f32[2,4,6,2,136,128]{5,4,3,2,1,0:T(8,128)S(1)}, f32[2,5,2,136,128]{4,3,2,1,0:T(8,128)S(1)}, f32[2,6,2,112,128]{4,3,2,1,0:T(8,128)S(1)}, bf16[6,8,16,128]{3,2,1,0:T(8,128)(2,1)S(1)}) custom-call(bf16[4,6,2,112,128]{4,3,2,1,0:T(8,128)(2,1)S(1)} %get-tuple-element.25.kf, bf16[4,6,2,112,128]{4,3,2,1,0:T(8,128)(2,1)S(1)} %collective-permute-done.rf, ...), custom_call_target="tpu_custom_call" | custom-call | flops 1000000000 | bytes 20000000 | tf_op jit(solution)/shard_map/inner/pallas_call | solution.py:435
  9.1 1.3 %collective-permute-start.2 = (bf16[6,8,16,128]{3,2,1,0:T(8,128)(2,1)S(1)}, bf16[6,8,16,128]{3,2,1,0:T(8,128)(2,1)S(1)}, u32[]{:S(2)}, u32[]{:S(2)}) collective-permute-start(bf16[6,8,16,128]{3,2,1,0:T(8,128)(2,1)S(1)} %get-tuple-element.29), channel_id=1, source_target_pairs={{16,0},{17,1},{18,2},{19,3},{20,4},{21,5},{22,6},{23,7},{24,8},{25... | collective-permute-start | bytes 589832 | tf_op jit(solution)/shard_map/ppermute | solution.py:447
  10.4 5.0 %collective-permute-done.3.ra = bf16[72,16,128]{2,1,0:T(8,128)(2,1)S(1)} collective-permute-done((bf16[72,16,128]{2,1,0:T(8,128)(2,1)S(1)}, bf16[72,16,128]{2,1,0:T(8,128)(2,1)S(1)}, u32[]{:S(2)}, u32[]{:S(2)}) %collective-permute-start.3) | collective-permute-done | bytes 294944 | tf_op jit(solution)/shard_map/ppermute | solution.py:416
  15.4 3.6 %collective-permute-done.4.rb = bf16[72,16,128]{2,1,0:T(8,128)(2,1)S(1)} collective-permute-done((bf16[72,16,128]{2,1,0:T(8,128)(2,1)S(1)}, bf16[72,16,128]{2,1,0:T(8,128)(2,1)S(1)}, u32[]{:S(2)}, u32[]{:S(2)}) %collective-permute-start.4) | collective-permute-done | bytes 294944 | tf_op jit(solution)/shard_map/ppermute | solution.py:417
  18.9 0.3 rim.1
  19.3 1.3 %collective-permute-start.6 = (bf16[6,3,16,128]{3,2,1,0:T(8,128)(2,1)S(1)}, bf16[6,3,16,128]{3,2,1,0:T(8,128)(2,1)S(1)}, u32[]{:S(2)}, u32[]{:S(2)}) collective-permute-start(bf16[6,3,16,128]{3,2,1,0:T(8,128)(2,1)S(1)} %get-tuple-element.35), channel_id=1, source_target_pairs={{16,15},{17,8},{18,9},{19,10},{20,11},{21,12},{22,13},{23,14},{24,... | collective-permute-start | bytes 221192 | tf_op jit(solution)/shard_map/ppermute | solution.py:472
  20.6 1.3 %collective-permute-start.5 = (bf16[6,3,16,128]{3,2,1,0:T(8,128)(2,1)S(1)}, bf16[6,3,16,128]{3,2,1,0:T(8,128)(2,1)S(1)}, u32[]{:S(2)}, u32[]{:S(2)}) collective-permute-start(bf16[6,3,16,128]{3,2,1,0:T(8,128)(2,1)S(1)} %get-tuple-element.35), channel_id=1, source_target_pairs={{16,0},{17,1},{18,2},{19,3},{20,4},{21,5},{22,6},{23,7},{24,8},{25... | collective-permute-start | bytes 221192 | tf_op jit(solution)/shard_map/ppermute | solution.py:473
  21.9 10.8 %collective-permute-done.6.far = bf16[6,3,16,128]{3,2,1,0:T(8,128)(2,1)S(1)} collective-permute-done((bf16[6,3,16,128]{3,2,1,0:T(8,128)(2,1)S(1)}, bf16[6,3,16,128]{3,2,1,0:T(8,128)(2,1)S(1)}, u32[]{:S(2)}, u32[]{:S(2)}) %collective-permute-start.6) | collective-permute-done | bytes 73760 | tf_op jit(solution)/shard_map/ppermute | solution.py:472
  32.7 0.0 collective-permute-done.5.near
  32.7 0.0 collective-permute-done.2.core
  32.7 7.6 %late.1 = (f32[6,2,64,128]{3,2,1,0:T(8,128)S(1)}, f32[6,2,64,128]{3,2,1,0:T(8,128)S(1)}) custom-call(bf16[6,8,16,128]{3,2,1,0:T(8,128)(2,1)S(1)} %collective-permute-done.2.core, bf16[6,3,16,128]{3,2,1,0:T(8,128)(2,1)S(1)} %collective-permute-done.5.near, ...), custom_call_target="tpu_custom_call", output_to_operand_aliasing={{0}: (4, {}), {1}: (5, {})} | custom-call | tf_op jit(solution)/shard_map/late/pallas_call | solution.py:474
  40.3 0.2 collective-permute-start.7
  40.5 1.6 %collective-permute-done.7.got = f32[6,2,64,128]{3,2,1,0:T(8,128)S(1)} collective-permute-done((f32[6,2,64,128]{3,2,1,0:T(8,128)S(1)}, f32[6,2,64,128]{3,2,1,0:T(8,128)S(1)}, u32[]{:S(2)}, u32[]{:S(2)}) %collective-permute-start.7) | collective-permute-done | bytes 393248 | tf_op jit(solution)/shard_map/ppermute | solution.py:488
  42.1 1.2 %finish.1 = f32[1,6,256,128]{3,2,1,0:T(8,128)} custom-call(f32[6,2,64,128]{3,2,1,0:T(8,128)S(1)} %get-tuple-element.43.keep, f32[6,2,64,128]{3,2,1,0:T(8,128)S(1)} %collective-permute-done.7.got), custom_call_target="tpu_custom_call" | custom-call | tf_op jit(solution)/shard_map/finish/pallas_call | solution.py:489
Async XLA Ops:
  2.3 6.3 %collective-permute-start = (bf16[4,6,2,112,128]{4,3,2,1,0:T(8,128)(2,1)S(1)}, bf16[4,6,2,112,128]{4,3,2,1,0:T(8,128)(2,1)S(1)}, u32[]{:S(2)}, u32[]{:S(2)}) collective-permute-start(bf16[4,6,2,112,128]{4,3,2,1,0:T(8,128)(2,1)S(1)} %get-tuple-element.26), channel_id=1, source_target_pairs={{0,8},{8,0},{16,24},{24,16},{1,9},{9,1},{17,25},{25,17},{2,10},{10... | collective-permute-start | bytes 4128776 | tf_op jit(solution)/shard_map/ppermute | solution.py:414
  2.8 5.8 %collective-permute-start.1 = (f32[5,2,112,128]{3,2,1,0:T(8,128)S(1)}, f32[5,2,112,128]{3,2,1,0:T(8,128)S(1)}, u32[]{:S(2)}, u32[]{:S(2)}) collective-permute-start(f32[5,2,112,128]{3,2,1,0:T(8,128)S(1)} %get-tuple-element.28), channel_id=1, source_target_pairs={{0,8},{8,0},{16,24},{24,16},{1,9},{9,1},{17,25},{25,17},{2,10},{10... | collective-permute-start | bytes 1720328 | tf_op jit(solution)/shard_map/ppermute | solution.py:415
  2.9 12.5 %collective-permute-start.3 = (bf16[72,16,128]{2,1,0:T(8,128)(2,1)S(1)}, bf16[72,16,128]{2,1,0:T(8,128)(2,1)S(1)}, u32[]{:S(2)}, u32[]{:S(2)}) collective-permute-start(bf16[72,16,128]{2,1,0:T(8,128)(2,1)S(1)} %get-tuple-element.30), channel_id=1, source_target_pairs={{0,15},{1,8},{2,9},{3,10},{4,11},{5,12},{6,13},{7,14},{8,1},{9,2},... | collective-permute-start | bytes 884744 | tf_op jit(solution)/shard_map/ppermute | solution.py:416
  8.5 10.4 %collective-permute-start.4 = (bf16[72,16,128]{2,1,0:T(8,128)(2,1)S(1)}, bf16[72,16,128]{2,1,0:T(8,128)(2,1)S(1)}, u32[]{:S(2)}, u32[]{:S(2)}) collective-permute-start(bf16[72,16,128]{2,1,0:T(8,128)(2,1)S(1)} %get-tuple-element.31), channel_id=1, source_target_pairs={{0,1},{1,2},{2,3},{3,4},{4,5},{5,6},{6,7},{7,0},{8,15},{9,8},{10,9... | collective-permute-start | bytes 884744 | tf_op jit(solution)/shard_map/ppermute | solution.py:417
  9.1 23.6 %collective-permute-start.2 = (bf16[6,8,16,128]{3,2,1,0:T(8,128)(2,1)S(1)}, bf16[6,8,16,128]{3,2,1,0:T(8,128)(2,1)S(1)}, u32[]{:S(2)}, u32[]{:S(2)}) collective-permute-start(bf16[6,8,16,128]{3,2,1,0:T(8,128)(2,1)S(1)} %get-tuple-element.29), channel_id=1, source_target_pairs={{16,0},{17,1},{18,2},{19,3},{20,4},{21,5},{22,6},{23,7},{24,8},{25... | collective-permute-start | bytes 589832 | tf_op jit(solution)/shard_map/ppermute | solution.py:447
  19.3 13.4 %collective-permute-start.6 = (bf16[6,3,16,128]{3,2,1,0:T(8,128)(2,1)S(1)}, bf16[6,3,16,128]{3,2,1,0:T(8,128)(2,1)S(1)}, u32[]{:S(2)}, u32[]{:S(2)}) collective-permute-start(bf16[6,3,16,128]{3,2,1,0:T(8,128)(2,1)S(1)} %get-tuple-element.35), channel_id=1, source_target_pairs={{16,15},{17,8},{18,9},{19,10},{20,11},{21,12},{22,13},{23,14},{24,... | collective-permute-start | bytes 221192 | tf_op jit(solution)/shard_map/ppermute | solution.py:472
  20.6 12.1 %collective-permute-start.5 = (bf16[6,3,16,128]{3,2,1,0:T(8,128)(2,1)S(1)}, bf16[6,3,16,128]{3,2,1,0:T(8,128)(2,1)S(1)}, u32[]{:S(2)}, u32[]{:S(2)}) collective-permute-start(bf16[6,3,16,128]{3,2,1,0:T(8,128)(2,1)S(1)} %get-tuple-element.35), channel_id=1, source_target_pairs={{16,0},{17,1},{18,2},{19,3},{20,4},{21,5},{22,6},{23,7},{24,8},{25... | collective-permute-start | bytes 221192 | tf_op jit(solution)/shard_map/ppermute | solution.py:473
  40.3 1.8 %collective-permute-start.7 = (f32[6,2,64,128]{3,2,1,0:T(8,128)S(1)}, f32[6,2,64,128]{3,2,1,0:T(8,128)S(1)}, u32[]{:S(2)}, u32[]{:S(2)}) collective-permute-start(f32[6,2,64,128]{3,2,1,0:T(8,128)S(1)} %get-tuple-element.44), channel_id=1, source_target_pairs={{0,8},{8,0},{16,24},{24,16},{1,9},{9,1},{17,25},{25,17},{2,10},{10... | collective-permute-start | bytes 1179656 | tf_op jit(solution)/shard_map/ppermute | solution.py:488

commit v3 on v2

--- a/solution.py
+++ b/solution.py
@@ -35,6 +35,8 @@
         self.core = self.message - self.halo
         self.wide, self.narrow = self.main // SUB, (self.main - self.halo) // SUB
         self.inset = self.halo // 2
+        self.rim = 3 * self.halo
+        self.base = -self.inset % SUB
 
 
 def half_and_chip():
@@ -145,11 +147,11 @@
                 for p in range(2):
                     self.r[i + 1, f, p] = at[f, p, pl.ds(offset + i, SUB, stride=span), :]
 
-    def store(self, at, span):
+    def store(self, at, span, base=0):
         for i in range(span):
             for f in range(self.z.fields):
                 for p in range(2):
-                    at[f, p, pl.ds(i, SUB, stride=span), :] = self.r[i + 1, f, p]
+                    at[f, p, pl.ds(base + i, SUB, stride=span), :] = self.r[i + 1, f, p]
 
     def sweep(self, src, dst, i, source):
         co = self.co
@@ -250,7 +252,7 @@
 
 
 def rim_kernel(z, active, ra, rb, inner, rows_f_in, rows_c_in, rows_f, rows_c, ko, so, edge, *refs):
-    late_operators, (obuf, tmp), scratch = refs[:4], refs[4:6], refs[6:]
+    late_operators, (obuf, tmp), scratch = refs[:5], refs[5:7], refs[7:]
     half, chip = half_and_chip()
     for q, pay in ((half, ra), (1 - half, rb)):
 
@@ -269,15 +271,19 @@
 
     @pl.when(chip != active)
     def _():
-        for q, span, offset in ((0, z.wide, z.halo * half), (1, z.narrow, z.halo * half + z.inset)):
-            band = Band(z, scratch[:4] + late_operators[2 * q : 2 * q + 2])
-            band.set_operators(rows_c, q, offset, span)
+        co_core, co_rim, co_late, mix_first, mix_last = late_operators
+        for q, co, mix, columns, offset in (
+            (0, co_core, mix_first, z.core, z.halo * (2 - half)),
+            (0, co_rim, mix_first, z.rim, (z.window - z.rim) * half),
+            (1, co_late, mix_last, z.main - z.halo, z.halo * half + z.inset),
+        ):
+            Band(z, scratch[:4] + (co, mix)).set_operators(rows_c, q, offset, columns // SUB)
 
     @pl.when(chip == active)
     def _():
         band = Band(z, scratch)
-        span = 3 * z.halo // SUB
-        offset = (z.window - 3 * z.halo) * half
+        span = z.rim // SUB
+        offset = (z.window - z.rim) * half
         rim = slice(z.halo, 2 * z.halo)
         band.load(rows_f.at[0, z.steps - 1], offset, span)
 
@@ -304,33 +310,54 @@
         so[...] = obuf[1]
 
 
-def late_kernel(z, active, core, near, far, rows_f, ko_in, so_in, co0, kk0, co1, kk1, ko, so, obuf, tmp, *scratch):
+def put_tiles(z, tmp, tiles, at):
+    for f in range(z.fields):
+        for n, tile in enumerate(tiles(f)):
+            for p in range(2):
+                tmp[f, p, aligned(at + SUB * n, SUB), :] = tile.astype(F32)[SUB * p : SUB * (p + 1)]
+
+
+def early_kernel(z, active, core, rows_f, co, mix, state, tmp, *scratch):
     half, chip = half_and_chip()
 
     @pl.when(chip == active)
     def _():
-        offset = z.halo * half
-
-        def put(ref, at):
-            for f in range(z.fields):
-                for g in range(ref.shape[1]):
-                    tile = ref[f, g].astype(F32)
-                    for p in range(2):
-                        tmp[f, p, aligned(at + SUB * g, SUB), :] = tile[SUB * p : SUB * (p + 1)]
-
-        put(core, 2 * z.halo * (1 - half))
-        put(near, z.halo + (z.core - z.halo) * half)
-        put(far, z.message * half)
-        band = Band(z, scratch + (co0, kk0))
-        band.load(tmp, 0, z.wide)
-        band.steps(rows_f, 0, 0, offset, z.wide)
-        band.store(tmp, z.wide)
+        band = Band(z, scratch + (co, mix))
+        span = z.core // SUB
+        put_tiles(z, tmp, lambda f: [core[f, g] for g in range(z.core // SUB)], 0)
+        band.load(tmp, 0, span)
+        band.steps(rows_f, 0, 0, z.halo * (2 - half), span)
+        band.store(state, span, z.base)
+
+
+def late_kernel(
+    z, active, core, near, far, state, rows_f, co_rim, mix_first, co_late, mix_last, ko_in, so_in, ko, so, obuf, tmp, *scratch
+):
+    half, chip = half_and_chip()
+
+    @pl.when(chip == active)
+    def _():
+        groups = z.halo // SUB
+        span = z.rim // SUB
+        put_tiles(z, tmp, lambda f: [far[f, g] for g in range(groups)], 2 * z.halo * half)
+        put_tiles(z, tmp, lambda f: [near[f, g] for g in range(groups)], z.halo)
+        first = (z.core // SUB - groups) * half
+        put_tiles(z, tmp, lambda f: [core[f, first + g] for g in range(groups)], 2 * z.halo * (1 - half))
+        band = Band(z, scratch + (co_rim, mix_first))
+        band.load(tmp, 0, span)
+        band.steps(rows_f, 0, 0, (z.window - z.rim) * half, span)
+        band.store(tmp, span, z.base)
+        outer, inner = 2 * z.halo, z.core - z.halo
+        start = z.inset + z.base
         for f in range(z.fields):
             for p in range(2):
-                obuf[1 - half, f, p] = tmp[f, p, z.halo : z.halo + z.own, :]
-        band = Band(z, scratch + (co1, kk1))
-        band.load(tmp, z.inset, z.narrow)
-        band.steps(rows_f, 1, 0, offset + z.inset, z.narrow)
+                rim = tmp[f, p, start : start + outer, :]
+                tmp[f, p, aligned(inner * half, outer), :] = rim
+                tmp[f, p, aligned(outer * (1 - half), inner), :] = state[f, p, start : start + inner, :]
+                obuf[1 - half, f, p] = tmp[f, p, z.inset : z.inset + z.own, :]
+        band = Band(z, scratch + (co_late, mix_last))
+        band.load(tmp, 0, z.narrow)
+        band.steps(rows_f, 1, 0, z.halo * half + z.inset, z.narrow)
         band.store(tmp, z.narrow)
         for f in range(z.fields):
             for p in range(2):
@@ -420,11 +447,13 @@
         state = pltpu.VMEM((span + 2, z.fields, 2, SUB, z.lanes), F32)
         return [state] * 4
 
-    def operators(span):
-        return [shape(dims, F32) for dims in ((span + 2, 8, 2, SUB, z.lanes), (z.fields**2, SUB, z.lanes))]
-
-    def operator_scratch(span):
-        return [pltpu.VMEM(spec.shape, spec.dtype) for spec in operators(span)]
+    def stencil(columns):
+        return shape((columns // SUB + 2, 8, 2, SUB, z.lanes), F32)
+
+    mixing = shape((z.fields**2, SUB, z.lanes), F32)
+
+    def operator_scratch(columns):
+        return [pltpu.VMEM(spec.shape, spec.dtype) for spec in (stencil(columns), mixing)]
 
     rows_f_shape = shape((2, z.steps, z.fields, 2, z.window, z.lanes), F32)
     rows_c_shape = shape((2, 5, 2, z.window, z.lanes), F32)
@@ -437,15 +466,15 @@
         out_shape=[rows_f_shape, rows_c_shape, shape((2, z.fields, 2, z.main, z.lanes), F32), tiles(z.core)],
         in_specs=in_vmem(4),
         out_specs=in_vmem(4),
-        scratch_shapes=band_scratch(z.wide) + operator_scratch(z.wide),
+        scratch_shapes=band_scratch(z.wide) + operator_scratch(z.main),
         compiler_params=params,
         cost_estimate=pl.CostEstimate(flops=10**9, bytes_accessed=2 * 10**7, transcendentals=0),
         name="inner",
     )(keep_f, got_f, keep_c, got_c)
-    down = [(device(t, s), device(t - 2, s)) for t, s in everyone if t >= 2]
+    down = [(device(t, s), device(t ^ 2, s)) for t, s in everyone]
     across = [(device(t, s), device((t ^ 1) - 2, s + 1 if t % 2 else s - 1)) for t, s in everyone if t >= 2]
     core = lax.ppermute(core, ("tm", "space"), down)
-    rows_f, rows_c, kept, sent, edge, *late_operators = pl.pallas_call(
+    rows_f, rows_c, kept, sent, edge, co_core, co_rim, co_late, mix_first, mix_last = pl.pallas_call(
         functools.partial(rim_kernel, z, 1),
         out_shape=[
             rows_f_shape,
@@ -453,38 +482,50 @@
             shape(half_dims, F32),
             shape(half_dims, F32),
             tiles(z.halo),
-        ]
-        + operators(z.wide)
-        + operators(z.narrow),
+            stencil(z.core),
+            stencil(z.rim),
+            stencil(z.main - z.halo),
+            mixing,
+            mixing,
+        ],
         in_specs=in_vmem(5),
-        out_specs=in_vmem(9),
+        out_specs=in_vmem(10),
         input_output_aliases={3: 0, 4: 1},
         scratch_shapes=[
             pltpu.VMEM((2,) + half_dims, F32),
-            pltpu.VMEM((z.fields, 2, 3 * z.halo, z.lanes), F32),
+            pltpu.VMEM((z.fields, 2, z.rim, z.lanes), F32),
         ]
         + band_scratch(z.wide)
-        + operator_scratch(3 * z.halo // SUB),
+        + operator_scratch(z.rim),
         compiler_params=params,
         cost_estimate=pl.CostEstimate(flops=10**9, bytes_accessed=2 * 10**7, transcendentals=0),
         name="rim",
     )(got_a, got_b, inner, rows_f, rows_c)
+    state = pl.pallas_call(
+        functools.partial(early_kernel, z, 0),
+        out_shape=shape((z.fields, 2, z.core + SUB, z.lanes), F32),
+        in_specs=in_vmem(4),
+        out_specs=pl.BlockSpec(memory_space=pltpu.VMEM),
+        scratch_shapes=[pltpu.VMEM((z.fields, 2, z.core, z.lanes), F32)] + band_scratch(z.core // SUB),
+        compiler_params=params,
+        name="early",
+    )(core, rows_f, co_core, mix_first)
     far = lax.ppermute(edge, ("tm", "space"), across)
-    near = lax.ppermute(edge, ("tm", "space"), down)
+    near = lax.ppermute(edge, ("tm", "space"), [(i, j) for i, j in down if i > j])
     kept, sent = pl.pallas_call(
         functools.partial(late_kernel, z, 0),
         out_shape=[shape(half_dims, F32), shape(half_dims, F32)],
-        in_specs=in_vmem(10),
+        in_specs=in_vmem(11),
         out_specs=in_vmem(2),
-        input_output_aliases={4: 0, 5: 1},
+        input_output_aliases={9: 0, 10: 1},
         scratch_shapes=[
             pltpu.VMEM((2,) + half_dims, F32),
             pltpu.VMEM((z.fields, 2, z.main, z.lanes), F32),
         ]
-        + band_scratch(z.wide),
+        + band_scratch(z.narrow),
         compiler_params=params,
         name="late",
-    )(core, near, far, rows_f, kept, sent, *late_operators)
+    )(core, near, far, state, rows_f, co_rim, mix_first, co_late, mix_last, kept, sent)
     got = lax.ppermute(sent, "tm", partner)
     return pl.pallas_call(
         functools.partial(finish_kernel, z),

time: 43.4 us -> 41.8 us (0.963)
  waiting for transfers between devices: 20.9 us -> 9.57 us
  starting transfers between devices: 10.3 us -> 19.2 us
  Pallas kernels: 11.9 us -> 12.9 us
    ppermute x1, starting transfers between devices: 1.29 us -> 10.1 us  [per_device(): core = lax.ppermute(core, ('tm', 'space'), down)]
    ppermute x1, waiting for transfers between devices: 10.8 us -> 5.59 us  [per_device(): far = lax.ppermute(edge, ('tm', 'space'), across)]
    ppermute x1, waiting for transfers between devices: 5 us -> 0.01 us  [per_device(): got_a = lax.ppermute(pay_a, ('tm', 'space'), perm_a)]
    ppermute x1, waiting for transfers between devices: 3.56 us -> 0.01 us  [per_device(): got_b = lax.ppermute(pay_b, ('tm', 'space'), perm_b)]
    pallas_call x0 -> x1, Pallas kernels: none -> 2.46 us  [per_device(): pl.pallas_call(functools.partial(early_kernel, z, 0), out_shape=shape((z....]
    ppermute x1, waiting for transfers between devices: 0.01 us -> 2.36 us  [per_device(): core = lax.ppermute(core, ('tm', 'space'), down)]
    pallas_call x1, Pallas kernels: 7.62 us -> 6.05 us  [per_device(): pl.pallas_call(functools.partial(late_kernel, z, 0), out_shape=[shape(hal...]
  transfers between devices with their start and end apart: 8 -> 8, of which waited for: 4 -> 3; matrix products, arithmetic and copies ran while one was open for 0% -> 0% of each run, Pallas kernels for 2% -> 8%
where the time goes in v3:
time: 41.8 us; the launch traced here: 41.7 us
  starting transfers between devices  19.2 us (46%)
  Pallas kernels  12.9 us (31%)
  waiting for transfers between devices  9.57 us (23%)
    ppermute x1, starting transfers between devices, per_device(): core = lax.ppermute(core, ('tm', 'space'), down)  10.1 us
    pallas_call x1, Pallas kernels, per_device(): pl.pallas_call(functools.partial(late_kernel, z, 0), out_shape=[shape(hal...  6.05 us
    ppermute x1, starting transfers between devices, per_device(): got_a = lax.ppermute(pay_a, ('tm', 'space'), perm_a)  5.67 us
    ppermute x1, waiting for transfers between devices, per_device(): far = lax.ppermute(edge, ('tm', 'space'), across)  5.59 us
    pallas_call x1, Pallas kernels, per_device(): pl.pallas_call(functools.partial(early_kernel, z, 0), out_shape=shape((z....  2.46 us
    ppermute x1, waiting for transfers between devices, per_device(): core = lax.ppermute(core, ('tm', 'space'), down)  2.36 us
    pallas_call x1, Pallas kernels, per_device(): pl.pallas_call(functools.partial(prepare_kernel, z), out_shape=[shape(f_s...  2.25 us
    ppermute x1, waiting for transfers between devices, per_device(): got = lax.ppermute(sent, 'tm', partner)  1.61 us
  transfers between devices with their start and end apart: 8, of which 3 were waited for; matrix products, arithmetic and copies ran while one was open for 0% of the time, Pallas kernels for 8%

profile of v3, /device:TPU:0, one launch (start us, length us, event | category | flops | bytes accessed | tf_op | source)
XLA Modules:
  0.0 41.7 jit_solution(17342217133986956248)
XLA Ops:
  0.0 2.2 %prepare.1 = (bf16[4,6,2,112,128]{4,3,2,1,0:T(8,128)(2,1)S(1)}, bf16[4,6,2,112,128]{4,3,2,1,0:T(8,128)(2,1)S(1)}, f32[5,2,112,128]{3,2,1,0:T(8,128)S(1)}, f32[5,...) custom-call(bf16[1,4,6,256,128]{4,3,2,1,0:T(8,128)(2,1)} %fo_in.1, ...), custom_call_target="tpu_custom_call" | custom-call | tf_op jit(solution)/shard_map/prepare/pallas_call | solution.py:399
  2.3 0.5 %collective-permute-start = (bf16[4,6,2,112,128]{4,3,2,1,0:T(8,128)(2,1)S(1)}, bf16[4,6,2,112,128]{4,3,2,1,0:T(8,128)(2,1)S(1)}, u32[]{:S(2)}, u32[]{:S(2)}) collective-permute-start(bf16[4,6,2,112,128]{4,3,2,1,0:T(8,128)(2,1)S(1)} %get-tuple-element.27), channel_id=1, source_target_pairs={{0,8},{8,0},{16,24},{24,16},{1,9},{9,1},{17,25},{25,17},{2,10},{10... | collective-permute-start | bytes 4128776 | tf_op jit(solution)/shard_map/ppermute | solution.py:441
  2.8 0.1 collective-permute-start.1
  2.9 5.7 %collective-permute-start.3 = (bf16[72,16,128]{2,1,0:T(8,128)(2,1)S(1)}, bf16[72,16,128]{2,1,0:T(8,128)(2,1)S(1)}, u32[]{:S(2)}, u32[]{:S(2)}) collective-permute-start(bf16[72,16,128]{2,1,0:T(8,128)(2,1)S(1)} %get-tuple-element.31), channel_id=1, source_target_pairs={{0,15},{1,8},{2,9},{3,10},{4,11},{5,12},{6,13},{7,14},{8,1},{9,2},... | collective-permute-start | bytes 884744 | tf_op jit(solution)/shard_map/ppermute | solution.py:443
  8.5 0.0 collective-permute-start.4
  8.5 0.0 collective-permute-done.1.rc
  8.5 0.0 collective-permute-done.rf
  8.5 0.5 %inner.1 = (f32[2,4,6,2,136,128]{5,4,3,2,1,0:T(8,128)S(1)}, f32[2,5,2,136,128]{4,3,2,1,0:T(8,128)S(1)}, f32[2,6,2,112,128]{4,3,2,1,0:T(8,128)S(1)}, bf16[6,8,16,128]{3,2,1,0:T(8,128)(2,1)S(1)}) custom-call(bf16[4,6,2,112,128]{4,3,2,1,0:T(8,128)(2,1)S(1)} %get-tuple-element.26.kf, bf16[4,6,2,112,128]{4,3,2,1,0:T(8,128)(2,1)S(1)} %collective-permute-done.rf, ...), custom_call_target="tpu_custom_call" | custom-call | flops 1000000000 | bytes 20000000 | tf_op jit(solution)/shard_map/inner/pallas_call | solution.py:464
  9.1 10.1 %collective-permute-start.2 = (bf16[6,8,16,128]{3,2,1,0:T(8,128)(2,1)S(1)}, bf16[6,8,16,128]{3,2,1,0:T(8,128)(2,1)S(1)}, u32[]{:S(2)}, u32[]{:S(2)}) collective-permute-start(bf16[6,8,16,128]{3,2,1,0:T(8,128)(2,1)S(1)} %get-tuple-element.30), channel_id=1, source_target_pairs={{0,16},{1,17},{2,18},{3,19},{4,20},{5,21},{6,22},{7,23},{8,24},{9,... | collective-permute-start | bytes 589832 | tf_op jit(solution)/shard_map/ppermute | solution.py:476
  19.2 0.0 collective-permute-done.3.ra
  19.2 0.0 collective-permute-done.4.rb
  19.2 0.4 rim.1
  19.6 1.3 %collective-permute-start.6 = (bf16[6,3,16,128]{3,2,1,0:T(8,128)(2,1)S(1)}, bf16[6,3,16,128]{3,2,1,0:T(8,128)(2,1)S(1)}, u32[]{:S(2)}, u32[]{:S(2)}) collective-permute-start(bf16[6,3,16,128]{3,2,1,0:T(8,128)(2,1)S(1)} %get-tuple-element.36), channel_id=1, source_target_pairs={{16,15},{17,8},{18,9},{19,10},{20,11},{21,12},{22,13},{23,14},{24,... | collective-permute-start | bytes 221192 | tf_op jit(solution)/shard_map/ppermute | solution.py:513
  20.9 1.3 %collective-permute-start.5 = (bf16[6,3,16,128]{3,2,1,0:T(8,128)(2,1)S(1)}, bf16[6,3,16,128]{3,2,1,0:T(8,128)(2,1)S(1)}, u32[]{:S(2)}, u32[]{:S(2)}) collective-permute-start(bf16[6,3,16,128]{3,2,1,0:T(8,128)(2,1)S(1)} %get-tuple-element.36), channel_id=1, source_target_pairs={{16,0},{17,1},{18,2},{19,3},{20,4},{21,5},{22,6},{23,7},{24,8},{25... | collective-permute-start | bytes 221192 | tf_op jit(solution)/shard_map/ppermute | solution.py:514
  22.2 2.4 %collective-permute-done.2.core = bf16[6,8,16,128]{3,2,1,0:T(8,128)(2,1)S(1)} collective-permute-done((bf16[6,8,16,128]{3,2,1,0:T(8,128)(2,1)S(1)}, bf16[6,8,16,128]{3,2,1,0:T(8,128)(2,1)S(1)}, u32[]{:S(2)}, u32[]{:S(2)}) %collective-permute-start.2) | collective-permute-done | bytes 196640 | tf_op jit(solution)/shard_map/ppermute | solution.py:476
  24.6 2.5 %early.1.state = f32[6,2,72,128]{3,2,1,0:T(8,128)S(1)} custom-call(bf16[6,8,16,128]{3,2,1,0:T(8,128)(2,1)S(1)} %collective-permute-done.2.core, f32[2,4,6,2,136,128]{5,4,3,2,1,0:T(8,128)S(1)} %get-tuple-element.37.rows_f, f32[10,8,2,8,128]{4,3,2,1,0:T(8,128)S(1)} %get-tuple-element.38.co, f32[36,8,128]{2,1,0:T(8,128)S(1)} %get-tuple-element.39.mix.mix_first), custom_call_target="tpu_custom_call" | custom-call | tf_op jit(solution)/shard_map/early/pallas_call | solution.py:504
  27.1 5.6 %collective-permute-done.6.far = bf16[6,3,16,128]{3,2,1,0:T(8,128)(2,1)S(1)} collective-permute-done((bf16[6,3,16,128]{3,2,1,0:T(8,128)(2,1)S(1)}, bf16[6,3,16,128]{3,2,1,0:T(8,128)(2,1)S(1)}, u32[]{:S(2)}, u32[]{:S(2)}) %collective-permute-start.6) | collective-permute-done | bytes 73760 | tf_op jit(solution)/shard_map/ppermute | solution.py:513
  32.7 0.0 collective-permute-done.5.near
  32.7 6.1 %late.1 = (f32[6,2,64,128]{3,2,1,0:T(8,128)S(1)}, f32[6,2,64,128]{3,2,1,0:T(8,128)S(1)}) custom-call(bf16[6,8,16,128]{3,2,1,0:T(8,128)(2,1)S(1)} %collective-permute-done.2.core, bf16[6,3,16,128]{3,2,1,0:T(8,128)(2,1)S(1)} %collective-permute-done.5.near, ...), custom_call_target="tpu_custom_call", output_to_operand_aliasing={{0}: (9, {}), {1}: (10, {})} | custom-call | tf_op jit(solution)/shard_map/late/pallas_call | solution.py:515
  38.7 0.2 collective-permute-start.7
  38.9 1.6 %collective-permute-done.7.got = f32[6,2,64,128]{3,2,1,0:T(8,128)S(1)} collective-permute-done((f32[6,2,64,128]{3,2,1,0:T(8,128)S(1)}, f32[6,2,64,128]{3,2,1,0:T(8,128)S(1)}, u32[]{:S(2)}, u32[]{:S(2)}) %collective-permute-start.7) | collective-permute-done | bytes 393248 | tf_op jit(solution)/shard_map/ppermute | solution.py:529
  40.5 1.2 %finish.1 = f32[1,6,256,128]{3,2,1,0:T(8,128)} custom-call(f32[6,2,64,128]{3,2,1,0:T(8,128)S(1)} %get-tuple-element.45.keep, f32[6,2,64,128]{3,2,1,0:T(8,128)S(1)} %collective-permute-done.7.got), custom_call_target="tpu_custom_call" | custom-call | tf_op jit(solution)/shard_map/finish/pallas_call | solution.py:530
Async XLA Ops:
  2.3 6.3 %collective-permute-start = (bf16[4,6,2,112,128]{4,3,2,1,0:T(8,128)(2,1)S(1)}, bf16[4,6,2,112,128]{4,3,2,1,0:T(8,128)(2,1)S(1)}, u32[]{:S(2)}, u32[]{:S(2)}) collective-permute-start(bf16[4,6,2,112,128]{4,3,2,1,0:T(8,128)(2,1)S(1)} %get-tuple-element.27), channel_id=1, source_target_pairs={{0,8},{8,0},{16,24},{24,16},{1,9},{9,1},{17,25},{25,17},{2,10},{10... | collective-permute-start | bytes 4128776 | tf_op jit(solution)/shard_map/ppermute | solution.py:441
  2.8 5.8 %collective-permute-start.1 = (f32[5,2,112,128]{3,2,1,0:T(8,128)S(1)}, f32[5,2,112,128]{3,2,1,0:T(8,128)S(1)}, u32[]{:S(2)}, u32[]{:S(2)}) collective-permute-start(f32[5,2,112,128]{3,2,1,0:T(8,128)S(1)} %get-tuple-element.29), channel_id=1, source_target_pairs={{0,8},{8,0},{16,24},{24,16},{1,9},{9,1},{17,25},{25,17},{2,10},{10... | collective-permute-start | bytes 1720328 | tf_op jit(solution)/shard_map/ppermute | solution.py:442
  2.9 16.4 %collective-permute-start.3 = (bf16[72,16,128]{2,1,0:T(8,128)(2,1)S(1)}, bf16[72,16,128]{2,1,0:T(8,128)(2,1)S(1)}, u32[]{:S(2)}, u32[]{:S(2)}) collective-permute-start(bf16[72,16,128]{2,1,0:T(8,128)(2,1)S(1)} %get-tuple-element.31), channel_id=1, source_target_pairs={{0,15},{1,8},{2,9},{3,10},{4,11},{5,12},{6,13},{7,14},{8,1},{9,2},... | collective-permute-start | bytes 884744 | tf_op jit(solution)/shard_map/ppermute | solution.py:443
  8.5 10.7 %collective-permute-start.4 = (bf16[72,16,128]{2,1,0:T(8,128)(2,1)S(1)}, bf16[72,16,128]{2,1,0:T(8,128)(2,1)S(1)}, u32[]{:S(2)}, u32[]{:S(2)}) collective-permute-start(bf16[72,16,128]{2,1,0:T(8,128)(2,1)S(1)} %get-tuple-element.32), channel_id=1, source_target_pairs={{0,1},{1,2},{2,3},{3,4},{4,5},{5,6},{6,7},{7,0},{8,15},{9,8},{10,9... | collective-permute-start | bytes 884744 | tf_op jit(solution)/shard_map/ppermute | solution.py:444
  9.1 15.5 %collective-permute-start.2 = (bf16[6,8,16,128]{3,2,1,0:T(8,128)(2,1)S(1)}, bf16[6,8,16,128]{3,2,1,0:T(8,128)(2,1)S(1)}, u32[]{:S(2)}, u32[]{:S(2)}) collective-permute-start(bf16[6,8,16,128]{3,2,1,0:T(8,128)(2,1)S(1)} %get-tuple-element.30), channel_id=1, source_target_pairs={{0,16},{1,17},{2,18},{3,19},{4,20},{5,21},{6,22},{7,23},{8,24},{9,... | collective-permute-start | bytes 589832 | tf_op jit(solution)/shard_map/ppermute | solution.py:476
  19.6 13.0 %collective-permute-start.6 = (bf16[6,3,16,128]{3,2,1,0:T(8,128)(2,1)S(1)}, bf16[6,3,16,128]{3,2,1,0:T(8,128)(2,1)S(1)}, u32[]{:S(2)}, u32[]{:S(2)}) collective-permute-start(bf16[6,3,16,128]{3,2,1,0:T(8,128)(2,1)S(1)} %get-tuple-element.36), channel_id=1, source_target_pairs={{16,15},{17,8},{18,9},{19,10},{20,11},{21,12},{22,13},{23,14},{24,... | collective-permute-start | bytes 221192 | tf_op jit(solution)/shard_map/ppermute | solution.py:513
  20.9 11.7 %collective-permute-start.5 = (bf16[6,3,16,128]{3,2,1,0:T(8,128)(2,1)S(1)}, bf16[6,3,16,128]{3,2,1,0:T(8,128)(2,1)S(1)}, u32[]{:S(2)}, u32[]{:S(2)}) collective-permute-start(bf16[6,3,16,128]{3,2,1,0:T(8,128)(2,1)S(1)} %get-tuple-element.36), channel_id=1, source_target_pairs={{16,0},{17,1},{18,2},{19,3},{20,4},{21,5},{22,6},{23,7},{24,8},{25... | collective-permute-start | bytes 221192 | tf_op jit(solution)/shard_map/ppermute | solution.py:514
  38.7 1.8 %collective-permute-start.7 = (f32[6,2,64,128]{3,2,1,0:T(8,128)S(1)}, f32[6,2,64,128]{3,2,1,0:T(8,128)S(1)}, u32[]{:S(2)}, u32[]{:S(2)}) collective-permute-start(f32[6,2,64,128]{3,2,1,0:T(8,128)S(1)} %get-tuple-element.46), channel_id=1, source_target_pairs={{0,8},{8,0},{16,24},{24,16},{1,9},{9,1},{17,25},{25,17},{2,10},{10... | collective-permute-start | bytes 1179656 | tf_op jit(solution)/shard_map/ppermute | solution.py:529

commit v4 on v3

--- a/solution.py
+++ b/solution.py
@@ -472,7 +472,7 @@
         name="inner",
     )(keep_f, got_f, keep_c, got_c)
     down = [(device(t, s), device(t ^ 2, s)) for t, s in everyone]
-    across = [(device(t, s), device((t ^ 1) - 2, s + 1 if t % 2 else s - 1)) for t, s in everyone if t >= 2]
+    across = [(device(t, s), device((t ^ 1) - 2, s + 1 if t % 2 else s - 1) if t >= 2 else device(t + 2, s)) for t, s in everyone]
     core = lax.ppermute(core, ("tm", "space"), down)
     rows_f, rows_c, kept, sent, edge, co_core, co_rim, co_late, mix_first, mix_last = pl.pallas_call(
         functools.partial(rim_kernel, z, 1),
@@ -511,7 +511,7 @@
         name="early",
     )(core, rows_f, co_core, mix_first)
     far = lax.ppermute(edge, ("tm", "space"), across)
-    near = lax.ppermute(edge, ("tm", "space"), [(i, j) for i, j in down if i > j])
+    near = lax.ppermute(edge, ("tm", "space"), down)
     kept, sent = pl.pallas_call(
         functools.partial(late_kernel, z, 0),
         out_shape=[shape(half_dims, F32), shape(half_dims, F32)],

time: 41.8 us -> 40.6 us (0.971)
  waiting for transfers between devices: 9.57 us -> 4.21 us
  starting transfers between devices: 19.2 us -> 23.3 us
    ppermute x1, starting transfers between devices: 1.29 us -> 6.75 us  [per_device(): far = lax.ppermute(edge, ('tm', 'space'), across)]
    ppermute x1, waiting for transfers between devices: 5.59 us -> 2.48 us  [per_device(): far = lax.ppermute(edge, ('tm', 'space'), across)]
    ppermute x1, waiting for transfers between devices: 2.36 us -> 0.01 us  [per_device(): core = lax.ppermute(core, ('tm', 'space'), down)]
    ppermute x1, starting transfers between devices: 1.29 us -> 0.08 us  [per_device(): near = lax.ppermute(edge, ('tm', 'space'), down)]
  transfers between devices with their start and end apart: 8 -> 8, of which waited for: 3 -> 2; matrix products, arithmetic and copies ran while one was open for 0% -> 0% of each run, Pallas kernels for 8% -> 8%
where the time goes in v4:
time: 40.6 us; the launch traced here: 40.4 us
  starting transfers between devices  23.3 us (57%)
  Pallas kernels  12.9 us (32%)
  waiting for transfers between devices  4.21 us (10%)
    ppermute x1, starting transfers between devices, per_device(): core = lax.ppermute(core, ('tm', 'space'), down)  10.1 us
    ppermute x1, starting transfers between devices, per_device(): far = lax.ppermute(edge, ('tm', 'space'), across)  6.75 us
    pallas_call x1, Pallas kernels, per_device(): pl.pallas_call(functools.partial(late_kernel, z, 0), out_shape=[shape(hal...  6.05 us
    ppermute x1, starting transfers between devices, per_device(): got_a = lax.ppermute(pay_a, ('tm', 'space'), perm_a)  5.67 us
    ppermute x1, waiting for transfers between devices, per_device(): far = lax.ppermute(edge, ('tm', 'space'), across)  2.48 us
    pallas_call x1, Pallas kernels, per_device(): pl.pallas_call(functools.partial(early_kernel, z, 0), out_shape=shape((z....  2.47 us
    pallas_call x1, Pallas kernels, per_device(): pl.pallas_call(functools.partial(prepare_kernel, z), out_shape=[shape(f_s...  2.25 us
    ppermute x1, waiting for transfers between devices, per_device(): got = lax.ppermute(sent, 'tm', partner)  1.7 us
  transfers between devices with their start and end apart: 8, of which 2 were waited for; matrix products, arithmetic and copies ran while one was open for 0% of the time, Pallas kernels for 8%

profile of v4, /device:TPU:0, one launch (start us, length us, event | category | flops | bytes accessed | tf_op | source)
XLA Modules:
  0.0 40.4 jit_solution(11590019625329800626)
XLA Ops:
  0.0 2.2 %prepare.1 = (bf16[4,6,2,112,128]{4,3,2,1,0:T(8,128)(2,1)S(1)}, bf16[4,6,2,112,128]{4,3,2,1,0:T(8,128)(2,1)S(1)}, f32[5,2,112,128]{3,2,1,0:T(8,128)S(1)}, f32[5,...) custom-call(bf16[1,4,6,256,128]{4,3,2,1,0:T(8,128)(2,1)} %fo_in.1, ...), custom_call_target="tpu_custom_call" | custom-call | tf_op jit(solution)/shard_map/prepare/pallas_call | solution.py:399
  2.3 0.5 %collective-permute-start = (bf16[4,6,2,112,128]{4,3,2,1,0:T(8,128)(2,1)S(1)}, bf16[4,6,2,112,128]{4,3,2,1,0:T(8,128)(2,1)S(1)}, u32[]{:S(2)}, u32[]{:S(2)}) collective-permute-start(bf16[4,6,2,112,128]{4,3,2,1,0:T(8,128)(2,1)S(1)} %get-tuple-element.27), channel_id=1, source_target_pairs={{0,8},{8,0},{16,24},{24,16},{1,9},{9,1},{17,25},{25,17},{2,10},{10... | collective-permute-start | bytes 4128776 | tf_op jit(solution)/shard_map/ppermute | solution.py:441
  2.8 0.1 collective-permute-start.1
  2.9 5.7 %collective-permute-start.3 = (bf16[72,16,128]{2,1,0:T(8,128)(2,1)S(1)}, bf16[72,16,128]{2,1,0:T(8,128)(2,1)S(1)}, u32[]{:S(2)}, u32[]{:S(2)}) collective-permute-start(bf16[72,16,128]{2,1,0:T(8,128)(2,1)S(1)} %get-tuple-element.31), channel_id=1, source_target_pairs={{0,15},{1,8},{2,9},{3,10},{4,11},{5,12},{6,13},{7,14},{8,1},{9,2},... | collective-permute-start | bytes 884744 | tf_op jit(solution)/shard_map/ppermute | solution.py:443
  8.5 0.0 collective-permute-start.4
  8.5 0.0 collective-permute-done.1.rc
  8.5 0.0 collective-permute-done.rf
  8.5 0.5 %inner.1 = (f32[2,4,6,2,136,128]{5,4,3,2,1,0:T(8,128)S(1)}, f32[2,5,2,136,128]{4,3,2,1,0:T(8,128)S(1)}, f32[2,6,2,112,128]{4,3,2,1,0:T(8,128)S(1)}, bf16[6,8,16,128]{3,2,1,0:T(8,128)(2,1)S(1)}) custom-call(bf16[4,6,2,112,128]{4,3,2,1,0:T(8,128)(2,1)S(1)} %get-tuple-element.26.kf, bf16[4,6,2,112,128]{4,3,2,1,0:T(8,128)(2,1)S(1)} %collective-permute-done.rf, ...), custom_call_target="tpu_custom_call" | custom-call | flops 1000000000 | bytes 20000000 | tf_op jit(solution)/shard_map/inner/pallas_call | solution.py:464
  9.1 10.1 %collective-permute-start.2 = (bf16[6,8,16,128]{3,2,1,0:T(8,128)(2,1)S(1)}, bf16[6,8,16,128]{3,2,1,0:T(8,128)(2,1)S(1)}, u32[]{:S(2)}, u32[]{:S(2)}) collective-permute-start(bf16[6,8,16,128]{3,2,1,0:T(8,128)(2,1)S(1)} %get-tuple-element.30), channel_id=1, source_target_pairs={{0,16},{1,17},{2,18},{3,19},{4,20},{5,21},{6,22},{7,23},{8,24},{9,... | collective-permute-start | bytes 589832 | tf_op jit(solution)/shard_map/ppermute | solution.py:476
  19.2 0.0 collective-permute-done.3.ra
  19.2 0.0 collective-permute-done.4.rb
  19.2 0.4 rim.1
  19.6 6.7 %collective-permute-start.6 = (bf16[6,3,16,128]{3,2,1,0:T(8,128)(2,1)S(1)}, bf16[6,3,16,128]{3,2,1,0:T(8,128)(2,1)S(1)}, u32[]{:S(2)}, u32[]{:S(2)}) collective-permute-start(bf16[6,3,16,128]{3,2,1,0:T(8,128)(2,1)S(1)} %get-tuple-element.36), channel_id=1, source_target_pairs={{0,16},{1,17},{2,18},{3,19},{4,20},{5,21},{6,22},{7,23},{8,24},{9,... | collective-permute-start | bytes 221192 | tf_op jit(solution)/shard_map/ppermute | solution.py:513
  26.4 0.1 collective-permute-start.5
  26.5 0.0 collective-permute-done.2.core
  26.5 2.5 %early.1.state = f32[6,2,72,128]{3,2,1,0:T(8,128)S(1)} custom-call(bf16[6,8,16,128]{3,2,1,0:T(8,128)(2,1)S(1)} %collective-permute-done.2.core, f32[2,4,6,2,136,128]{5,4,3,2,1,0:T(8,128)S(1)} %get-tuple-element.37.rows_f, f32[10,8,2,8,128]{4,3,2,1,0:T(8,128)S(1)} %get-tuple-element.38.co, f32[36,8,128]{2,1,0:T(8,128)S(1)} %get-tuple-element.39.mix.mix_first), custom_call_target="tpu_custom_call" | custom-call | tf_op jit(solution)/shard_map/early/pallas_call | solution.py:504
  28.9 2.5 %collective-permute-done.6.far = bf16[6,3,16,128]{3,2,1,0:T(8,128)(2,1)S(1)} collective-permute-done((bf16[6,3,16,128]{3,2,1,0:T(8,128)(2,1)S(1)}, bf16[6,3,16,128]{3,2,1,0:T(8,128)(2,1)S(1)}, u32[]{:S(2)}, u32[]{:S(2)}) %collective-permute-start.6) | collective-permute-done | bytes 73760 | tf_op jit(solution)/shard_map/ppermute | solution.py:513
  31.4 0.0 collective-permute-done.5.near
  31.4 6.1 %late.1 = (f32[6,2,64,128]{3,2,1,0:T(8,128)S(1)}, f32[6,2,64,128]{3,2,1,0:T(8,128)S(1)}) custom-call(bf16[6,8,16,128]{3,2,1,0:T(8,128)(2,1)S(1)} %collective-permute-done.2.core, bf16[6,3,16,128]{3,2,1,0:T(8,128)(2,1)S(1)} %collective-permute-done.5.near, ...), custom_call_target="tpu_custom_call", output_to_operand_aliasing={{0}: (9, {}), {1}: (10, {})} | custom-call | tf_op jit(solution)/shard_map/late/pallas_call | solution.py:515
  37.5 0.1 collective-permute-start.7
  37.6 1.7 %collective-permute-done.7.got = f32[6,2,64,128]{3,2,1,0:T(8,128)S(1)} collective-permute-done((f32[6,2,64,128]{3,2,1,0:T(8,128)S(1)}, f32[6,2,64,128]{3,2,1,0:T(8,128)S(1)}, u32[]{:S(2)}, u32[]{:S(2)}) %collective-permute-start.7) | collective-permute-done | bytes 393248 | tf_op jit(solution)/shard_map/ppermute | solution.py:529
  39.3 1.2 %finish.1 = f32[1,6,256,128]{3,2,1,0:T(8,128)} custom-call(f32[6,2,64,128]{3,2,1,0:T(8,128)S(1)} %get-tuple-element.45.keep, f32[6,2,64,128]{3,2,1,0:T(8,128)S(1)} %collective-permute-done.7.got), custom_call_target="tpu_custom_call" | custom-call | tf_op jit(solution)/shard_map/finish/pallas_call | solution.py:530
Async XLA Ops:
  2.3 6.3 %collective-permute-start = (bf16[4,6,2,112,128]{4,3,2,1,0:T(8,128)(2,1)S(1)}, bf16[4,6,2,112,128]{4,3,2,1,0:T(8,128)(2,1)S(1)}, u32[]{:S(2)}, u32[]{:S(2)}) collective-permute-start(bf16[4,6,2,112,128]{4,3,2,1,0:T(8,128)(2,1)S(1)} %get-tuple-element.27), channel_id=1, source_target_pairs={{0,8},{8,0},{16,24},{24,16},{1,9},{9,1},{17,25},{25,17},{2,10},{10... | collective-permute-start | bytes 4128776 | tf_op jit(solution)/shard_map/ppermute | solution.py:441
  2.8 5.8 %collective-permute-start.1 = (f32[5,2,112,128]{3,2,1,0:T(8,128)S(1)}, f32[5,2,112,128]{3,2,1,0:T(8,128)S(1)}, u32[]{:S(2)}, u32[]{:S(2)}) collective-permute-start(f32[5,2,112,128]{3,2,1,0:T(8,128)S(1)} %get-tuple-element.29), channel_id=1, source_target_pairs={{0,8},{8,0},{16,24},{24,16},{1,9},{9,1},{17,25},{25,17},{2,10},{10... | collective-permute-start | bytes 1720328 | tf_op jit(solution)/shard_map/ppermute | solution.py:442
  2.9 16.4 %collective-permute-start.3 = (bf16[72,16,128]{2,1,0:T(8,128)(2,1)S(1)}, bf16[72,16,128]{2,1,0:T(8,128)(2,1)S(1)}, u32[]{:S(2)}, u32[]{:S(2)}) collective-permute-start(bf16[72,16,128]{2,1,0:T(8,128)(2,1)S(1)} %get-tuple-element.31), channel_id=1, source_target_pairs={{0,15},{1,8},{2,9},{3,10},{4,11},{5,12},{6,13},{7,14},{8,1},{9,2},... | collective-permute-start | bytes 884744 | tf_op jit(solution)/shard_map/ppermute | solution.py:443
  8.5 10.7 %collective-permute-start.4 = (bf16[72,16,128]{2,1,0:T(8,128)(2,1)S(1)}, bf16[72,16,128]{2,1,0:T(8,128)(2,1)S(1)}, u32[]{:S(2)}, u32[]{:S(2)}) collective-permute-start(bf16[72,16,128]{2,1,0:T(8,128)(2,1)S(1)} %get-tuple-element.32), channel_id=1, source_target_pairs={{0,1},{1,2},{2,3},{3,4},{4,5},{5,6},{6,7},{7,0},{8,15},{9,8},{10,9... | collective-permute-start | bytes 884744 | tf_op jit(solution)/shard_map/ppermute | solution.py:444
  9.1 17.4 %collective-permute-start.2 = (bf16[6,8,16,128]{3,2,1,0:T(8,128)(2,1)S(1)}, bf16[6,8,16,128]{3,2,1,0:T(8,128)(2,1)S(1)}, u32[]{:S(2)}, u32[]{:S(2)}) collective-permute-start(bf16[6,8,16,128]{3,2,1,0:T(8,128)(2,1)S(1)} %get-tuple-element.30), channel_id=1, source_target_pairs={{0,16},{1,17},{2,18},{3,19},{4,20},{5,21},{6,22},{7,23},{8,24},{9,... | collective-permute-start | bytes 589832 | tf_op jit(solution)/shard_map/ppermute | solution.py:476
  19.6 11.8 %collective-permute-start.6 = (bf16[6,3,16,128]{3,2,1,0:T(8,128)(2,1)S(1)}, bf16[6,3,16,128]{3,2,1,0:T(8,128)(2,1)S(1)}, u32[]{:S(2)}, u32[]{:S(2)}) collective-permute-start(bf16[6,3,16,128]{3,2,1,0:T(8,128)(2,1)S(1)} %get-tuple-element.36), channel_id=1, source_target_pairs={{0,16},{1,17},{2,18},{3,19},{4,20},{5,21},{6,22},{7,23},{8,24},{9,... | collective-permute-start | bytes 221192 | tf_op jit(solution)/shard_map/ppermute | solution.py:513
  26.4 5.1 %collective-permute-start.5 = (bf16[6,3,16,128]{3,2,1,0:T(8,128)(2,1)S(1)}, bf16[6,3,16,128]{3,2,1,0:T(8,128)(2,1)S(1)}, u32[]{:S(2)}, u32[]{:S(2)}) collective-permute-start(bf16[6,3,16,128]{3,2,1,0:T(8,128)(2,1)S(1)} %get-tuple-element.36), channel_id=1, source_target_pairs={{0,16},{1,17},{2,18},{3,19},{4,20},{5,21},{6,22},{7,23},{8,24},{9,... | collective-permute-start | bytes 221192 | tf_op jit(solution)/shard_map/ppermute | solution.py:514
  37.5 1.8 %collective-permute-start.7 = (f32[6,2,64,128]{3,2,1,0:T(8,128)S(1)}, f32[6,2,64,128]{3,2,1,0:T(8,128)S(1)}, u32[]{:S(2)}, u32[]{:S(2)}) collective-permute-start(f32[6,2,64,128]{3,2,1,0:T(8,128)S(1)} %get-tuple-element.46), channel_id=1, source_target_pairs={{0,8},{8,0},{16,24},{24,16},{1,9},{9,1},{17,25},{25,17},{2,10},{10... | collective-permute-start | bytes 1179656 | tf_op jit(solution)/shard_map/ppermute | solution.py:529

commit v5 on v4

--- a/solution.py
+++ b/solution.py
@@ -26,16 +26,18 @@
         self.span = self.window // SUB
         self.shift = self.strip - self.main
         self.own = self.strip // 2
-        self.groups = [-(-REACH * (self.steps + k) // SUB) for k in range(self.steps)]
-        self.group_start = [self.fields * sum(self.groups[:k]) for k in range(self.steps)]
-        self.coef_start = self.fields * sum(self.groups)
-        self.coef_groups = self.halo // SUB
-        self.payload = self.coef_start + 4 * self.coef_groups
+        self.depths = [REACH * (self.steps + k) for k in range(self.steps)]
+        self.depth = self.depths[-1]
+        self.starts = [self.fields * sum(self.depths[:k]) for k in range(self.steps)]
+        self.coef_start = self.fields * sum(self.depths)
+        self.payload = -(-(self.coef_start + 4 * self.depth) // SUB)
         self.message = self.own + self.halo
         self.core = self.message - self.halo
         self.wide, self.narrow = self.main // SUB, (self.main - self.halo) // SUB
         self.inset = self.halo // 2
-        self.rim = 3 * self.halo
+        self.outer = 3 * self.halo
+        self.rim = -(-3 * self.depth // SUB) * SUB
+        self.rim_own = self.rim - 2 * self.depth
         self.base = -self.inset % SUB
 
 
@@ -44,7 +46,7 @@
     return lax.rem(tm, 2), tm // 2
 
 
-def prepare_kernel(z, fo_in, zc, mc, zf, mf, cp_in, keep_f, send_f, keep_c, send_c, pay_a, pay_b, fo, co, cp, buf, sems):
+def prepare_kernel(z, fo_in, zc, mc, zf, mf, cp_in, keep_f, send_f, keep_c, send_c, pay_a, pay_b, fo, co, cp, buf, edges, sems):
     half, _ = half_and_chip()
     left = half == 0
     row = lax.broadcasted_iota(jnp.int32, (z.rows, z.strip), 0)
@@ -60,17 +62,13 @@
         buf[slot] = values
         return [buf[slot, pl.ds(p, z.lanes, stride=2), :].T for p in range(2)]
 
-    def split(both, groups, start, keep, send):
+    def split(both, depth, start, keep, send):
         for p in range(2):
             low, high = both[p][: z.main], both[p][z.shift :]
             keep[p] = jnp.where(left, low, high).astype(keep.dtype)
             send[p] = jnp.where(left, high, low).astype(send.dtype)
-        for g in range(groups):
-            lo, hi = SUB * g, z.strip - SUB * (groups - g)
-            west = jnp.concatenate([both[p][lo : lo + SUB] for p in range(2)], axis=0)
-            east = jnp.concatenate([both[p][hi : hi + SUB] for p in range(2)], axis=0)
-            pay_a[start + g] = jnp.where(left, west, east).astype(BF16)
-            pay_b[start + g] = jnp.where(left, east, west).astype(BF16)
+            edges[0, p, start : start + depth, :] = both[p][:depth]
+            edges[1, p, start : start + depth, :] = both[p][z.strip - depth :]
 
     slots = buf.shape[0]
     count = 0
@@ -80,7 +78,7 @@
         if c == 1:
             values = jnp.where(row < z.rows - 1, values, jnp.zeros_like(values))
         both = columns(values, count % slots)
-        split(both, z.coef_groups, z.coef_start + c * z.coef_groups, keep_c.at[c], send_c.at[c])
+        split(both, z.depth, z.coef_start + c * z.depth, keep_c.at[c], send_c.at[c])
         count += 1
     mixing_copy.wait()
     for ref in (keep_c, send_c):
@@ -90,8 +88,13 @@
         forcing_copies[k].wait()
         for f in range(z.fields):
             both = columns(fo[k, f].astype(F32), count % slots)
-            split(both, z.groups[k], z.group_start[k] + f * z.groups[k], keep_f.at[k, f], send_f.at[k, f])
+            split(both, z.depths[k], z.starts[k] + f * z.depths[k], keep_f.at[k, f], send_f.at[k, f])
             count += 1
+    for g in range(z.payload):
+        at = slice(SUB * g, SUB * (g + 1))
+        west, east = (jnp.concatenate([edges[n, p, at, :] for p in range(2)], axis=0) for n in range(2))
+        pay_a[g] = jnp.where(left, west, east).astype(BF16)
+        pay_b[g] = jnp.where(left, east, west).astype(BF16)
 
 
 def fill_ghosts(ref, span, count):
@@ -238,43 +241,49 @@
         band = Band(z, scratch)
         span = z.main // SUB
         band.load(rows_f.at[0, z.steps - 1], main_at, span)
-
-        def sub_window(q, carry):
-            band.set_operators(rows_c, q, main_at, span)
-            band.steps(rows_f, q, 1 - q, main_at, span)
-            band.store(inner.at[q], span)
-            return carry
-
-        lax.fori_loop(0, 2, sub_window, 0)
+        band.set_operators(rows_c, 0, main_at, span)
+        band.steps(rows_f, 0, 1, main_at, span)
+        band.store(inner.at[0], span)
+        cut = REACH * (z.steps - 1) // SUB * SUB
+        span -= 2 * cut // SUB
+        band.load(inner.at[0], cut, span)
+        band.set_operators(rows_c, 1, main_at + cut, span)
+        band.steps(rows_f, 1, 0, main_at + cut, span)
+        band.store(inner.at[1], span, cut)
         for f in range(z.fields):
             for g in range(z.core // SUB):
                 core[f, g] = tile_of(inner.at[1], f, slice(z.halo + SUB * g, z.halo + SUB * (g + 1)))
 
 
 def rim_kernel(z, active, ra, rb, inner, rows_f_in, rows_c_in, rows_f, rows_c, ko, so, edge, *refs):
-    late_operators, (obuf, tmp), scratch = refs[:5], refs[5:7], refs[7:]
+    late_operators, (obuf, tmp, edges), scratch = refs[:5], refs[5:8], refs[8:]
     half, chip = half_and_chip()
-    for q, pay in ((half, ra), (1 - half, rb)):
-
-        def put(ref, start, groups):
-            for g in range(groups):
-                tile = pay[start + g].astype(F32)
-                at = jnp.where(half == 0, z.halo - SUB * (groups - g), z.main + SUB * g)
+    for n, pay in enumerate((ra, rb)):
+        for g in range(z.payload):
+            tile = pay[g].astype(F32)
+            for p in range(2):
+                edges[n, p, SUB * g : SUB * (g + 1), :] = tile[SUB * p : SUB * (p + 1)]
+
+    def place_edges(side):
+        for n, q in ((0, side), (1, 1 - side)):
+            blocks = [(rows_c.at[q, c], z.coef_start + c * z.depth, z.depth) for c in range(4)]
+            for k in range(z.steps):
+                for f in range(z.fields):
+                    blocks.append((rows_f.at[q, k, f], z.starts[k] + f * z.depths[k], z.depths[k]))
+            for ref, start, depth in blocks:
+                at = z.main if side else z.halo - depth
                 for p in range(2):
-                    ref[p, aligned(at, SUB), :] = tile[SUB * p : SUB * (p + 1)]
-
-        for c in range(4):
-            put(rows_c.at[q, c], z.coef_start + c * z.coef_groups, z.coef_groups)
-        for k in range(z.steps):
-            for f in range(z.fields):
-                put(rows_f.at[q, k, f], z.group_start[k] + f * z.groups[k], z.groups[k])
+                    ref[p, at : at + depth, :] = edges[n, p, start : start + depth, :]
+
+    for side in range(2):
+        pl.when(half == side)(functools.partial(place_edges, side))
 
     @pl.when(chip != active)
     def _():
         co_core, co_rim, co_late, mix_first, mix_last = late_operators
         for q, co, mix, columns, offset in (
             (0, co_core, mix_first, z.core, z.halo * (2 - half)),
-            (0, co_rim, mix_first, z.rim, (z.window - z.rim) * half),
+            (0, co_rim, mix_first, z.outer, (z.window - z.outer) * half),
             (1, co_late, mix_last, z.main - z.halo, z.halo * half + z.inset),
         ):
             Band(z, scratch[:4] + (co, mix)).set_operators(rows_c, q, offset, columns // SUB)
@@ -282,30 +291,41 @@
     @pl.when(chip == active)
     def _():
         band = Band(z, scratch)
-        span = z.rim // SUB
-        offset = (z.window - z.rim) * half
-        rim = slice(z.halo, 2 * z.halo)
-        band.load(rows_f.at[0, z.steps - 1], offset, span)
-
-        def sub_window(q, carry):
-            band.set_operators(rows_c, q, offset, span)
-            band.steps(rows_f, q, 1 - q, offset, span)
-            band.store(tmp, span)
-
-            @pl.when(q == 1)
-            def _():
-                for f in range(z.fields):
-                    for g in range(z.halo // SUB):
-                        edge[f, g] = tile_of(tmp, f, slice(z.halo + SUB * g, z.halo + SUB * (g + 1)))
-
-            place = jnp.where(q == half, 1, 0)
+        start = z.halo - z.depth
+        offset = start + (z.main + z.depth - z.rim - start) * half
+        base = start + (2 * z.halo + z.depth - z.rim - start) * half
+        sublane = lax.broadcasted_iota(jnp.int32, (SUB, z.lanes), 0)
+        mine = []
+        for g in range(z.halo // SUB):
+            at = sublane + SUB * g
+            mine.append(jnp.where(half == 0, at, z.halo - 1 - at) < z.rim_own)
+
+        def keep(q):
+            place = jnp.where(half == q, 1, 0)
             for f in range(z.fields):
+                merged = []
                 for p in range(2):
                     obuf[place, f, p] = inner[q, f, p, aligned((z.main - z.own) * half, z.own), :]
-                    obuf[place, f, p, aligned((z.own - z.halo) * half, z.halo), :] = tmp[f, p, rim, :]
-            return carry
-
-        lax.fori_loop(0, 2, sub_window, 0)
+                    for g in range(z.halo // SUB):
+                        rim = tmp[f, p, z.halo + SUB * g : z.halo + SUB * (g + 1), :]
+                        own = inner[q, f, p, aligned((z.main - z.halo) * half + SUB * g, SUB), :]
+                        merged.append(jnp.where(mine[g], rim, own))
+                        obuf[place, f, p, aligned((z.own - z.halo) * half + SUB * g, SUB), :] = merged[-1]
+                if q == 1:
+                    for g in range(z.halo // SUB):
+                        edge[f, g] = jnp.concatenate([merged[g], merged[g + z.halo // SUB]], axis=0).astype(BF16)
+
+        band.load(rows_f.at[0, z.steps - 1], offset, z.rim // SUB)
+        band.set_operators(rows_c, 0, offset, z.rim // SUB)
+        band.steps(rows_f, 0, 1, offset, z.rim // SUB)
+        band.store(tmp, z.rim // SUB, base)
+        keep(0)
+        offset = z.inset + (z.main - 2 * z.halo) * half
+        band.load(tmp, z.inset, 2 * z.halo // SUB)
+        band.set_operators(rows_c, 1, offset, 2 * z.halo // SUB)
+        band.steps(rows_f, 1, 0, offset, 2 * z.halo // SUB)
+        band.store(tmp, 2 * z.halo // SUB, z.inset)
+        keep(1)
         ko[...] = obuf[0]
         so[...] = obuf[1]
 
@@ -338,14 +358,14 @@
     @pl.when(chip == active)
     def _():
         groups = z.halo // SUB
-        span = z.rim // SUB
+        span = z.outer // SUB
         put_tiles(z, tmp, lambda f: [far[f, g] for g in range(groups)], 2 * z.halo * half)
         put_tiles(z, tmp, lambda f: [near[f, g] for g in range(groups)], z.halo)
         first = (z.core // SUB - groups) * half
         put_tiles(z, tmp, lambda f: [core[f, first + g] for g in range(groups)], 2 * z.halo * (1 - half))
         band = Band(z, scratch + (co_rim, mix_first))
         band.load(tmp, 0, span)
-        band.steps(rows_f, 0, 0, (z.window - z.rim) * half, span)
+        band.steps(rows_f, 0, 0, (z.window - z.outer) * half, span)
         band.store(tmp, span, z.base)
         outer, inner = 2 * z.halo, z.core - z.halo
         start = z.inset + z.base
@@ -413,6 +433,7 @@
             pltpu.VMEM((4, z.rows, z.strip), F32),
             pltpu.VMEM((z.fields, 1, z.fields), F32),
             pltpu.VMEM((4, z.rows, z.strip), F32),
+            pltpu.VMEM((2, 2, SUB * z.payload, z.lanes), F32),
             pltpu.SemaphoreType.DMA((5 + z.steps,)),
         ],
         compiler_params=params,
@@ -483,7 +504,7 @@
             shape(half_dims, F32),
             tiles(z.halo),
             stencil(z.core),
-            stencil(z.rim),
+            stencil(z.outer),
             stencil(z.main - z.halo),
             mixing,
             mixing,
@@ -493,7 +514,8 @@
         input_output_aliases={3: 0, 4: 1},
         scratch_shapes=[
             pltpu.VMEM((2,) + half_dims, F32),
-            pltpu.VMEM((z.fields, 2, z.rim, z.lanes), F32),
+            pltpu.VMEM((z.fields, 2, z.rim + SUB, z.lanes), F32),
+            pltpu.VMEM((2, 2, SUB * z.payload, z.lanes), F32),
         ]
         + band_scratch(z.wide)
         + operator_scratch(z.rim),

time: 40.6 us -> 38.4 us (0.946)
  starting transfers between devices: 23.3 us -> 20.9 us
  Pallas kernels: 12.9 us -> 13.5 us
    ppermute x1, starting transfers between devices: 6.75 us -> 4.47 us  [per_device(): far = lax.ppermute(edge, ('tm', 'space'), across)]
    ppermute x1, waiting for transfers between devices: 2.48 us -> 1.91 us  [per_device(): far = lax.ppermute(edge, ('tm', 'space'), across)]
  transfers between devices with their start and end apart: 8 -> 8, of which waited for: 2 -> 3; matrix products, arithmetic and copies ran while one was open for 0% -> 0% of each run, Pallas kernels for 8% -> 9%
where the time goes in v5:
time: 38.4 us; the launch traced here: 38.3 us
  starting transfers between devices  20.9 us (54%)
  Pallas kernels  13.5 us (35%)
  waiting for transfers between devices  3.81 us (10%)
    ppermute x1, starting transfers between devices, per_device(): core = lax.ppermute(core, ('tm', 'space'), down)  9.79 us
    pallas_call x1, Pallas kernels, per_device(): pl.pallas_call(functools.partial(late_kernel, z, 0), out_shape=[shape(hal...  6.21 us
    ppermute x1, starting transfers between devices, per_device(): got_a = lax.ppermute(pay_a, ('tm', 'space'), perm_a)  5.67 us
    ppermute x1, starting transfers between devices, per_device(): far = lax.ppermute(edge, ('tm', 'space'), across)  4.47 us
    pallas_call x1, Pallas kernels, per_device(): pl.pallas_call(functools.partial(prepare_kernel, z), out_shape=[shape(f_s...  2.63 us
    pallas_call x1, Pallas kernels, per_device(): pl.pallas_call(functools.partial(early_kernel, z, 0), out_shape=shape((z....  2.56 us
    ppermute x1, waiting for transfers between devices, per_device(): far = lax.ppermute(edge, ('tm', 'space'), across)  1.91 us
    ppermute x1, waiting for transfers between devices, per_device(): got = lax.ppermute(sent, 'tm', partner)  1.71 us
  transfers between devices with their start and end apart: 8, of which 3 were waited for; matrix products, arithmetic and copies ran while one was open for 0% of the time, Pallas kernels for 9%

profile of v5, /device:TPU:0, one launch (start us, length us, event | category | flops | bytes accessed | tf_op | source)
XLA Modules:
  0.0 38.3 jit_solution(1314766937372154143)
XLA Ops:
  0.0 2.6 %prepare.1 = (bf16[4,6,2,112,128]{4,3,2,1,0:T(8,128)(2,1)S(1)}, bf16[4,6,2,112,128]{4,3,2,1,0:T(8,128)(2,1)S(1)}, f32[5,2,112,128]{3,2,1,0:T(8,128)S(1)}, f32[5,...) custom-call(bf16[1,4,6,256,128]{4,3,2,1,0:T(8,128)(2,1)} %fo_in.1, ...), custom_call_target="tpu_custom_call" | custom-call | tf_op jit(solution)/shard_map/prepare/pallas_call | solution.py:419
  2.6 0.5 %collective-permute-start = (bf16[4,6,2,112,128]{4,3,2,1,0:T(8,128)(2,1)S(1)}, bf16[4,6,2,112,128]{4,3,2,1,0:T(8,128)(2,1)S(1)}, u32[]{:S(2)}, u32[]{:S(2)}) collective-permute-start(bf16[4,6,2,112,128]{4,3,2,1,0:T(8,128)(2,1)S(1)} %get-tuple-element.27), channel_id=1, source_target_pairs={{0,8},{8,0},{16,24},{24,16},{1,9},{9,1},{17,25},{25,17},{2,10},{10... | collective-permute-start | bytes 4128776 | tf_op jit(solution)/shard_map/ppermute | solution.py:462
  3.2 0.1 collective-permute-start.1
  3.2 5.7 %collective-permute-start.3 = (bf16[60,16,128]{2,1,0:T(8,128)(2,1)S(1)}, bf16[60,16,128]{2,1,0:T(8,128)(2,1)S(1)}, u32[]{:S(2)}, u32[]{:S(2)}) collective-permute-start(bf16[60,16,128]{2,1,0:T(8,128)(2,1)S(1)} %get-tuple-element.31), channel_id=1, source_target_pairs={{0,15},{1,8},{2,9},{3,10},{4,11},{5,12},{6,13},{7,14},{8,1},{9,2},... | collective-permute-start | bytes 737288 | tf_op jit(solution)/shard_map/ppermute | solution.py:464
  8.9 0.0 collective-permute-start.4
  8.9 0.0 collective-permute-done.1.rc
  8.9 0.0 collective-permute-done.rf
  8.9 0.5 %inner.1 = (f32[2,4,6,2,136,128]{5,4,3,2,1,0:T(8,128)S(1)}, f32[2,5,2,136,128]{4,3,2,1,0:T(8,128)S(1)}, f32[2,6,2,112,128]{4,3,2,1,0:T(8,128)S(1)}, bf16[6,8,16,128]{3,2,1,0:T(8,128)(2,1)S(1)}) custom-call(bf16[4,6,2,112,128]{4,3,2,1,0:T(8,128)(2,1)S(1)} %get-tuple-element.26.kf, bf16[4,6,2,112,128]{4,3,2,1,0:T(8,128)(2,1)S(1)} %collective-permute-done.rf, ...), custom_call_target="tpu_custom_call" | custom-call | flops 1000000000 | bytes 20000000 | tf_op jit(solution)/shard_map/inner/pallas_call | solution.py:485
  9.5 9.8 %collective-permute-start.2 = (bf16[6,8,16,128]{3,2,1,0:T(8,128)(2,1)S(1)}, bf16[6,8,16,128]{3,2,1,0:T(8,128)(2,1)S(1)}, u32[]{:S(2)}, u32[]{:S(2)}) collective-permute-start(bf16[6,8,16,128]{3,2,1,0:T(8,128)(2,1)S(1)} %get-tuple-element.30), channel_id=1, source_target_pairs={{0,16},{1,17},{2,18},{3,19},{4,20},{5,21},{6,22},{7,23},{8,24},{9,... | collective-permute-start | bytes 589832 | tf_op jit(solution)/shard_map/ppermute | solution.py:497
  19.3 0.0 collective-permute-done.3.ra
  19.3 0.0 collective-permute-done.4.rb
  19.3 0.5 %rim.1 = (f32[2,4,6,2,136,128]{5,4,3,2,1,0:T(8,128)S(1)}, f32[2,5,2,136,128]{4,3,2,1,0:T(8,128)S(1)}, f32[6,2,64,128]{3,2,1,0:T(8,128)S(1)}, f32[6,2,64,128]{3,2...) custom-call(bf16[60,16,128]{2,1,0:T(8,128)(2,1)S(1)} %collective-per, ...), custom_call_target="tpu_custom_call", output_to_operand_aliasing={{0}: (3, {}), {1}: (4, {})} | custom-call | flops 1000000000 | bytes 20000000 | tf_op jit(solution)/shard_map/rim/pallas_call | solution.py:498
  19.7 4.5 %collective-permute-start.6 = (bf16[6,3,16,128]{3,2,1,0:T(8,128)(2,1)S(1)}, bf16[6,3,16,128]{3,2,1,0:T(8,128)(2,1)S(1)}, u32[]{:S(2)}, u32[]{:S(2)}) collective-permute-start(bf16[6,3,16,128]{3,2,1,0:T(8,128)(2,1)S(1)} %get-tuple-element.36), channel_id=1, source_target_pairs={{0,16},{1,17},{2,18},{3,19},{4,20},{5,21},{6,22},{7,23},{8,24},{9,... | collective-permute-start | bytes 221192 | tf_op jit(solution)/shard_map/ppermute | solution.py:535
  24.2 0.3 collective-permute-start.5
  24.5 0.2 collective-permute-done.2.core
  24.6 2.6 %early.1.state = f32[6,2,72,128]{3,2,1,0:T(8,128)S(1)} custom-call(bf16[6,8,16,128]{3,2,1,0:T(8,128)(2,1)S(1)} %collective-permute-done.2.core, f32[2,4,6,2,136,128]{5,4,3,2,1,0:T(8,128)S(1)} %get-tuple-element.37.rows_f, f32[10,8,2,8,128]{4,3,2,1,0:T(8,128)S(1)} %get-tuple-element.38.co, f32[36,8,128]{2,1,0:T(8,128)S(1)} %get-tuple-element.39.mix.mix_first), custom_call_target="tpu_custom_call" | custom-call | tf_op jit(solution)/shard_map/early/pallas_call | solution.py:526
  27.2 1.9 %collective-permute-done.6.far = bf16[6,3,16,128]{3,2,1,0:T(8,128)(2,1)S(1)} collective-permute-done((bf16[6,3,16,128]{3,2,1,0:T(8,128)(2,1)S(1)}, bf16[6,3,16,128]{3,2,1,0:T(8,128)(2,1)S(1)}, u32[]{:S(2)}, u32[]{:S(2)}) %collective-permute-start.6) | collective-permute-done | bytes 73760 | tf_op jit(solution)/shard_map/ppermute | solution.py:535
  29.1 0.0 collective-permute-done.5.near
  29.1 6.2 %late.1 = (f32[6,2,64,128]{3,2,1,0:T(8,128)S(1)}, f32[6,2,64,128]{3,2,1,0:T(8,128)S(1)}) custom-call(bf16[6,8,16,128]{3,2,1,0:T(8,128)(2,1)S(1)} %collective-permute-done.2.core, bf16[6,3,16,128]{3,2,1,0:T(8,128)(2,1)S(1)} %collective-permute-done.5.near, ...), custom_call_target="tpu_custom_call", output_to_operand_aliasing={{0}: (9, {}), {1}: (10, {})} | custom-call | tf_op jit(solution)/shard_map/late/pallas_call | solution.py:537
  35.3 0.1 collective-permute-start.7
  35.4 1.7 %collective-permute-done.7.got = f32[6,2,64,128]{3,2,1,0:T(8,128)S(1)} collective-permute-done((f32[6,2,64,128]{3,2,1,0:T(8,128)S(1)}, f32[6,2,64,128]{3,2,1,0:T(8,128)S(1)}, u32[]{:S(2)}, u32[]{:S(2)}) %collective-permute-start.7) | collective-permute-done | bytes 393248 | tf_op jit(solution)/shard_map/ppermute | solution.py:551
  37.1 1.2 %finish.1 = f32[1,6,256,128]{3,2,1,0:T(8,128)} custom-call(f32[6,2,64,128]{3,2,1,0:T(8,128)S(1)} %get-tuple-element.45.keep, f32[6,2,64,128]{3,2,1,0:T(8,128)S(1)} %collective-permute-done.7.got), custom_call_target="tpu_custom_call" | custom-call | tf_op jit(solution)/shard_map/finish/pallas_call | solution.py:552
Async XLA Ops:
  2.6 6.3 %collective-permute-start = (bf16[4,6,2,112,128]{4,3,2,1,0:T(8,128)(2,1)S(1)}, bf16[4,6,2,112,128]{4,3,2,1,0:T(8,128)(2,1)S(1)}, u32[]{:S(2)}, u32[]{:S(2)}) collective-permute-start(bf16[4,6,2,112,128]{4,3,2,1,0:T(8,128)(2,1)S(1)} %get-tuple-element.27), channel_id=1, source_target_pairs={{0,8},{8,0},{16,24},{24,16},{1,9},{9,1},{17,25},{25,17},{2,10},{10... | collective-permute-start | bytes 4128776 | tf_op jit(solution)/shard_map/ppermute | solution.py:462
  3.2 5.8 %collective-permute-start.1 = (f32[5,2,112,128]{3,2,1,0:T(8,128)S(1)}, f32[5,2,112,128]{3,2,1,0:T(8,128)S(1)}, u32[]{:S(2)}, u32[]{:S(2)}) collective-permute-start(f32[5,2,112,128]{3,2,1,0:T(8,128)S(1)} %get-tuple-element.29), channel_id=1, source_target_pairs={{0,8},{8,0},{16,24},{24,16},{1,9},{9,1},{17,25},{25,17},{2,10},{10... | collective-permute-start | bytes 1720328 | tf_op jit(solution)/shard_map/ppermute | solution.py:463
  3.2 16.0 %collective-permute-start.3 = (bf16[60,16,128]{2,1,0:T(8,128)(2,1)S(1)}, bf16[60,16,128]{2,1,0:T(8,128)(2,1)S(1)}, u32[]{:S(2)}, u32[]{:S(2)}) collective-permute-start(bf16[60,16,128]{2,1,0:T(8,128)(2,1)S(1)} %get-tuple-element.31), channel_id=1, source_target_pairs={{0,15},{1,8},{2,9},{3,10},{4,11},{5,12},{6,13},{7,14},{8,1},{9,2},... | collective-permute-start | bytes 737288 | tf_op jit(solution)/shard_map/ppermute | solution.py:464
  8.9 10.4 %collective-permute-start.4 = (bf16[60,16,128]{2,1,0:T(8,128)(2,1)S(1)}, bf16[60,16,128]{2,1,0:T(8,128)(2,1)S(1)}, u32[]{:S(2)}, u32[]{:S(2)}) collective-permute-start(bf16[60,16,128]{2,1,0:T(8,128)(2,1)S(1)} %get-tuple-element.32), channel_id=1, source_target_pairs={{0,1},{1,2},{2,3},{3,4},{4,5},{5,6},{6,7},{7,0},{8,15},{9,8},{10,9... | collective-permute-start | bytes 737288 | tf_op jit(solution)/shard_map/ppermute | solution.py:465
  9.5 15.2 %collective-permute-start.2 = (bf16[6,8,16,128]{3,2,1,0:T(8,128)(2,1)S(1)}, bf16[6,8,16,128]{3,2,1,0:T(8,128)(2,1)S(1)}, u32[]{:S(2)}, u32[]{:S(2)}) collective-permute-start(bf16[6,8,16,128]{3,2,1,0:T(8,128)(2,1)S(1)} %get-tuple-element.30), channel_id=1, source_target_pairs={{0,16},{1,17},{2,18},{3,19},{4,20},{5,21},{6,22},{7,23},{8,24},{9,... | collective-permute-start | bytes 589832 | tf_op jit(solution)/shard_map/ppermute | solution.py:497
  19.7 9.4 %collective-permute-start.6 = (bf16[6,3,16,128]{3,2,1,0:T(8,128)(2,1)S(1)}, bf16[6,3,16,128]{3,2,1,0:T(8,128)(2,1)S(1)}, u32[]{:S(2)}, u32[]{:S(2)}) collective-permute-start(bf16[6,3,16,128]{3,2,1,0:T(8,128)(2,1)S(1)} %get-tuple-element.36), channel_id=1, source_target_pairs={{0,16},{1,17},{2,18},{3,19},{4,20},{5,21},{6,22},{7,23},{8,24},{9,... | collective-permute-start | bytes 221192 | tf_op jit(solution)/shard_map/ppermute | solution.py:535
  24.2 4.9 %collective-permute-start.5 = (bf16[6,3,16,128]{3,2,1,0:T(8,128)(2,1)S(1)}, bf16[6,3,16,128]{3,2,1,0:T(8,128)(2,1)S(1)}, u32[]{:S(2)}, u32[]{:S(2)}) collective-permute-start(bf16[6,3,16,128]{3,2,1,0:T(8,128)(2,1)S(1)} %get-tuple-element.36), channel_id=1, source_target_pairs={{0,16},{1,17},{2,18},{3,19},{4,20},{5,21},{6,22},{7,23},{8,24},{9,... | collective-permute-start | bytes 221192 | tf_op jit(solution)/shard_map/ppermute | solution.py:536
  35.3 1.8 %collective-permute-start.7 = (f32[6,2,64,128]{3,2,1,0:T(8,128)S(1)}, f32[6,2,64,128]{3,2,1,0:T(8,128)S(1)}, u32[]{:S(2)}, u32[]{:S(2)}) collective-permute-start(f32[6,2,64,128]{3,2,1,0:T(8,128)S(1)} %get-tuple-element.46), channel_id=1, source_target_pairs={{0,8},{8,0},{16,24},{24,16},{1,9},{9,1},{17,25},{25,17},{2,10},{10... | collective-permute-start | bytes 1179656 | tf_op jit(solution)/shard_map/ppermute | solution.py:551

commit v6 on v5

--- a/solution.py
+++ b/solution.py
@@ -30,7 +30,9 @@
         self.depth = self.depths[-1]
         self.starts = [self.fields * sum(self.depths[:k]) for k in range(self.steps)]
         self.coef_start = self.fields * sum(self.depths)
-        self.payload = -(-(self.coef_start + 4 * self.depth) // SUB)
+        self.coef_depths = [self.halo - c for c in range(4)]
+        self.coef_starts = [self.coef_start + sum(self.coef_depths[:c]) for c in range(4)]
+        self.payload = -(-(self.coef_start + sum(self.coef_depths)) // SUB)
         self.message = self.own + self.halo
         self.core = self.message - self.halo
         self.wide, self.narrow = self.main // SUB, (self.main - self.halo) // SUB
@@ -53,7 +55,11 @@
     coef_copies = [
         pltpu.make_async_copy(ref.at[0], co.at[c], sems.at[c]) for c, ref in enumerate((zf, mf, zc, mc))
     ]
-    forcing_copies = [pltpu.make_async_copy(fo_in.at[0, k], fo.at[k], sems.at[5 + k]) for k in range(z.steps)]
+    part = z.fields // 2
+    forcing_copies = []
+    for n in range(2 * z.steps):
+        block = (n // 2, pl.ds(n % 2 * part, part))
+        forcing_copies.append(pltpu.make_async_copy(fo_in.at[(0, *block)], fo.at[block], sems.at[5 + n]))
     mixing_copy = pltpu.make_async_copy(cp_in, cp, sems.at[4])
     for copy in coef_copies + [mixing_copy] + forcing_copies:
         copy.start()
@@ -78,15 +84,16 @@
         if c == 1:
             values = jnp.where(row < z.rows - 1, values, jnp.zeros_like(values))
         both = columns(values, count % slots)
-        split(both, z.depth, z.coef_start + c * z.depth, keep_c.at[c], send_c.at[c])
+        split(both, z.coef_depths[c], z.coef_starts[c], keep_c.at[c], send_c.at[c])
         count += 1
     mixing_copy.wait()
     for ref in (keep_c, send_c):
         for g in range(z.fields):
             ref[4, 0, g : g + 1, : z.fields] = cp[g]
     for k in range(z.steps):
-        forcing_copies[k].wait()
         for f in range(z.fields):
+            if f % part == 0:
+                forcing_copies[2 * k + f // part].wait()
             both = columns(fo[k, f].astype(F32), count % slots)
             split(both, z.depths[k], z.starts[k] + f * z.depths[k], keep_f.at[k, f], send_f.at[k, f])
             count += 1
@@ -137,12 +144,6 @@
                 co[i, 4, p] = OMEGA * south[p]
                 co[i, 5, p] = (0.5 * OMEGA) * u1[i, 2, p]
                 co[i, 6, p] = (0.5 * OMEGA) * u1[i, 3, p]
-        for g in range(z.fields):
-            for f in range(z.fields):
-                value = rows_c[q, 4, 0, g : g + 1, f : f + 1]
-                if f == g:
-                    value = value + 1.0
-                self.kk[g * z.fields + f] = jnp.broadcast_to(OMEGA * value, (SUB, z.lanes))
 
     def load(self, at, offset, span):
         for i in range(span):
@@ -209,6 +210,15 @@
         lax.fori_loop(begin, last + 1, one, 0)
 
 
+def set_mixing(z, mix, table):
+    for g in range(z.fields):
+        for f in range(z.fields):
+            value = table[g : g + 1, f : f + 1]
+            if f == g:
+                value = value + 1.0
+            mix[g * z.fields + f] = jnp.broadcast_to(OMEGA * value, (SUB, z.lanes))
+
+
 def aligned(offset, count):
     return pl.ds(pl.multiple_of(offset, SUB), count)
 
@@ -217,8 +227,9 @@
     return jnp.concatenate([ref[f, p, at, :] for p in range(2)], axis=0).astype(BF16)
 
 
-def inner_kernel(z, active, kf, rf, kc, rc, rows_f, rows_c, inner, core, *scratch):
+def inner_kernel(z, active, kf, rf, kc, rc, rows_f, rows_c, inner, core, mix_first, mix_last, *scratch):
     half, chip = half_and_chip()
+    *scratch, tables = scratch
     main_at = z.halo * (1 - half)
     blank = jnp.zeros((z.halo, z.lanes), F32)
 
@@ -230,15 +241,18 @@
         for c in range(4):
             for p in range(2):
                 put(rows_c.at[q, c, p], coefs[c, p])
-        rows_c[q, 4, 0, :SUB, :] = coefs[4, 0, :SUB, :]
+        tables[q, :, :] = coefs[4, 0, :SUB, :]
         for k in range(z.steps):
             for f in range(z.fields):
                 for p in range(2):
                     put(rows_f.at[q, k, f, p], forcing[k, f, p])
 
+    set_mixing(z, mix_first, tables.at[0])
+    set_mixing(z, mix_last, tables.at[1])
+
     @pl.when(chip == active)
     def _():
-        band = Band(z, scratch)
+        band = Band(z, (*scratch, mix_first))
         span = z.main // SUB
         band.load(rows_f.at[0, z.steps - 1], main_at, span)
         band.set_operators(rows_c, 0, main_at, span)
@@ -246,6 +260,7 @@
         band.store(inner.at[0], span)
         cut = REACH * (z.steps - 1) // SUB * SUB
         span -= 2 * cut // SUB
+        band = Band(z, (*scratch, mix_last))
         band.load(inner.at[0], cut, span)
         band.set_operators(rows_c, 1, main_at + cut, span)
         band.steps(rows_f, 1, 0, main_at + cut, span)
@@ -255,8 +270,8 @@
                 core[f, g] = tile_of(inner.at[1], f, slice(z.halo + SUB * g, z.halo + SUB * (g + 1)))
 
 
-def rim_kernel(z, active, ra, rb, inner, rows_f_in, rows_c_in, rows_f, rows_c, ko, so, edge, *refs):
-    late_operators, (obuf, tmp, edges), scratch = refs[:5], refs[5:8], refs[8:]
+def rim_kernel(z, active, ra, rb, inner, mix_first, mix_last, rows_f_in, rows_c_in, rows_f, rows_c, ko, so, edge, *refs):
+    (co_core, co_rim, co_late), (obuf, tmp, edges), scratch = refs[:3], refs[3:6], refs[6:]
     half, chip = half_and_chip()
     for n, pay in enumerate((ra, rb)):
         for g in range(z.payload):
@@ -266,7 +281,7 @@
 
     def place_edges(side):
         for n, q in ((0, side), (1, 1 - side)):
-            blocks = [(rows_c.at[q, c], z.coef_start + c * z.depth, z.depth) for c in range(4)]
+            blocks = [(rows_c.at[q, c], z.coef_starts[c], z.coef_depths[c]) for c in range(4)]
             for k in range(z.steps):
                 for f in range(z.fields):
                     blocks.append((rows_f.at[q, k, f], z.starts[k] + f * z.depths[k], z.depths[k]))
@@ -280,17 +295,16 @@
 
     @pl.when(chip != active)
     def _():
-        co_core, co_rim, co_late, mix_first, mix_last = late_operators
         for q, co, mix, columns, offset in (
             (0, co_core, mix_first, z.core, z.halo * (2 - half)),
             (0, co_rim, mix_first, z.outer, (z.window - z.outer) * half),
             (1, co_late, mix_last, z.main - z.halo, z.halo * half + z.inset),
         ):
-            Band(z, scratch[:4] + (co, mix)).set_operators(rows_c, q, offset, columns // SUB)
+            Band(z, (*scratch[:4], co, mix)).set_operators(rows_c, q, offset, columns // SUB)
 
     @pl.when(chip == active)
     def _():
-        band = Band(z, scratch)
+        band = Band(z, (*scratch, mix_first))
         start = z.halo - z.depth
         offset = start + (z.main + z.depth - z.rim - start) * half
         base = start + (2 * z.halo + z.depth - z.rim - start) * half
@@ -320,6 +334,7 @@
         band.steps(rows_f, 0, 1, offset, z.rim // SUB)
         band.store(tmp, z.rim // SUB, base)
         keep(0)
+        band = Band(z, (*scratch, mix_last))
         offset = z.inset + (z.main - 2 * z.halo) * half
         band.load(tmp, z.inset, 2 * z.halo // SUB)
         band.set_operators(rows_c, 1, offset, 2 * z.halo // SUB)
@@ -386,14 +401,19 @@
         so[...] = obuf[1]
 
 
-def finish_kernel(z, keep, got, out):
+def finish_kernel(z, keep, got, out, rows, sems):
     half, _ = half_and_chip()
+    copies = []
     for f in range(z.fields):
         for p in range(2):
             a, b = keep[f, p], got[f, p]
             west = jnp.where(half == 0, a, b)
             east = jnp.where(half == 0, b, a)
-            out[0, f, pl.ds(p, z.lanes, stride=2), :] = jnp.concatenate([west, east], axis=0).T
+            rows[f, pl.ds(p, z.lanes, stride=2), :] = jnp.concatenate([west, east], axis=0).T
+        copies.append(pltpu.make_async_copy(rows.at[f], out.at[0, f], sems.at[f]))
+        copies[-1].start()
+    for copy in copies:
+        copy.wait()
 
 
 def shape(dims, dtype):
@@ -434,7 +454,7 @@
             pltpu.VMEM((z.fields, 1, z.fields), F32),
             pltpu.VMEM((4, z.rows, z.strip), F32),
             pltpu.VMEM((2, 2, SUB * z.payload, z.lanes), F32),
-            pltpu.SemaphoreType.DMA((5 + z.steps,)),
+            pltpu.SemaphoreType.DMA((5 + 2 * z.steps,)),
         ],
         compiler_params=params,
         name="prepare",
@@ -473,21 +493,28 @@
 
     mixing = shape((z.fields**2, SUB, z.lanes), F32)
 
-    def operator_scratch(columns):
-        return [pltpu.VMEM(spec.shape, spec.dtype) for spec in (stencil(columns), mixing)]
+    def stencil_scratch(columns):
+        return [pltpu.VMEM(stencil(columns).shape, F32)]
 
     rows_f_shape = shape((2, z.steps, z.fields, 2, z.window, z.lanes), F32)
-    rows_c_shape = shape((2, 5, 2, z.window, z.lanes), F32)
+    rows_c_shape = shape((2, 4, 2, z.window, z.lanes), F32)
     half_dims = (z.fields, 2, z.own, z.lanes)
     def tiles(columns):
         return shape((z.fields, columns // SUB, 2 * SUB, z.lanes), BF16)
 
-    rows_f, rows_c, inner, core = pl.pallas_call(
+    rows_f, rows_c, inner, core, mix_first, mix_last = pl.pallas_call(
         functools.partial(inner_kernel, z, 1),
-        out_shape=[rows_f_shape, rows_c_shape, shape((2, z.fields, 2, z.main, z.lanes), F32), tiles(z.core)],
+        out_shape=[
+            rows_f_shape,
+            rows_c_shape,
+            shape((2, z.fields, 2, z.main, z.lanes), F32),
+            tiles(z.core),
+            mixing,
+            mixing,
+        ],
         in_specs=in_vmem(4),
-        out_specs=in_vmem(4),
-        scratch_shapes=band_scratch(z.wide) + operator_scratch(z.main),
+        out_specs=in_vmem(6),
+        scratch_shapes=band_scratch(z.wide) + stencil_scratch(z.main) + [pltpu.VMEM((2, SUB, z.lanes), F32)],
         compiler_params=params,
         cost_estimate=pl.CostEstimate(flops=10**9, bytes_accessed=2 * 10**7, transcendentals=0),
         name="inner",
@@ -495,7 +522,7 @@
     down = [(device(t, s), device(t ^ 2, s)) for t, s in everyone]
     across = [(device(t, s), device((t ^ 1) - 2, s + 1 if t % 2 else s - 1) if t >= 2 else device(t + 2, s)) for t, s in everyone]
     core = lax.ppermute(core, ("tm", "space"), down)
-    rows_f, rows_c, kept, sent, edge, co_core, co_rim, co_late, mix_first, mix_last = pl.pallas_call(
+    rows_f, rows_c, kept, sent, edge, co_core, co_rim, co_late = pl.pallas_call(
         functools.partial(rim_kernel, z, 1),
         out_shape=[
             rows_f_shape,
@@ -506,23 +533,21 @@
             stencil(z.core),
             stencil(z.outer),
             stencil(z.main - z.halo),
-            mixing,
-            mixing,
         ],
-        in_specs=in_vmem(5),
-        out_specs=in_vmem(10),
-        input_output_aliases={3: 0, 4: 1},
+        in_specs=in_vmem(7),
+        out_specs=in_vmem(8),
+        input_output_aliases={5: 0, 6: 1},
         scratch_shapes=[
             pltpu.VMEM((2,) + half_dims, F32),
             pltpu.VMEM((z.fields, 2, z.rim + SUB, z.lanes), F32),
             pltpu.VMEM((2, 2, SUB * z.payload, z.lanes), F32),
         ]
         + band_scratch(z.wide)
-        + operator_scratch(z.rim),
+        + stencil_scratch(z.rim),
         compiler_params=params,
         cost_estimate=pl.CostEstimate(flops=10**9, bytes_accessed=2 * 10**7, transcendentals=0),
         name="rim",
-    )(got_a, got_b, inner, rows_f, rows_c)
+    )(got_a, got_b, inner, mix_first, mix_last, rows_f, rows_c)
     state = pl.pallas_call(
         functools.partial(early_kernel, z, 0),
         out_shape=shape((z.fields, 2, z.core + SUB, z.lanes), F32),
@@ -553,7 +578,11 @@
         functools.partial(finish_kernel, z),
         out_shape=shape((1, z.fields, z.rows, z.strip), F32),
         in_specs=in_vmem(2),
-        out_specs=pl.BlockSpec(memory_space=pltpu.VMEM),
+        out_specs=pl.BlockSpec(memory_space=pltpu.HBM),
+        scratch_shapes=[
+            pltpu.VMEM((z.fields, z.rows, z.strip), F32),
+            pltpu.SemaphoreType.DMA((z.fields,)),
+        ],
         compiler_params=params,
         name="finish",
     )(kept, got)

time: 38.4 us -> 38 us (0.990)
  starting transfers between devices: 20.9 us -> 20.5 us
    ppermute x1, starting transfers between devices: 9.79 us -> 9.31 us  [per_device(): core = lax.ppermute(core, ('tm', 'space'), down)]
where the time goes in v6:
time: 38 us; the launch traced here: 37.8 us
  starting transfers between devices  20.5 us (54%)
  Pallas kernels  13.6 us (36%)
  waiting for transfers between devices  3.7 us (10%)
    ppermute x1, starting transfers between devices, per_device(): core = lax.ppermute(core, ('tm', 'space'), down)  9.31 us
    pallas_call x1, Pallas kernels, per_device(): pl.pallas_call(functools.partial(late_kernel, z, 0), out_shape=[shape(hal...  6.06 us
    ppermute x1, starting transfers between devices, per_device(): got_a = lax.ppermute(pay_a, ('tm', 'space'), perm_a)  5.67 us
    ppermute x1, starting transfers between devices, per_device(): far = lax.ppermute(edge, ('tm', 'space'), across)  4.76 us
    pallas_call x1, Pallas kernels, per_device(): pl.pallas_call(functools.partial(prepare_kernel, z), out_shape=[shape(f_s...  2.95 us
    pallas_call x1, Pallas kernels, per_device(): pl.pallas_call(functools.partial(early_kernel, z, 0), out_shape=shape((z....  2.47 us
    ppermute x1, waiting for transfers between devices, per_device(): far = lax.ppermute(edge, ('tm', 'space'), across)  1.81 us
    ppermute x1, waiting for transfers between devices, per_device(): got = lax.ppermute(sent, 'tm', partner)  1.71 us
  transfers between devices with their start and end apart: 8, of which 3 were waited for; matrix products, arithmetic and copies ran while one was open for 0% of the time, Pallas kernels for 9%

profile of v6, /device:TPU:0, one launch (start us, length us, event | category | flops | bytes accessed | tf_op | source)
XLA Modules:
  0.0 37.8 jit_solution(2954476122632873262)
XLA Ops:
  0.0 2.9 %prepare.1 = (bf16[4,6,2,112,128]{4,3,2,1,0:T(8,128)(2,1)S(1)}, bf16[4,6,2,112,128]{4,3,2,1,0:T(8,128)(2,1)S(1)}, f32[5,2,112,128]{3,2,1,0:T(8,128)S(1)}, f32[5,...) custom-call(bf16[1,4,6,256,128]{4,3,2,1,0:T(8,128)(2,1)} %fo_in.1, ...), custom_call_target="tpu_custom_call" | custom-call | tf_op jit(solution)/shard_map/prepare/pallas_call | solution.py:439
  3.0 0.5 %collective-permute-start = (bf16[4,6,2,112,128]{4,3,2,1,0:T(8,128)(2,1)S(1)}, bf16[4,6,2,112,128]{4,3,2,1,0:T(8,128)(2,1)S(1)}, u32[]{:S(2)}, u32[]{:S(2)}) collective-permute-start(bf16[4,6,2,112,128]{4,3,2,1,0:T(8,128)(2,1)S(1)} %get-tuple-element.27), channel_id=1, source_target_pairs={{0,8},{8,0},{16,24},{24,16},{1,9},{9,1},{17,25},{25,17},{2,10},{10... | collective-permute-start | bytes 4128776 | tf_op jit(solution)/shard_map/ppermute | solution.py:482
  3.5 0.1 collective-permute-start.1
  3.6 5.7 %collective-permute-start.3 = (bf16[61,16,128]{2,1,0:T(8,128)(2,1)S(1)}, bf16[61,16,128]{2,1,0:T(8,128)(2,1)S(1)}, u32[]{:S(2)}, u32[]{:S(2)}) collective-permute-start(bf16[61,16,128]{2,1,0:T(8,128)(2,1)S(1)} %get-tuple-element.31), channel_id=1, source_target_pairs={{0,15},{1,8},{2,9},{3,10},{4,11},{5,12},{6,13},{7,14},{8,1},{9,2},... | collective-permute-start | bytes 749576 | tf_op jit(solution)/shard_map/ppermute | solution.py:484
  9.2 0.0 collective-permute-start.4
  9.2 0.0 collective-permute-done.1.rc
  9.2 0.0 collective-permute-done.rf
  9.2 0.7 %inner.1 = (f32[2,4,6,2,136,128]{5,4,3,2,1,0:T(8,128)S(1)}, f32[2,4,2,136,128]{4,3,2,1,0:T(8,128)S(1)}, f32[2,6,2,112,128]{4,3,2,1,0:T(8,128)S(1)}, bf16[6,8,16,...) custom-call(bf16[4,6,2,112,128]{4,3,2,1,0:T(8,128)(2,1)S(1)} %get-tuple-element.26.kf, ...), custom_call_target="tpu_custom_call" | custom-call | flops 1000000000 | bytes 20000000 | tf_op jit(solution)/shard_map/inner/pallas_call | solution.py:505
  10.0 9.3 %collective-permute-start.2 = (bf16[6,8,16,128]{3,2,1,0:T(8,128)(2,1)S(1)}, bf16[6,8,16,128]{3,2,1,0:T(8,128)(2,1)S(1)}, u32[]{:S(2)}, u32[]{:S(2)}) collective-permute-start(bf16[6,8,16,128]{3,2,1,0:T(8,128)(2,1)S(1)} %get-tuple-element.30), channel_id=1, source_target_pairs={{0,16},{1,17},{2,18},{3,19},{4,20},{5,21},{6,22},{7,23},{8,24},{9,... | collective-permute-start | bytes 589832 | tf_op jit(solution)/shard_map/ppermute | solution.py:524
  19.3 0.0 collective-permute-done.3.ra
  19.3 0.0 collective-permute-done.4.rb
  19.3 0.4 rim.1
  19.6 4.8 %collective-permute-start.6 = (bf16[6,3,16,128]{3,2,1,0:T(8,128)(2,1)S(1)}, bf16[6,3,16,128]{3,2,1,0:T(8,128)(2,1)S(1)}, u32[]{:S(2)}, u32[]{:S(2)}) collective-permute-start(bf16[6,3,16,128]{3,2,1,0:T(8,128)(2,1)S(1)} %get-tuple-element.38), channel_id=1, source_target_pairs={{0,16},{1,17},{2,18},{3,19},{4,20},{5,21},{6,22},{7,23},{8,24},{9,... | collective-permute-start | bytes 221192 | tf_op jit(solution)/shard_map/ppermute | solution.py:560
  24.4 0.1 collective-permute-start.5
  24.5 0.2 collective-permute-done.2.core
  24.7 2.5 %early.1.state = f32[6,2,72,128]{3,2,1,0:T(8,128)S(1)} custom-call(bf16[6,8,16,128]{3,2,1,0:T(8,128)(2,1)S(1)} %collective-permute-done.2.core, f32[2,4,6,2,136,128]{5,4,3,2,1,0:T(8,128)S(1)} %get-tuple-element.39.rows_f, f32[10,8,2,8,128]{4,3,2,1,0:T(8,128)S(1)} %get-tuple-element.40.co, f32[36,8,128]{2,1,0:T(8,128)S(1)} %get-tuple-element.34.mix_first.mix), custom_call_target="tpu_custom_call" | custom-call | tf_op jit(solution)/shard_map/early/pallas_call | solution.py:551
  27.1 1.8 %collective-permute-done.6.far = bf16[6,3,16,128]{3,2,1,0:T(8,128)(2,1)S(1)} collective-permute-done((bf16[6,3,16,128]{3,2,1,0:T(8,128)(2,1)S(1)}, bf16[6,3,16,128]{3,2,1,0:T(8,128)(2,1)S(1)}, u32[]{:S(2)}, u32[]{:S(2)}) %collective-permute-start.6) | collective-permute-done | bytes 73760 | tf_op jit(solution)/shard_map/ppermute | solution.py:560
  28.9 0.0 collective-permute-done.5.near
  28.9 6.1 %late.1 = (f32[6,2,64,128]{3,2,1,0:T(8,128)S(1)}, f32[6,2,64,128]{3,2,1,0:T(8,128)S(1)}) custom-call(bf16[6,8,16,128]{3,2,1,0:T(8,128)(2,1)S(1)} %collective-permute-done.2.core, bf16[6,3,16,128]{3,2,1,0:T(8,128)(2,1)S(1)} %collective-permute-done.5.near, ...), custom_call_target="tpu_custom_call", output_to_operand_aliasing={{0}: (9, {}), {1}: (10, {})} | custom-call | tf_op jit(solution)/shard_map/late/pallas_call | solution.py:562
  35.0 0.1 collective-permute-start.7
  35.1 1.7 %collective-permute-done.7.got = f32[6,2,64,128]{3,2,1,0:T(8,128)S(1)} collective-permute-done((f32[6,2,64,128]{3,2,1,0:T(8,128)S(1)}, f32[6,2,64,128]{3,2,1,0:T(8,128)S(1)}, u32[]{:S(2)}, u32[]{:S(2)}) %collective-permute-start.7) | collective-permute-done | bytes 393248 | tf_op jit(solution)/shard_map/ppermute | solution.py:576
  36.8 1.0 %finish.1 = f32[1,6,256,128]{3,2,1,0:T(8,128)} custom-call(f32[6,2,64,128]{3,2,1,0:T(8,128)S(1)} %get-tuple-element.45.keep, f32[6,2,64,128]{3,2,1,0:T(8,128)S(1)} %collective-permute-done.7.got), custom_call_target="tpu_custom_call" | custom-call | tf_op jit(solution)/shard_map/finish/pallas_call | solution.py:577
Async XLA Ops:
  3.0 6.3 %collective-permute-start = (bf16[4,6,2,112,128]{4,3,2,1,0:T(8,128)(2,1)S(1)}, bf16[4,6,2,112,128]{4,3,2,1,0:T(8,128)(2,1)S(1)}, u32[]{:S(2)}, u32[]{:S(2)}) collective-permute-start(bf16[4,6,2,112,128]{4,3,2,1,0:T(8,128)(2,1)S(1)} %get-tuple-element.27), channel_id=1, source_target_pairs={{0,8},{8,0},{16,24},{24,16},{1,9},{9,1},{17,25},{25,17},{2,10},{10... | collective-permute-start | bytes 4128776 | tf_op jit(solution)/shard_map/ppermute | solution.py:482
  3.5 5.8 %collective-permute-start.1 = (f32[5,2,112,128]{3,2,1,0:T(8,128)S(1)}, f32[5,2,112,128]{3,2,1,0:T(8,128)S(1)}, u32[]{:S(2)}, u32[]{:S(2)}) collective-permute-start(f32[5,2,112,128]{3,2,1,0:T(8,128)S(1)} %get-tuple-element.29), channel_id=1, source_target_pairs={{0,8},{8,0},{16,24},{24,16},{1,9},{9,1},{17,25},{25,17},{2,10},{10... | collective-permute-start | bytes 1720328 | tf_op jit(solution)/shard_map/ppermute | solution.py:483
  3.6 15.7 %collective-permute-start.3 = (bf16[61,16,128]{2,1,0:T(8,128)(2,1)S(1)}, bf16[61,16,128]{2,1,0:T(8,128)(2,1)S(1)}, u32[]{:S(2)}, u32[]{:S(2)}) collective-permute-start(bf16[61,16,128]{2,1,0:T(8,128)(2,1)S(1)} %get-tuple-element.31), channel_id=1, source_target_pairs={{0,15},{1,8},{2,9},{3,10},{4,11},{5,12},{6,13},{7,14},{8,1},{9,2},... | collective-permute-start | bytes 749576 | tf_op jit(solution)/shard_map/ppermute | solution.py:484
  9.2 10.1 %collective-permute-start.4 = (bf16[61,16,128]{2,1,0:T(8,128)(2,1)S(1)}, bf16[61,16,128]{2,1,0:T(8,128)(2,1)S(1)}, u32[]{:S(2)}, u32[]{:S(2)}) collective-permute-start(bf16[61,16,128]{2,1,0:T(8,128)(2,1)S(1)} %get-tuple-element.32), channel_id=1, source_target_pairs={{0,1},{1,2},{2,3},{3,4},{4,5},{5,6},{6,7},{7,0},{8,15},{9,8},{10,9... | collective-permute-start | bytes 749576 | tf_op jit(solution)/shard_map/ppermute | solution.py:485
  10.0 14.7 %collective-permute-start.2 = (bf16[6,8,16,128]{3,2,1,0:T(8,128)(2,1)S(1)}, bf16[6,8,16,128]{3,2,1,0:T(8,128)(2,1)S(1)}, u32[]{:S(2)}, u32[]{:S(2)}) collective-permute-start(bf16[6,8,16,128]{3,2,1,0:T(8,128)(2,1)S(1)} %get-tuple-element.30), channel_id=1, source_target_pairs={{0,16},{1,17},{2,18},{3,19},{4,20},{5,21},{6,22},{7,23},{8,24},{9,... | collective-permute-start | bytes 589832 | tf_op jit(solution)/shard_map/ppermute | solution.py:524
  19.6 9.3 %collective-permute-start.6 = (bf16[6,3,16,128]{3,2,1,0:T(8,128)(2,1)S(1)}, bf16[6,3,16,128]{3,2,1,0:T(8,128)(2,1)S(1)}, u32[]{:S(2)}, u32[]{:S(2)}) collective-permute-start(bf16[6,3,16,128]{3,2,1,0:T(8,128)(2,1)S(1)} %get-tuple-element.38), channel_id=1, source_target_pairs={{0,16},{1,17},{2,18},{3,19},{4,20},{5,21},{6,22},{7,23},{8,24},{9,... | collective-permute-start | bytes 221192 | tf_op jit(solution)/shard_map/ppermute | solution.py:560
  24.4 4.5 %collective-permute-start.5 = (bf16[6,3,16,128]{3,2,1,0:T(8,128)(2,1)S(1)}, bf16[6,3,16,128]{3,2,1,0:T(8,128)(2,1)S(1)}, u32[]{:S(2)}, u32[]{:S(2)}) collective-permute-start(bf16[6,3,16,128]{3,2,1,0:T(8,128)(2,1)S(1)} %get-tuple-element.38), channel_id=1, source_target_pairs={{0,16},{1,17},{2,18},{3,19},{4,20},{5,21},{6,22},{7,23},{8,24},{9,... | collective-permute-start | bytes 221192 | tf_op jit(solution)/shard_map/ppermute | solution.py:561
  35.0 1.8 %collective-permute-start.7 = (f32[6,2,64,128]{3,2,1,0:T(8,128)S(1)}, f32[6,2,64,128]{3,2,1,0:T(8,128)S(1)}, u32[]{:S(2)}, u32[]{:S(2)}) collective-permute-start(f32[6,2,64,128]{3,2,1,0:T(8,128)S(1)} %get-tuple-element.46), channel_id=1, source_target_pairs={{0,8},{8,0},{16,24},{24,16},{1,9},{9,1},{17,25},{25,17},{2,10},{10... | collective-permute-start | bytes 1179656 | tf_op jit(solution)/shard_map/ppermute | solution.py:576

commit v7 on v6

--- a/solution.py
+++ b/solution.py
@@ -55,11 +55,11 @@
     coef_copies = [
         pltpu.make_async_copy(ref.at[0], co.at[c], sems.at[c]) for c, ref in enumerate((zf, mf, zc, mc))
     ]
-    part = z.fields // 2
+    part = z.steps // 4
     forcing_copies = []
-    for n in range(2 * z.steps):
-        block = (n // 2, pl.ds(n % 2 * part, part))
-        forcing_copies.append(pltpu.make_async_copy(fo_in.at[(0, *block)], fo.at[block], sems.at[5 + n]))
+    for n in range(4):
+        block = pl.ds(n * part, part)
+        forcing_copies.append(pltpu.make_async_copy(fo_in.at[0, block], fo.at[block], sems.at[5 + n]))
     mixing_copy = pltpu.make_async_copy(cp_in, cp, sems.at[4])
     for copy in coef_copies + [mixing_copy] + forcing_copies:
         copy.start()
@@ -91,9 +91,9 @@
         for g in range(z.fields):
             ref[4, 0, g : g + 1, : z.fields] = cp[g]
     for k in range(z.steps):
+        if k % part == 0:
+            forcing_copies[k // part].wait()
         for f in range(z.fields):
-            if f % part == 0:
-                forcing_copies[2 * k + f // part].wait()
             both = columns(fo[k, f].astype(F32), count % slots)
             split(both, z.depths[k], z.starts[k] + f * z.depths[k], keep_f.at[k, f], send_f.at[k, f])
             count += 1

time: 38 us -> 37.7 us (level)
  no operation moved by 1% of the time
where the time goes in v7:
time: 37.7 us; the launch traced here: 37.6 us
  starting transfers between devices  20.5 us (54%)
  Pallas kernels  13.3 us (35%)
  waiting for transfers between devices  3.7 us (10%)
    ppermute x1, starting transfers between devices, per_device(): core = lax.ppermute(core, ('tm', 'space'), down)  9.31 us
    pallas_call x1, Pallas kernels, per_device(): pl.pallas_call(functools.partial(late_kernel, z, 0), out_shape=[shape(hal...  6.06 us
    ppermute x1, starting transfers between devices, per_device(): got_a = lax.ppermute(pay_a, ('tm', 'space'), perm_a)  5.67 us
    ppermute x1, starting transfers between devices, per_device(): far = lax.ppermute(edge, ('tm', 'space'), across)  4.76 us
    pallas_call x1, Pallas kernels, per_device(): pl.pallas_call(functools.partial(prepare_kernel, z), out_shape=[shape(f_s...  2.67 us
    pallas_call x1, Pallas kernels, per_device(): pl.pallas_call(functools.partial(early_kernel, z, 0), out_shape=shape((z....  2.47 us
    ppermute x1, waiting for transfers between devices, per_device(): far = lax.ppermute(edge, ('tm', 'space'), across)  1.81 us
    ppermute x1, waiting for transfers between devices, per_device(): got = lax.ppermute(sent, 'tm', partner)  1.71 us
  transfers between devices with their start and end apart: 8, of which 3 were waited for; matrix products, arithmetic and copies ran while one was open for 0% of the time, Pallas kernels for 9%

profile of v7, /device:TPU:0, one launch (start us, length us, event | category | flops | bytes accessed | tf_op | source)
XLA Modules:
  0.0 37.6 jit_solution(7408796320962013208)
XLA Ops:
  0.0 2.7 %prepare.1 = (bf16[4,6,2,112,128]{4,3,2,1,0:T(8,128)(2,1)S(1)}, bf16[4,6,2,112,128]{4,3,2,1,0:T(8,128)(2,1)S(1)}, f32[5,2,112,128]{3,2,1,0:T(8,128)S(1)}, f32[5,...) custom-call(bf16[1,4,6,256,128]{4,3,2,1,0:T(8,128)(2,1)} %fo_in.1, ...), custom_call_target="tpu_custom_call" | custom-call | tf_op jit(solution)/shard_map/prepare/pallas_call | solution.py:439
  2.7 0.5 %collective-permute-start = (bf16[4,6,2,112,128]{4,3,2,1,0:T(8,128)(2,1)S(1)}, bf16[4,6,2,112,128]{4,3,2,1,0:T(8,128)(2,1)S(1)}, u32[]{:S(2)}, u32[]{:S(2)}) collective-permute-start(bf16[4,6,2,112,128]{4,3,2,1,0:T(8,128)(2,1)S(1)} %get-tuple-element.27), channel_id=1, source_target_pairs={{0,8},{8,0},{16,24},{24,16},{1,9},{9,1},{17,25},{25,17},{2,10},{10... | collective-permute-start | bytes 4128776 | tf_op jit(solution)/shard_map/ppermute | solution.py:482
  3.2 0.1 collective-permute-start.1
  3.3 5.7 %collective-permute-start.3 = (bf16[61,16,128]{2,1,0:T(8,128)(2,1)S(1)}, bf16[61,16,128]{2,1,0:T(8,128)(2,1)S(1)}, u32[]{:S(2)}, u32[]{:S(2)}) collective-permute-start(bf16[61,16,128]{2,1,0:T(8,128)(2,1)S(1)} %get-tuple-element.31), channel_id=1, source_target_pairs={{0,15},{1,8},{2,9},{3,10},{4,11},{5,12},{6,13},{7,14},{8,1},{9,2},... | collective-permute-start | bytes 749576 | tf_op jit(solution)/shard_map/ppermute | solution.py:484
  8.9 0.0 collective-permute-start.4
  8.9 0.0 collective-permute-done.1.rc
  8.9 0.0 collective-permute-done.rf
  9.0 0.7 %inner.1 = (f32[2,4,6,2,136,128]{5,4,3,2,1,0:T(8,128)S(1)}, f32[2,4,2,136,128]{4,3,2,1,0:T(8,128)S(1)}, f32[2,6,2,112,128]{4,3,2,1,0:T(8,128)S(1)}, bf16[6,8,16,...) custom-call(bf16[4,6,2,112,128]{4,3,2,1,0:T(8,128)(2,1)S(1)} %get-tuple-element.26.kf, ...), custom_call_target="tpu_custom_call" | custom-call | flops 1000000000 | bytes 20000000 | tf_op jit(solution)/shard_map/inner/pallas_call | solution.py:505
  9.7 9.3 %collective-permute-start.2 = (bf16[6,8,16,128]{3,2,1,0:T(8,128)(2,1)S(1)}, bf16[6,8,16,128]{3,2,1,0:T(8,128)(2,1)S(1)}, u32[]{:S(2)}, u32[]{:S(2)}) collective-permute-start(bf16[6,8,16,128]{3,2,1,0:T(8,128)(2,1)S(1)} %get-tuple-element.30), channel_id=1, source_target_pairs={{0,16},{1,17},{2,18},{3,19},{4,20},{5,21},{6,22},{7,23},{8,24},{9,... | collective-permute-start | bytes 589832 | tf_op jit(solution)/shard_map/ppermute | solution.py:524
  19.0 0.0 collective-permute-done.3.ra
  19.0 0.0 collective-permute-done.4.rb
  19.0 0.4 rim.1
  19.4 4.8 %collective-permute-start.6 = (bf16[6,3,16,128]{3,2,1,0:T(8,128)(2,1)S(1)}, bf16[6,3,16,128]{3,2,1,0:T(8,128)(2,1)S(1)}, u32[]{:S(2)}, u32[]{:S(2)}) collective-permute-start(bf16[6,3,16,128]{3,2,1,0:T(8,128)(2,1)S(1)} %get-tuple-element.38), channel_id=1, source_target_pairs={{0,16},{1,17},{2,18},{3,19},{4,20},{5,21},{6,22},{7,23},{8,24},{9,... | collective-permute-start | bytes 221192 | tf_op jit(solution)/shard_map/ppermute | solution.py:560
  24.1 0.1 collective-permute-start.5
  24.2 0.2 collective-permute-done.2.core
  24.4 2.5 %early.1.state = f32[6,2,72,128]{3,2,1,0:T(8,128)S(1)} custom-call(bf16[6,8,16,128]{3,2,1,0:T(8,128)(2,1)S(1)} %collective-permute-done.2.core, f32[2,4,6,2,136,128]{5,4,3,2,1,0:T(8,128)S(1)} %get-tuple-element.39.rows_f, f32[10,8,2,8,128]{4,3,2,1,0:T(8,128)S(1)} %get-tuple-element.40.co, f32[36,8,128]{2,1,0:T(8,128)S(1)} %get-tuple-element.34.mix_first.mix), custom_call_target="tpu_custom_call" | custom-call | tf_op jit(solution)/shard_map/early/pallas_call | solution.py:551
  26.9 1.8 %collective-permute-done.6.far = bf16[6,3,16,128]{3,2,1,0:T(8,128)(2,1)S(1)} collective-permute-done((bf16[6,3,16,128]{3,2,1,0:T(8,128)(2,1)S(1)}, bf16[6,3,16,128]{3,2,1,0:T(8,128)(2,1)S(1)}, u32[]{:S(2)}, u32[]{:S(2)}) %collective-permute-start.6) | collective-permute-done | bytes 73760 | tf_op jit(solution)/shard_map/ppermute | solution.py:560
  28.7 0.0 collective-permute-done.5.near
  28.7 6.1 %late.1 = (f32[6,2,64,128]{3,2,1,0:T(8,128)S(1)}, f32[6,2,64,128]{3,2,1,0:T(8,128)S(1)}) custom-call(bf16[6,8,16,128]{3,2,1,0:T(8,128)(2,1)S(1)} %collective-permute-done.2.core, bf16[6,3,16,128]{3,2,1,0:T(8,128)(2,1)S(1)} %collective-permute-done.5.near, ...), custom_call_target="tpu_custom_call", output_to_operand_aliasing={{0}: (9, {}), {1}: (10, {})} | custom-call | tf_op jit(solution)/shard_map/late/pallas_call | solution.py:562
  34.7 0.1 collective-permute-start.7
  34.8 1.7 %collective-permute-done.7.got = f32[6,2,64,128]{3,2,1,0:T(8,128)S(1)} collective-permute-done((f32[6,2,64,128]{3,2,1,0:T(8,128)S(1)}, f32[6,2,64,128]{3,2,1,0:T(8,128)S(1)}, u32[]{:S(2)}, u32[]{:S(2)}) %collective-permute-start.7) | collective-permute-done | bytes 393248 | tf_op jit(solution)/shard_map/ppermute | solution.py:576
  36.5 1.0 %finish.1 = f32[1,6,256,128]{3,2,1,0:T(8,128)} custom-call(f32[6,2,64,128]{3,2,1,0:T(8,128)S(1)} %get-tuple-element.45.keep, f32[6,2,64,128]{3,2,1,0:T(8,128)S(1)} %collective-permute-done.7.got), custom_call_target="tpu_custom_call" | custom-call | tf_op jit(solution)/shard_map/finish/pallas_call | solution.py:577
Async XLA Ops:
  2.7 6.3 %collective-permute-start = (bf16[4,6,2,112,128]{4,3,2,1,0:T(8,128)(2,1)S(1)}, bf16[4,6,2,112,128]{4,3,2,1,0:T(8,128)(2,1)S(1)}, u32[]{:S(2)}, u32[]{:S(2)}) collective-permute-start(bf16[4,6,2,112,128]{4,3,2,1,0:T(8,128)(2,1)S(1)} %get-tuple-element.27), channel_id=1, source_target_pairs={{0,8},{8,0},{16,24},{24,16},{1,9},{9,1},{17,25},{25,17},{2,10},{10... | collective-permute-start | bytes 4128776 | tf_op jit(solution)/shard_map/ppermute | solution.py:482
  3.2 5.8 %collective-permute-start.1 = (f32[5,2,112,128]{3,2,1,0:T(8,128)S(1)}, f32[5,2,112,128]{3,2,1,0:T(8,128)S(1)}, u32[]{:S(2)}, u32[]{:S(2)}) collective-permute-start(f32[5,2,112,128]{3,2,1,0:T(8,128)S(1)} %get-tuple-element.29), channel_id=1, source_target_pairs={{0,8},{8,0},{16,24},{24,16},{1,9},{9,1},{17,25},{25,17},{2,10},{10... | collective-permute-start | bytes 1720328 | tf_op jit(solution)/shard_map/ppermute | solution.py:483
  3.3 15.7 %collective-permute-start.3 = (bf16[61,16,128]{2,1,0:T(8,128)(2,1)S(1)}, bf16[61,16,128]{2,1,0:T(8,128)(2,1)S(1)}, u32[]{:S(2)}, u32[]{:S(2)}) collective-permute-start(bf16[61,16,128]{2,1,0:T(8,128)(2,1)S(1)} %get-tuple-element.31), channel_id=1, source_target_pairs={{0,15},{1,8},{2,9},{3,10},{4,11},{5,12},{6,13},{7,14},{8,1},{9,2},... | collective-permute-start | bytes 749576 | tf_op jit(solution)/shard_map/ppermute | solution.py:484
  8.9 10.1 %collective-permute-start.4 = (bf16[61,16,128]{2,1,0:T(8,128)(2,1)S(1)}, bf16[61,16,128]{2,1,0:T(8,128)(2,1)S(1)}, u32[]{:S(2)}, u32[]{:S(2)}) collective-permute-start(bf16[61,16,128]{2,1,0:T(8,128)(2,1)S(1)} %get-tuple-element.32), channel_id=1, source_target_pairs={{0,1},{1,2},{2,3},{3,4},{4,5},{5,6},{6,7},{7,0},{8,15},{9,8},{10,9... | collective-permute-start | bytes 749576 | tf_op jit(solution)/shard_map/ppermute | solution.py:485
  9.7 14.7 %collective-permute-start.2 = (bf16[6,8,16,128]{3,2,1,0:T(8,128)(2,1)S(1)}, bf16[6,8,16,128]{3,2,1,0:T(8,128)(2,1)S(1)}, u32[]{:S(2)}, u32[]{:S(2)}) collective-permute-start(bf16[6,8,16,128]{3,2,1,0:T(8,128)(2,1)S(1)} %get-tuple-element.30), channel_id=1, source_target_pairs={{0,16},{1,17},{2,18},{3,19},{4,20},{5,21},{6,22},{7,23},{8,24},{9,... | collective-permute-start | bytes 589832 | tf_op jit(solution)/shard_map/ppermute | solution.py:524
  19.4 9.3 %collective-permute-start.6 = (bf16[6,3,16,128]{3,2,1,0:T(8,128)(2,1)S(1)}, bf16[6,3,16,128]{3,2,1,0:T(8,128)(2,1)S(1)}, u32[]{:S(2)}, u32[]{:S(2)}) collective-permute-start(bf16[6,3,16,128]{3,2,1,0:T(8,128)(2,1)S(1)} %get-tuple-element.38), channel_id=1, source_target_pairs={{0,16},{1,17},{2,18},{3,19},{4,20},{5,21},{6,22},{7,23},{8,24},{9,... | collective-permute-start | bytes 221192 | tf_op jit(solution)/shard_map/ppermute | solution.py:560
  24.1 4.5 %collective-permute-start.5 = (bf16[6,3,16,128]{3,2,1,0:T(8,128)(2,1)S(1)}, bf16[6,3,16,128]{3,2,1,0:T(8,128)(2,1)S(1)}, u32[]{:S(2)}, u32[]{:S(2)}) collective-permute-start(bf16[6,3,16,128]{3,2,1,0:T(8,128)(2,1)S(1)} %get-tuple-element.38), channel_id=1, source_target_pairs={{0,16},{1,17},{2,18},{3,19},{4,20},{5,21},{6,22},{7,23},{8,24},{9,... | collective-permute-start | bytes 221192 | tf_op jit(solution)/shard_map/ppermute | solution.py:561
  34.7 1.8 %collective-permute-start.7 = (f32[6,2,64,128]{3,2,1,0:T(8,128)S(1)}, f32[6,2,64,128]{3,2,1,0:T(8,128)S(1)}, u32[]{:S(2)}, u32[]{:S(2)}) collective-permute-start(f32[6,2,64,128]{3,2,1,0:T(8,128)S(1)} %get-tuple-element.46), channel_id=1, source_target_pairs={{0,8},{8,0},{16,24},{24,16},{1,9},{9,1},{17,25},{25,17},{2,10},{10... | collective-permute-start | bytes 1179656 | tf_op jit(solution)/shard_map/ppermute | solution.py:576

commit v8 on v7

--- a/solution.py
+++ b/solution.py
@@ -227,26 +227,40 @@
     return jnp.concatenate([ref[f, p, at, :] for p in range(2)], axis=0).astype(BF16)
 
 
-def inner_kernel(z, active, kf, rf, kc, rc, rows_f, rows_c, inner, core, mix_first, mix_last, *scratch):
+def put_rows(z, half, rows_f, rows_c, q, forcing, coefs):
+    at = aligned(z.halo * (1 - half), z.main)
+    for c in range(4):
+        for p in range(2):
+            rows_c[q, c, p, at, :] = coefs[c, p]
+    for k in range(z.steps):
+        for f in range(z.fields):
+            for p in range(2):
+                rows_f[q, k, f, p, at, :] = forcing[k, f, p].astype(F32)
+
+
+def spread_kernel(z, kf, kc, rows_f, rows_c):
+    half, _ = half_and_chip()
+    put_rows(z, half, rows_f, rows_c, 1 - half, kf, kc)
+    blank = jnp.zeros((z.halo, z.lanes), F32)
+    edge = aligned(z.main * half, z.halo)
+    for q in range(2):
+        for p in range(2):
+            for c in range(4):
+                rows_c[q, c, p, edge, :] = blank
+            for k in range(z.steps):
+                for f in range(z.fields):
+                    rows_f[q, k, f, p, edge, :] = blank
+
+
+def inner_kernel(
+    z, active, rf, rc, kc, rows_f_in, rows_c_in, rows_f, rows_c, inner, core, mix_first, mix_last, *scratch
+):
     half, chip = half_and_chip()
     *scratch, tables = scratch
     main_at = z.halo * (1 - half)
-    blank = jnp.zeros((z.halo, z.lanes), F32)
-
-    def put(ref, values):
-        ref[aligned(main_at, z.main), :] = values.astype(F32)
-        ref[aligned(z.main * half, z.halo), :] = blank
-
-    for q, forcing, coefs in ((1 - half, kf, kc), (half, rf, rc)):
-        for c in range(4):
-            for p in range(2):
-                put(rows_c.at[q, c, p], coefs[c, p])
+    put_rows(z, half, rows_f, rows_c, half, rf, rc)
+    for q, coefs in ((1 - half, kc), (half, rc)):
         tables[q, :, :] = coefs[4, 0, :SUB, :]
-        for k in range(z.steps):
-            for f in range(z.fields):
-                for p in range(2):
-                    put(rows_f.at[q, k, f, p], forcing[k, f, p])
-
     set_mixing(z, mix_first, tables.at[0])
     set_mixing(z, mix_last, tables.at[1])
 
@@ -270,28 +284,36 @@
                 core[f, g] = tile_of(inner.at[1], f, slice(z.halo + SUB * g, z.halo + SUB * (g + 1)))
 
 
-def rim_kernel(z, active, ra, rb, inner, mix_first, mix_last, rows_f_in, rows_c_in, rows_f, rows_c, ko, so, edge, *refs):
+def place_halo(z, half, second, pay, edges, rows_f, rows_c):
+    for g in range(z.payload):
+        tile = pay[g].astype(F32)
+        for p in range(2):
+            edges[p, SUB * g : SUB * (g + 1), :] = tile[SUB * p : SUB * (p + 1)]
+
+    def place(side):
+        q = 1 - side if second else side
+        blocks = [(rows_c.at[q, c], z.coef_starts[c], z.coef_depths[c]) for c in range(4)]
+        for k in range(z.steps):
+            for f in range(z.fields):
+                blocks.append((rows_f.at[q, k, f], z.starts[k] + f * z.depths[k], z.depths[k]))
+        for ref, start, depth in blocks:
+            at = z.main if side else z.halo - depth
+            for p in range(2):
+                ref[p, at : at + depth, :] = edges[p, start : start + depth, :]
+
+    for side in range(2):
+        pl.when(half == side)(functools.partial(place, side))
+
+
+def halo_kernel(z, ra, rows_f_in, rows_c_in, rows_f, rows_c, edges):
+    half, _ = half_and_chip()
+    place_halo(z, half, False, ra, edges, rows_f, rows_c)
+
+
+def rim_kernel(z, active, rb, inner, mix_first, mix_last, rows_f_in, rows_c_in, rows_f, rows_c, ko, so, edge, *refs):
     (co_core, co_rim, co_late), (obuf, tmp, edges), scratch = refs[:3], refs[3:6], refs[6:]
     half, chip = half_and_chip()
-    for n, pay in enumerate((ra, rb)):
-        for g in range(z.payload):
-            tile = pay[g].astype(F32)
-            for p in range(2):
-                edges[n, p, SUB * g : SUB * (g + 1), :] = tile[SUB * p : SUB * (p + 1)]
-
-    def place_edges(side):
-        for n, q in ((0, side), (1, 1 - side)):
-            blocks = [(rows_c.at[q, c], z.coef_starts[c], z.coef_depths[c]) for c in range(4)]
-            for k in range(z.steps):
-                for f in range(z.fields):
-                    blocks.append((rows_f.at[q, k, f], z.starts[k] + f * z.depths[k], z.depths[k]))
-            for ref, start, depth in blocks:
-                at = z.main if side else z.halo - depth
-                for p in range(2):
-                    ref[p, at : at + depth, :] = edges[n, p, start : start + depth, :]
-
-    for side in range(2):
-        pl.when(half == side)(functools.partial(place_edges, side))
+    place_halo(z, half, True, rb, edges, rows_f, rows_c)
 
     @pl.when(chip != active)
     def _():
@@ -502,6 +524,14 @@
     def tiles(columns):
         return shape((z.fields, columns // SUB, 2 * SUB, z.lanes), BF16)
 
+    rows_f, rows_c = pl.pallas_call(
+        functools.partial(spread_kernel, z),
+        out_shape=[rows_f_shape, rows_c_shape],
+        in_specs=in_vmem(2),
+        out_specs=in_vmem(2),
+        compiler_params=params,
+        name="spread",
+    )(keep_f, keep_c)
     rows_f, rows_c, inner, core, mix_first, mix_last = pl.pallas_call(
         functools.partial(inner_kernel, z, 1),
         out_shape=[
@@ -512,16 +542,27 @@
             mixing,
             mixing,
         ],
-        in_specs=in_vmem(4),
+        in_specs=in_vmem(5),
         out_specs=in_vmem(6),
+        input_output_aliases={3: 0, 4: 1},
         scratch_shapes=band_scratch(z.wide) + stencil_scratch(z.main) + [pltpu.VMEM((2, SUB, z.lanes), F32)],
         compiler_params=params,
         cost_estimate=pl.CostEstimate(flops=10**9, bytes_accessed=2 * 10**7, transcendentals=0),
         name="inner",
-    )(keep_f, got_f, keep_c, got_c)
+    )(got_f, got_c, keep_c, rows_f, rows_c)
     down = [(device(t, s), device(t ^ 2, s)) for t, s in everyone]
     across = [(device(t, s), device((t ^ 1) - 2, s + 1 if t % 2 else s - 1) if t >= 2 else device(t + 2, s)) for t, s in everyone]
     core = lax.ppermute(core, ("tm", "space"), down)
+    rows_f, rows_c = pl.pallas_call(
+        functools.partial(halo_kernel, z),
+        out_shape=[rows_f_shape, rows_c_shape],
+        in_specs=in_vmem(3),
+        out_specs=in_vmem(2),
+        input_output_aliases={1: 0, 2: 1},
+        scratch_shapes=[pltpu.VMEM((2, SUB * z.payload, z.lanes), F32)],
+        compiler_params=params,
+        name="halo",
+    )(got_a, rows_f, rows_c)
     rows_f, rows_c, kept, sent, edge, co_core, co_rim, co_late = pl.pallas_call(
         functools.partial(rim_kernel, z, 1),
         out_shape=[
@@ -534,20 +575,20 @@
             stencil(z.outer),
             stencil(z.main - z.halo),
         ],
-        in_specs=in_vmem(7),
+        in_specs=in_vmem(6),
         out_specs=in_vmem(8),
-        input_output_aliases={5: 0, 6: 1},
+        input_output_aliases={4: 0, 5: 1},
         scratch_shapes=[
             pltpu.VMEM((2,) + half_dims, F32),
             pltpu.VMEM((z.fields, 2, z.rim + SUB, z.lanes), F32),
-            pltpu.VMEM((2, 2, SUB * z.payload, z.lanes), F32),
+            pltpu.VMEM((2, SUB * z.payload, z.lanes), F32),
         ]
         + band_scratch(z.wide)
         + stencil_scratch(z.rim),
         compiler_params=params,
         cost_estimate=pl.CostEstimate(flops=10**9, bytes_accessed=2 * 10**7, transcendentals=0),
         name="rim",
-    )(got_a, got_b, inner, mix_first, mix_last, rows_f, rows_c)
+    )(got_b, inner, mix_first, mix_last, rows_f, rows_c)
     state = pl.pallas_call(
         functools.partial(early_kernel, z, 0),
         out_shape=shape((z.fields, 2, z.core + SUB, z.lanes), F32),

time: 37.7 us -> 38 us (level)
  Pallas kernels: 13.3 us -> 13.9 us
    pallas_call x1, Pallas kernels: 6.06 us -> 6.47 us  [per_device(): pl.pallas_call(functools.partial(late_kernel, z, 0), out_shape=[shape(hal...]
    pallas_call x0 -> x2, Pallas kernels: none -> 0.39 us  [the longest x1 0.31 us: per_device(): pl.pallas_call(functools.partial(spread_kernel, z), out_shape=[rows_f_sha...]
  transfers between devices with their start and end apart: 8 -> 8, of which waited for: 3 -> 3; matrix products, arithmetic and copies ran while one was open for 0% -> 0% of each run, Pallas kernels for 9% -> 10%
where the time goes in v8:
time: 38 us; the launch traced here: 37.9 us
  starting transfers between devices  20.4 us (54%)
  Pallas kernels  13.9 us (37%)
  waiting for transfers between devices  3.52 us (9%)
    ppermute x1, starting transfers between devices, per_device(): core = lax.ppermute(core, ('tm', 'space'), down)  9.29 us
    pallas_call x1, Pallas kernels, per_device(): pl.pallas_call(functools.partial(late_kernel, z, 0), out_shape=[shape(hal...  6.47 us
    ppermute x1, starting transfers between devices, per_device(): got_a = lax.ppermute(pay_a, ('tm', 'space'), perm_a)  5.67 us
    ppermute x1, starting transfers between devices, per_device(): far = lax.ppermute(edge, ('tm', 'space'), across)  4.68 us
    pallas_call x1, Pallas kernels, per_device(): pl.pallas_call(functools.partial(prepare_kernel, z), out_shape=[shape(f_s...  2.67 us
    pallas_call x1, Pallas kernels, per_device(): pl.pallas_call(functools.partial(early_kernel, z, 0), out_shape=shape((z....  2.62 us
    ppermute x1, waiting for transfers between devices, per_device(): got = lax.ppermute(sent, 'tm', partner)  1.71 us
    ppermute x1, waiting for transfers between devices, per_device(): far = lax.ppermute(edge, ('tm', 'space'), across)  1.54 us
  transfers between devices with their start and end apart: 8, of which 3 were waited for; matrix products, arithmetic and copies ran while one was open for 0% of the time, Pallas kernels for 10%

profile of v8, /device:TPU:0, one launch (start us, length us, event | category | flops | bytes accessed | tf_op | source)
XLA Modules:
  0.0 37.9 jit_solution(12802637756642983871)
XLA Ops:
  0.0 2.7 %prepare.1 = (bf16[4,6,2,112,128]{4,3,2,1,0:T(8,128)(2,1)S(1)}, bf16[4,6,2,112,128]{4,3,2,1,0:T(8,128)(2,1)S(1)}, f32[5,2,112,128]{3,2,1,0:T(8,128)S(1)}, f32[5,...) custom-call(bf16[1,4,6,256,128]{4,3,2,1,0:T(8,128)(2,1)} %fo_in.1, ...), custom_call_target="tpu_custom_call" | custom-call | tf_op jit(solution)/shard_map/prepare/pallas_call | solution.py:461
  2.7 0.5 %collective-permute-start = (bf16[4,6,2,112,128]{4,3,2,1,0:T(8,128)(2,1)S(1)}, bf16[4,6,2,112,128]{4,3,2,1,0:T(8,128)(2,1)S(1)}, u32[]{:S(2)}, u32[]{:S(2)}) collective-permute-start(bf16[4,6,2,112,128]{4,3,2,1,0:T(8,128)(2,1)S(1)} %get-tuple-element.30), channel_id=1, source_target_pairs={{0,8},{8,0},{16,24},{24,16},{1,9},{9,1},{17,25},{25,17},{2,10},{10... | collective-permute-start | bytes 4128776 | tf_op jit(solution)/shard_map/ppermute | solution.py:504
  3.2 0.1 collective-permute-start.1
  3.3 5.7 %collective-permute-start.4 = (bf16[61,16,128]{2,1,0:T(8,128)(2,1)S(1)}, bf16[61,16,128]{2,1,0:T(8,128)(2,1)S(1)}, u32[]{:S(2)}, u32[]{:S(2)}) collective-permute-start(bf16[61,16,128]{2,1,0:T(8,128)(2,1)S(1)} %get-tuple-element.41), channel_id=1, source_target_pairs={{0,15},{1,8},{2,9},{3,10},{4,11},{5,12},{6,13},{7,14},{8,1},{9,2},... | collective-permute-start | bytes 749576 | tf_op jit(solution)/shard_map/ppermute | solution.py:506
  8.9 0.0 collective-permute-start.3
  8.9 0.3 spread.1
  9.3 0.0 collective-permute-done.1.rc
  9.3 0.0 collective-permute-done.rf
  9.3 0.4 %inner.1 = (f32[2,4,6,2,136,128]{5,4,3,2,1,0:T(8,128)S(1)}, f32[2,4,2,136,128]{4,3,2,1,0:T(8,128)S(1)}, f32[2,6,2,112,128]{4,3,2,1,0:T(8,128)S(1)}, bf16[6,8,16,...) custom-call(bf16[4,6,2,112,128]{4,3,2,1,0:T(8,128)(2,1)S(1)} %collec, ...), custom_call_target="tpu_custom_call", output_to_operand_aliasing={{0}: (3, {}), {1}: (4, {})} | custom-call | flops 1000000000 | bytes 20000000 | tf_op jit(solution)/shard_map/inner/pallas_call | solution.py:535
  9.7 9.3 %collective-permute-start.2 = (bf16[6,8,16,128]{3,2,1,0:T(8,128)(2,1)S(1)}, bf16[6,8,16,128]{3,2,1,0:T(8,128)(2,1)S(1)}, u32[]{:S(2)}, u32[]{:S(2)}) collective-permute-start(bf16[6,8,16,128]{3,2,1,0:T(8,128)(2,1)S(1)} %get-tuple-element.36), channel_id=1, source_target_pairs={{0,16},{1,17},{2,18},{3,19},{4,20},{5,21},{6,22},{7,23},{8,24},{9,... | collective-permute-start | bytes 589832 | tf_op jit(solution)/shard_map/ppermute | solution.py:555
  19.0 0.0 collective-permute-done.4.ra
  19.0 0.1 halo.1
  19.1 0.0 collective-permute-done.3.rb
  19.1 0.3 rim.1
  19.4 4.7 %collective-permute-start.6 = (bf16[6,3,16,128]{3,2,1,0:T(8,128)(2,1)S(1)}, bf16[6,3,16,128]{3,2,1,0:T(8,128)(2,1)S(1)}, u32[]{:S(2)}, u32[]{:S(2)}) collective-permute-start(bf16[6,3,16,128]{3,2,1,0:T(8,128)(2,1)S(1)} %get-tuple-element.46), channel_id=1, source_target_pairs={{0,16},{1,17},{2,18},{3,19},{4,20},{5,21},{6,22},{7,23},{8,24},{9,... | collective-permute-start | bytes 221192 | tf_op jit(solution)/shard_map/ppermute | solution.py:601
  24.1 0.1 collective-permute-start.5
  24.1 0.2 collective-permute-done.2.core
  24.4 2.6 %early.1.state = f32[6,2,72,128]{3,2,1,0:T(8,128)S(1)} custom-call(bf16[6,8,16,128]{3,2,1,0:T(8,128)(2,1)S(1)} %collective-permute-done.2.core, f32[2,4,6,2,136,128]{5,4,3,2,1,0:T(8,128)S(1)} %get-tuple-element.47.rows_f, f32[10,8,2,8,128]{4,3,2,1,0:T(8,128)S(1)} %get-tuple-element.48.co, f32[36,8,128]{2,1,0:T(8,128)S(1)} %get-tuple-element.39.mix_first.mix), custom_call_target="tpu_custom_call" | custom-call | tf_op jit(solution)/shard_map/early/pallas_call | solution.py:592
  27.0 1.5 %collective-permute-done.6.far = bf16[6,3,16,128]{3,2,1,0:T(8,128)(2,1)S(1)} collective-permute-done((bf16[6,3,16,128]{3,2,1,0:T(8,128)(2,1)S(1)}, bf16[6,3,16,128]{3,2,1,0:T(8,128)(2,1)S(1)}, u32[]{:S(2)}, u32[]{:S(2)}) %collective-permute-start.6) | collective-permute-done | bytes 73760 | tf_op jit(solution)/shard_map/ppermute | solution.py:601
  28.5 0.0 collective-permute-done.5.near
  28.6 6.5 %late.1 = (f32[6,2,64,128]{3,2,1,0:T(8,128)S(1)}, f32[6,2,64,128]{3,2,1,0:T(8,128)S(1)}) custom-call(bf16[6,8,16,128]{3,2,1,0:T(8,128)(2,1)S(1)} %collective-permute-done.2.core, bf16[6,3,16,128]{3,2,1,0:T(8,128)(2,1)S(1)} %collective-permute-done.5.near, ...), custom_call_target="tpu_custom_call", output_to_operand_aliasing={{0}: (9, {}), {1}: (10, {})} | custom-call | tf_op jit(solution)/shard_map/late/pallas_call | solution.py:603
  35.0 0.1 collective-permute-start.7
  35.1 1.7 %collective-permute-done.7.got = f32[6,2,64,128]{3,2,1,0:T(8,128)S(1)} collective-permute-done((f32[6,2,64,128]{3,2,1,0:T(8,128)S(1)}, f32[6,2,64,128]{3,2,1,0:T(8,128)S(1)}, u32[]{:S(2)}, u32[]{:S(2)}) %collective-permute-start.7) | collective-permute-done | bytes 393248 | tf_op jit(solution)/shard_map/ppermute | solution.py:617
  36.8 1.0 %finish.1 = f32[1,6,256,128]{3,2,1,0:T(8,128)} custom-call(f32[6,2,64,128]{3,2,1,0:T(8,128)S(1)} %get-tuple-element.53.keep, f32[6,2,64,128]{3,2,1,0:T(8,128)S(1)} %collective-permute-done.7.got), custom_call_target="tpu_custom_call" | custom-call | tf_op jit(solution)/shard_map/finish/pallas_call | solution.py:618
Async XLA Ops:
  2.7 6.6 %collective-permute-start = (bf16[4,6,2,112,128]{4,3,2,1,0:T(8,128)(2,1)S(1)}, bf16[4,6,2,112,128]{4,3,2,1,0:T(8,128)(2,1)S(1)}, u32[]{:S(2)}, u32[]{:S(2)}) collective-permute-start(bf16[4,6,2,112,128]{4,3,2,1,0:T(8,128)(2,1)S(1)} %get-tuple-element.30), channel_id=1, source_target_pairs={{0,8},{8,0},{16,24},{24,16},{1,9},{9,1},{17,25},{25,17},{2,10},{10... | collective-permute-start | bytes 4128776 | tf_op jit(solution)/shard_map/ppermute | solution.py:504
  3.2 6.1 %collective-permute-start.1 = (f32[5,2,112,128]{3,2,1,0:T(8,128)S(1)}, f32[5,2,112,128]{3,2,1,0:T(8,128)S(1)}, u32[]{:S(2)}, u32[]{:S(2)}) collective-permute-start(f32[5,2,112,128]{3,2,1,0:T(8,128)S(1)} %get-tuple-element.31), channel_id=1, source_target_pairs={{0,8},{8,0},{16,24},{24,16},{1,9},{9,1},{17,25},{25,17},{2,10},{10... | collective-permute-start | bytes 1720328 | tf_op jit(solution)/shard_map/ppermute | solution.py:505
  3.3 15.7 %collective-permute-start.4 = (bf16[61,16,128]{2,1,0:T(8,128)(2,1)S(1)}, bf16[61,16,128]{2,1,0:T(8,128)(2,1)S(1)}, u32[]{:S(2)}, u32[]{:S(2)}) collective-permute-start(bf16[61,16,128]{2,1,0:T(8,128)(2,1)S(1)} %get-tuple-element.41), channel_id=1, source_target_pairs={{0,15},{1,8},{2,9},{3,10},{4,11},{5,12},{6,13},{7,14},{8,1},{9,2},... | collective-permute-start | bytes 749576 | tf_op jit(solution)/shard_map/ppermute | solution.py:506
  8.9 10.1 %collective-permute-start.3 = (bf16[61,16,128]{2,1,0:T(8,128)(2,1)S(1)}, bf16[61,16,128]{2,1,0:T(8,128)(2,1)S(1)}, u32[]{:S(2)}, u32[]{:S(2)}) collective-permute-start(bf16[61,16,128]{2,1,0:T(8,128)(2,1)S(1)} %get-tuple-element.37), channel_id=1, source_target_pairs={{0,1},{1,2},{2,3},{3,4},{4,5},{5,6},{6,7},{7,0},{8,15},{9,8},{10,9... | collective-permute-start | bytes 749576 | tf_op jit(solution)/shard_map/ppermute | solution.py:507
  9.7 14.7 %collective-permute-start.2 = (bf16[6,8,16,128]{3,2,1,0:T(8,128)(2,1)S(1)}, bf16[6,8,16,128]{3,2,1,0:T(8,128)(2,1)S(1)}, u32[]{:S(2)}, u32[]{:S(2)}) collective-permute-start(bf16[6,8,16,128]{3,2,1,0:T(8,128)(2,1)S(1)} %get-tuple-element.36), channel_id=1, source_target_pairs={{0,16},{1,17},{2,18},{3,19},{4,20},{5,21},{6,22},{7,23},{8,24},{9,... | collective-permute-start | bytes 589832 | tf_op jit(solution)/shard_map/ppermute | solution.py:555
  19.4 9.2 %collective-permute-start.6 = (bf16[6,3,16,128]{3,2,1,0:T(8,128)(2,1)S(1)}, bf16[6,3,16,128]{3,2,1,0:T(8,128)(2,1)S(1)}, u32[]{:S(2)}, u32[]{:S(2)}) collective-permute-start(bf16[6,3,16,128]{3,2,1,0:T(8,128)(2,1)S(1)} %get-tuple-element.46), channel_id=1, source_target_pairs={{0,16},{1,17},{2,18},{3,19},{4,20},{5,21},{6,22},{7,23},{8,24},{9,... | collective-permute-start | bytes 221192 | tf_op jit(solution)/shard_map/ppermute | solution.py:601
  24.1 4.5 %collective-permute-start.5 = (bf16[6,3,16,128]{3,2,1,0:T(8,128)(2,1)S(1)}, bf16[6,3,16,128]{3,2,1,0:T(8,128)(2,1)S(1)}, u32[]{:S(2)}, u32[]{:S(2)}) collective-permute-start(bf16[6,3,16,128]{3,2,1,0:T(8,128)(2,1)S(1)} %get-tuple-element.46), channel_id=1, source_target_pairs={{0,16},{1,17},{2,18},{3,19},{4,20},{5,21},{6,22},{7,23},{8,24},{9,... | collective-permute-start | bytes 221192 | tf_op jit(solution)/shard_map/ppermute | solution.py:602
  35.0 1.8 %collective-permute-start.7 = (f32[6,2,64,128]{3,2,1,0:T(8,128)S(1)}, f32[6,2,64,128]{3,2,1,0:T(8,128)S(1)}, u32[]{:S(2)}, u32[]{:S(2)}) collective-permute-start(f32[6,2,64,128]{3,2,1,0:T(8,128)S(1)} %get-tuple-element.54), channel_id=1, source_target_pairs={{0,8},{8,0},{16,24},{24,16},{1,9},{9,1},{17,25},{25,17},{2,10},{10... | collective-permute-start | bytes 1179656 | tf_op jit(solution)/shard_map/ppermute | solution.py:617
